TPU v7x, 32 devices: a whole 2x2x4 slice. The times are simulated.
32 devices in a mesh: dp: 4 (over z), seq: 8 (over y, x, core).
Axes of the slice: x: 2, y: 2, z: 4, core: 2. Of those that a mesh axis runs over, the one named last changes fastest.
Arguments:
- tokens: bfloat16 [8, 1024, 2048], P('dp', 'seq'), may hold values from -6 to 6
- doc_ids: int32 [8, 1024], P('dp'), may hold values from 0 to 4, as said below
- cotangent: bfloat16 [8, 1024, 2048], P('dp', 'seq'), may hold values from -6 to 6
- norm1_gain: bfloat16 [2048], P(('dp', 'seq')), may hold values from 0.099609375 to 1.8984375
- w_query: bfloat16 [2048, 2048], P(('dp', 'seq')), may hold values from -0.125 to 0.125
- w_key: bfloat16 [2048, 2048], P(('dp', 'seq')), may hold values from -0.125 to 0.125
- w_value: bfloat16 [2048, 2048], P(('dp', 'seq')), may hold values from -0.125 to 0.125
- w_out: bfloat16 [2048, 2048], P(('dp', 'seq')), may hold values from -1 to 1
- norm2_gain: bfloat16 [2048], P(('dp', 'seq')), may hold values from 0.099609375 to 1.8984375
- w_gate: bfloat16 [2048, 8192], P(('dp', 'seq')), may hold values from -0.125 to 0.125
- w_up: bfloat16 [2048, 8192], P(('dp', 'seq')), may hold values from -0.125 to 0.125
- w_down: bfloat16 [8192, 2048], P(('dp', 'seq')), may hold values from -0.0625 to 0.0625
Outputs:
- out_tokens: bfloat16 [8, 1024, 2048], P('dp', 'seq')
- grad_tokens: bfloat16 [8, 1024, 2048], P('dp', 'seq')
- grad_norm1: float32 [2048], P(('dp', 'seq'))
- grad_query: float32 [2048, 2048], P(('dp', 'seq'))
- grad_key: float32 [2048, 2048], P(('dp', 'seq'))
- grad_value: float32 [2048, 2048], P(('dp', 'seq'))
- grad_out: float32 [2048, 2048], P(('dp', 'seq'))
- grad_norm2: float32 [2048], P(('dp', 'seq'))
- grad_gate: float32 [2048, 8192], P(('dp', 'seq'))
- grad_up: float32 [2048, 8192], P(('dp', 'seq'))
- grad_down: float32 [8192, 2048], P(('dp', 'seq'))
Inputs may be any that keep to these rules, and one draw needn't show every extreme that they name: `doc_ids`: each row holds exactly five documents numbered 0 to 4 in order, each of one token or more; document 2 begins within the first 128 tokens of its row and ends within the last 128.
All inputs are finite; a program needn't handle non-finite values.
Results may differ from a plain program's by a relative error of at most 0.017.
Values may be sent and summed in bfloat16 or wider, within the bound.
A program may use at most 640 MiB of HBM per device.

v0:
```python
import jax
import jax.numpy as jnp
from jax import lax
from jax.sharding import PartitionSpec as P

H = 32
HD = 64


rope_base = 130000.0
norm_eps = 1e-05


def rope_angles(doc_ids, head_size):
    places = lax.broadcasted_iota(jnp.int32, doc_ids.shape, 1)
    earlier = jnp.concatenate([doc_ids[:, :1], doc_ids[:, :-1]], axis=1)
    starts = lax.cummax(jnp.where(doc_ids != earlier, places, 0), axis=1)
    positions = (places - starts).astype(jnp.float32)
    frequency = rope_base ** (-(jnp.arange(head_size // 2, dtype=jnp.float32) * 2.0 / head_size))
    angles = positions[..., None] * frequency
    return (jnp.cos(angles), jnp.sin(angles))


def rotate(values, cos_table, sin_table):
    half_size = values.shape[-1] // 2
    lower_half, upper_half = (values[..., :half_size], values[..., half_size:])
    cos_wide = cos_table[..., None, :]
    sin_wide = sin_table[..., None, :]
    return jnp.concatenate(
        [
            lower_half * cos_wide - upper_half * sin_wide,
            upper_half * cos_wide + lower_half * sin_wide,
        ],
        axis=-1,
    )


def unrotate(values, cos_table, sin_table):
    half_size = values.shape[-1] // 2
    lower_half, upper_half = (values[..., :half_size], values[..., half_size:])
    cos_wide = cos_table[..., None, :]
    sin_wide = sin_table[..., None, :]
    return jnp.concatenate(
        [
            lower_half * cos_wide + upper_half * sin_wide,
            upper_half * cos_wide - lower_half * sin_wide,
        ],
        axis=-1,
    )


def rms_scale(values):
    return lax.rsqrt(jnp.mean(values * values, axis=-1, keepdims=True) + norm_eps)


def norm_back(values, inv_scale, gain_vec, grad_in):
    weighted = grad_in * gain_vec
    inner_mean = jnp.mean(weighted * values, axis=-1, keepdims=True)
    grad_values = inv_scale * weighted - values * (inv_scale * inv_scale * inv_scale) * inner_mean
    gain_term = jnp.sum(grad_in * values * inv_scale, axis=0)
    return (grad_values, gain_term)


def key_slice(source, block_start, block_size, head_size):
    piece = lax.dynamic_slice_in_dim(source, block_start, block_size, 1)
    return piece.reshape(piece.shape[0], block_size, piece.shape[2] // head_size, head_size)


def block_scores(query_rot, keys_all, doc_ids, query_ids, query_index, block_start, block_size):
    head_size = query_rot.shape[-1]
    key_block = key_slice(keys_all, block_start, block_size, head_size)
    raw_scores = (
        jnp.einsum("rqhd,rkhd->rhqk", query_rot, key_block, preferred_element_type=jnp.float32)
        * 0.125
    )
    key_ids = lax.dynamic_slice_in_dim(doc_ids, block_start, block_size, 1)
    key_index = block_start + lax.broadcasted_iota(jnp.int32, (block_size,), 0)
    allowed = (query_ids[:, :, None] == key_ids[:, None, :]) & (
        key_index[None, None, :] <= query_index[None, :, None]
    )
    return (raw_scores, allowed[:, None, :, :])


def block_probs(
    query_rot, keys_all, doc_ids, query_ids, query_index, log_total, block_start, block_size
):
    raw_scores, allowed = block_scores(
        query_rot, keys_all, doc_ids, query_ids, query_index, block_start, block_size
    )
    return jnp.exp(jnp.where(allowed, raw_scores - log_total[..., None], -1e30))


def attention_forward(query_rot, keys_all, values_all, doc_ids, query_ids, query_index, block_size):
    rows_here, query_count, head_count, head_size = query_rot.shape
    blocks = keys_all.shape[1] // block_size
    f32 = jnp.float32

    def peak_step(carried, block_index):
        block_start = block_index * block_size
        run_peak, run_total = carried
        raw_scores, allowed = block_scores(
            query_rot, keys_all, doc_ids, query_ids, query_index, block_start, block_size
        )
        masked = jnp.where(allowed, raw_scores, -1e30)
        new_peak = jnp.maximum(run_peak, jnp.max(masked, axis=-1))
        shifted = jnp.where(allowed, jnp.exp(masked - new_peak[..., None]), 0.0)
        return (
            (new_peak, run_total * jnp.exp(run_peak - new_peak) + jnp.sum(shifted, axis=-1)),
            None,
        )

    stat_shape = (rows_here, head_count, query_count)
    (run_peak, run_total), _ = lax.scan(
        peak_step,
        (jnp.full(stat_shape, -1e30, f32), jnp.zeros(stat_shape, f32)),
        jnp.arange(blocks, dtype=jnp.int32),
    )
    log_total = run_peak + jnp.log(run_total)

    def out_step(accumulated, block_index):
        block_start = block_index * block_size
        soft_probs = block_probs(
            query_rot, keys_all, doc_ids, query_ids, query_index, log_total, block_start, block_size
        ).astype(jnp.bfloat16)
        value_block = key_slice(values_all, block_start, block_size, head_size)
        return (
            accumulated
            + jnp.einsum("rhqk,rkhd->rqhd", soft_probs, value_block, preferred_element_type=f32),
            None,
        )

    attended, _ = lax.scan(
        out_step, jnp.zeros(query_rot.shape, f32), jnp.arange(blocks, dtype=jnp.int32)
    )
    return (attended, log_total)


def attention_backward(
    query_rot,
    keys_all,
    values_all,
    grad_attended,
    log_total,
    doc_ids,
    query_ids,
    query_index,
    block_size,
):
    rows_here, query_count, head_count, head_size = query_rot.shape
    length = keys_all.shape[1]
    width = keys_all.shape[2]
    blocks = length // block_size
    f32 = jnp.float32
    bf16 = jnp.bfloat16

    def inner_step(accumulated, block_index):
        block_start = block_index * block_size
        soft_probs = block_probs(
            query_rot, keys_all, doc_ids, query_ids, query_index, log_total, block_start, block_size
        )
        value_block = key_slice(values_all, block_start, block_size, head_size)
        grad_probs = jnp.einsum(
            "rqhd,rkhd->rhqk", grad_attended, value_block, preferred_element_type=f32
        )
        return (accumulated + jnp.sum(soft_probs * grad_probs, axis=-1), None)

    row_inner, _ = lax.scan(
        inner_step,
        jnp.zeros((rows_here, head_count, query_count), f32),
        jnp.arange(blocks, dtype=jnp.int32),
    )
    kv_shape = (rows_here, block_size, width)

    def grad_step(accumulated, block_index):
        block_start = block_index * block_size
        grad_accumulated = accumulated
        soft_probs = block_probs(
            query_rot, keys_all, doc_ids, query_ids, query_index, log_total, block_start, block_size
        )
        key_block = key_slice(keys_all, block_start, block_size, head_size)
        value_block = key_slice(values_all, block_start, block_size, head_size)
        grad_probs = jnp.einsum(
            "rqhd,rkhd->rhqk", grad_attended, value_block, preferred_element_type=f32
        )
        grad_scores = (soft_probs * (grad_probs - row_inner[..., None]) * 0.125).astype(bf16)
        grad_accumulated = grad_accumulated + jnp.einsum(
            "rhqk,rkhd->rqhd", grad_scores, key_block, preferred_element_type=f32
        )
        key_grad = jnp.einsum("rhqk,rqhd->rkhd", grad_scores, query_rot, preferred_element_type=f32)
        value_grad = jnp.einsum(
            "rhqk,rqhd->rkhd", soft_probs.astype(bf16), grad_attended, preferred_element_type=f32
        )
        accumulated, key_grad, value_grad = (
            grad_accumulated,
            key_grad.reshape(kv_shape),
            value_grad.reshape(kv_shape),
        )
        return (accumulated, (key_grad, value_grad))

    query_grad, (key_grads, value_grads) = lax.scan(
        grad_step, jnp.zeros(query_rot.shape, f32), jnp.arange(blocks, dtype=jnp.int32)
    )
    key_grad_row = jnp.moveaxis(key_grads, 0, 1).reshape(rows_here, length, width)
    value_grad_row = jnp.moveaxis(value_grads, 0, 1).reshape(rows_here, length, width)
    return (query_grad, key_grad_row, value_grad_row)


def gather_attention(norm1_gain, w_query, w_key, w_value, w_out):
    return (
        lax.all_gather(norm1_gain, ("dp", "seq"), axis=0, tiled=True),
        lax.all_gather(w_query, ("dp", "seq"), axis=0, tiled=True),
        lax.all_gather(w_key, ("dp", "seq"), axis=0, tiled=True),
        lax.all_gather(w_value, ("dp", "seq"), axis=0, tiled=True),
        lax.all_gather(w_out, ("dp", "seq"), axis=0, tiled=True),
    )


def layer_gathered(
    tokens,
    doc_ids,
    cotangent,
    norm1_gain,
    w_query,
    w_key,
    w_value,
    w_out,
    norm2_gain,
    w_gate,
    w_up,
    w_down,
):
    rows_here, shard_len, model_width = tokens.shape
    head_count = H
    head_size = HD
    length = doc_ids.shape[1]
    block_size = min(512, length)
    offset = lax.axis_index("seq") * shard_len
    tok_count = rows_here * shard_len
    bf16 = jnp.bfloat16
    f32 = jnp.float32
    gain_one, query_weight, key_weight, value_weight, out_weight = gather_attention(
        norm1_gain, w_query, w_key, w_value, w_out
    )
    cos_all, sin_all = rope_angles(doc_ids, head_size)
    cos_here = lax.dynamic_slice_in_dim(cos_all, offset, shard_len, 1)
    sin_here = lax.dynamic_slice_in_dim(sin_all, offset, shard_len, 1)
    query_ids = lax.dynamic_slice_in_dim(doc_ids, offset, shard_len, 1)
    query_index = offset + lax.broadcasted_iota(jnp.int32, (shard_len,), 0)
    inputs = tokens.astype(f32).reshape(tok_count, model_width)
    scale_one = rms_scale(inputs)
    gain_first = gain_one.astype(f32)
    normed_one = (inputs * scale_one * gain_first).astype(bf16)
    query_pre = jnp.dot(normed_one, query_weight, preferred_element_type=f32)
    key_pre = jnp.dot(normed_one, key_weight, preferred_element_type=f32)
    value_pre = jnp.dot(normed_one, value_weight, preferred_element_type=f32)
    head_shape = (rows_here, shard_len, head_count, head_size)
    query_rot = rotate(query_pre.reshape(head_shape), cos_here, sin_here).astype(bf16)
    key_rot = (
        rotate(key_pre.reshape(head_shape), cos_here, sin_here)
        .astype(bf16)
        .reshape(rows_here, shard_len, model_width)
    )
    value_low = value_pre.astype(bf16).reshape(rows_here, shard_len, model_width)
    keys_all, values_all = (
        lax.all_gather(key_rot, "seq", axis=1, tiled=True),
        lax.all_gather(value_low, "seq", axis=1, tiled=True),
    )
    attended, log_total = attention_forward(
        query_rot, keys_all, values_all, doc_ids, query_ids, query_index, block_size
    )
    attended_low = attended.reshape(tok_count, model_width).astype(bf16)
    hidden_state = inputs + jnp.dot(attended_low, out_weight, preferred_element_type=f32)
    gain_two, gate_weight, up_weight, down_weight = (
        lax.all_gather(norm2_gain, ("dp", "seq"), axis=0, tiled=True),
        lax.all_gather(w_gate, ("dp", "seq"), axis=0, tiled=True),
        lax.all_gather(w_up, ("dp", "seq"), axis=0, tiled=True),
        lax.all_gather(w_down, ("dp", "seq"), axis=0, tiled=True),
    )
    scale_two = rms_scale(hidden_state)
    gain_second = gain_two.astype(f32)
    normed_two = (hidden_state * scale_two * gain_second).astype(bf16)
    gate_pre = jnp.dot(normed_two, gate_weight, preferred_element_type=f32)
    up_pre = jnp.dot(normed_two, up_weight, preferred_element_type=f32)
    sigmoid_gate = jax.nn.sigmoid(gate_pre)
    silu_gate = gate_pre * sigmoid_gate
    activated = (silu_gate * up_pre).astype(bf16)
    result = hidden_state + jnp.dot(activated, down_weight, preferred_element_type=f32)
    out_tokens = result.astype(bf16).reshape(rows_here, shard_len, model_width)
    gain_two, gate_weight, up_weight, down_weight = (
        lax.all_gather(norm2_gain, ("dp", "seq"), axis=0, tiled=True),
        lax.all_gather(w_gate, ("dp", "seq"), axis=0, tiled=True),
        lax.all_gather(w_up, ("dp", "seq"), axis=0, tiled=True),
        lax.all_gather(w_down, ("dp", "seq"), axis=0, tiled=True),
    )
    gain_second = gain_two.astype(f32)
    grad_result = cotangent.astype(f32).reshape(tok_count, model_width)
    grad_mlp = grad_result.astype(bf16)
    grad_act = jnp.dot(grad_mlp, down_weight.T, preferred_element_type=f32)
    grad_gate_pre = (
        grad_act * up_pre * sigmoid_gate * (1.0 + gate_pre * (1.0 - sigmoid_gate))
    ).astype(bf16)
    grad_up_pre = (grad_act * silu_gate).astype(bf16)
    grad_normed_two = jnp.dot(grad_gate_pre, gate_weight.T, preferred_element_type=f32) + jnp.dot(
        grad_up_pre, up_weight.T, preferred_element_type=f32
    )
    grad_hidden_norm, gain_two_term = norm_back(
        hidden_state, scale_two, gain_second, grad_normed_two
    )
    grad_hidden = grad_result + grad_hidden_norm
    mlp_terms = (
        gain_two_term,
        jnp.dot(normed_two.T, grad_gate_pre, preferred_element_type=f32),
        jnp.dot(normed_two.T, grad_up_pre, preferred_element_type=f32),
        jnp.dot(activated.T, grad_mlp, preferred_element_type=f32),
    )
    grad_norm2, grad_gate, grad_up, grad_down = (
        lax.psum_scatter(mlp_terms[0], ("dp", "seq"), scatter_dimension=0, tiled=True),
        lax.psum_scatter(mlp_terms[1], ("dp", "seq"), scatter_dimension=0, tiled=True),
        lax.psum_scatter(mlp_terms[2], ("dp", "seq"), scatter_dimension=0, tiled=True),
        lax.psum_scatter(mlp_terms[3], ("dp", "seq"), scatter_dimension=0, tiled=True),
    )
    gain_one, query_weight, key_weight, value_weight, out_weight = gather_attention(
        norm1_gain, w_query, w_key, w_value, w_out
    )
    gain_first = gain_one.astype(f32)
    grad_branch = grad_hidden.astype(bf16)
    out_term = jnp.dot(attended_low.T, grad_branch, preferred_element_type=f32)
    grad_attended = (
        jnp.dot(grad_branch, out_weight.T, preferred_element_type=f32)
        .astype(bf16)
        .reshape(head_shape)
    )
    query_grad, key_grad_row, value_grad_row = attention_backward(
        query_rot,
        keys_all,
        values_all,
        grad_attended,
        log_total,
        doc_ids,
        query_ids,
        query_index,
        block_size,
    )
    key_sum, value_sum = (
        lax.psum_scatter(
            key_grad_row.astype(jnp.bfloat16), "seq", scatter_dimension=1, tiled=True
        ).astype(jnp.float32),
        lax.psum_scatter(
            value_grad_row.astype(jnp.bfloat16), "seq", scatter_dimension=1, tiled=True
        ).astype(jnp.float32),
    )
    grad_query_pre = (
        unrotate(query_grad, cos_here, sin_here).astype(bf16).reshape(tok_count, model_width)
    )
    grad_key_pre = (
        unrotate(key_sum.reshape(head_shape), cos_here, sin_here)
        .astype(bf16)
        .reshape(tok_count, model_width)
    )
    grad_value_pre = value_sum.astype(bf16).reshape(tok_count, model_width)
    grad_normed_one = (
        jnp.dot(grad_query_pre, query_weight.T, preferred_element_type=f32)
        + jnp.dot(grad_key_pre, key_weight.T, preferred_element_type=f32)
        + jnp.dot(grad_value_pre, value_weight.T, preferred_element_type=f32)
    )
    grad_input_norm, gain_one_term = norm_back(inputs, scale_one, gain_first, grad_normed_one)
    grad_tokens = (
        (grad_hidden + grad_input_norm).astype(bf16).reshape(rows_here, shard_len, model_width)
    )
    attention_terms = (
        gain_one_term,
        jnp.dot(normed_one.T, grad_query_pre, preferred_element_type=f32),
        jnp.dot(normed_one.T, grad_key_pre, preferred_element_type=f32),
        jnp.dot(normed_one.T, grad_value_pre, preferred_element_type=f32),
        out_term,
    )
    grad_norm1, grad_query, grad_key, grad_value, grad_out = (
        lax.psum_scatter(attention_terms[0], ("dp", "seq"), scatter_dimension=0, tiled=True),
        lax.psum_scatter(attention_terms[1], ("dp", "seq"), scatter_dimension=0, tiled=True),
        lax.psum_scatter(attention_terms[2], ("dp", "seq"), scatter_dimension=0, tiled=True),
        lax.psum_scatter(attention_terms[3], ("dp", "seq"), scatter_dimension=0, tiled=True),
        lax.psum_scatter(attention_terms[4], ("dp", "seq"), scatter_dimension=0, tiled=True),
    )
    return (
        out_tokens,
        grad_tokens,
        grad_norm1,
        grad_query,
        grad_key,
        grad_value,
        grad_out,
        grad_norm2,
        grad_gate,
        grad_up,
        grad_down,
    )


def body(
    tokens,
    doc_ids,
    cotangent,
    norm1_gain,
    w_query,
    w_key,
    w_value,
    w_out,
    norm2_gain,
    w_gate,
    w_up,
    w_down,
):
    return layer_gathered(
        tokens,
        doc_ids,
        cotangent,
        norm1_gain,
        w_query,
        w_key,
        w_value,
        w_out,
        norm2_gain,
        w_gate,
        w_up,
        w_down,
    )


def solution(mesh):
    return jax.shard_map(
        body,
        mesh=mesh,
        in_specs=(
            P("dp", "seq", None),
            P("dp", None),
            P("dp", "seq", None),
            P(("dp", "seq")),
            P(("dp", "seq"), None),
            P(("dp", "seq"), None),
            P(("dp", "seq"), None),
            P(("dp", "seq"), None),
            P(("dp", "seq")),
            P(("dp", "seq"), None),
            P(("dp", "seq"), None),
            P(("dp", "seq"), None),
        ),
        out_specs=(
            P("dp", "seq", None),
            P("dp", "seq", None),
            P(("dp", "seq")),
            P(("dp", "seq"), None),
            P(("dp", "seq"), None),
            P(("dp", "seq"), None),
            P(("dp", "seq"), None),
            P(("dp", "seq")),
            P(("dp", "seq"), None),
            P(("dp", "seq"), None),
            P(("dp", "seq"), None),
        ),
        check_vma=False,
    )
```

profile of v0, /device:TPU:0, one launch (start us, length us, event | category | flops | bytes accessed | tf_op | source)
XLA Modules:
  0.0 4325.1 jit_solution(9852645094252341433)
XLA Ops:
  11.2 43.2 all-reduce.5
  60.3 30.9 all-gather.18.cloned.1.call-done
  103.6 66.6 %all-gather.14.cloned.1.call-done = bf16[2048,2048]{1,0:T(8,128)(2,1)} async-done(((bf16[64,2048]{1,0:T(8,128)(2,1)}), bf16[2048,2048]{1,0:T(8,128)(2,1)}) %all-gather.14.cloned.1.call-update) | async-done | bytes 8388624 | tf_op jit(solution)/shard_map/all_gather | solution.py:212
  193.8 55.3 %all-gather.10.cloned.1.call-done = bf16[2048,2048]{1,0:T(8,128)(2,1)} async-done(((bf16[64,2048]{1,0:T(8,128)(2,1)}), bf16[2048,2048]{1,0:T(8,128)(2,1)}) %all-gather.10.cloned.1.call-update) | async-done | bytes 8388624 | tf_op jit(solution)/shard_map/all_gather | solution.py:213
  259.8 46.2 %all-gather.16.cloned.1.call-done = bf16[2,1024,2048]{1,2,0:T(8,128)(2,1)} async-done(((bf16[2,128,2048]{1,2,0:T(8,128)(2,1)}), bf16[2,1024,2048]{1,2,0:T(8,128)(2,1)}) %all-gather.16.cloned.1.call-update) | async-done | bytes 8388624 | tf_op jit(solution)/shard_map/all_gather | solution.py:265
  306.0 41.0 while.50
  364.3 39.7 while.51
  407.0 37.5 all-gather.20.cloned.1.call-done
  451.9 188.8 %all-gather.22.cloned.1.call-done = bf16[2048,8192]{1,0:T(8,128)(2,1)} async-done(((bf16[64,8192]{1,0:T(8,128)(2,1)}), bf16[2048,8192]{1,0:T(8,128)(2,1)}) %all-gather.22.cloned.1.call-update) | async-done | bytes 33554448 | tf_op jit(solution)/shard_map/all_gather | solution.py:275
  658.6 178.0 %all-gather.24.cloned.1.call-done = bf16[2048,8192]{1,0:T(8,128)(2,1)} async-done(((bf16[64,8192]{1,0:T(8,128)(2,1)}), bf16[2048,8192]{1,0:T(8,128)(2,1)}) %all-gather.24.cloned.1.call-update) | async-done | bytes 33554448 | tf_op jit(solution)/shard_map/all_gather | solution.py:276
  854.5 177.9 %all-gather.26.cloned.1.call-done = bf16[8192,2048]{1,0:T(8,128)(2,1)} async-done(((bf16[256,2048]{1,0:T(8,128)(2,1)}), bf16[8192,2048]{1,0:T(8,128)(2,1)}) %all-gather.26.cloned.1.call-update) | async-done | bytes 33554448 | tf_op jit(solution)/shard_map/all_gather | solution.py:277
  1105.3 41.8 while.52
  1147.1 144.0 %while.53 = (s32[]{:T(128)}, f32[2,128,32,64]{1,3,2,0:T(8,128)S(1)}, bf16[2,2,512,2048]{3,2,0,1:T(8,128)(2,1)}, bf16[2,2,512,2048]{3,2,0,1:T(8,128)(2,1)}, s32[2...) while((s32[]{:T(128)}, ...), condition=%wide.region_15.16_spmd.clone, body=%wide.region_14.15_spmd.clone.sunk | while | flops 2731868672 | bytes 206162304 | solution.py:200
  1305.2 55.5 %reduce-scatter.10.cloned.1.call-done = bf16[2,128,2048]{2,1,0:T(8,128)(2,1)} async-done(((bf16[2,1024,2048]{2,1,0:T(8,128)(2,1)}), bf16[2,128,2048]{2,1,0:T(8,128)(2,1)}) %reduce-scatter.10.cloned.1.call-update) | async-done | bytes 1048592 | tf_op jit(solution)/shard_map/reduce_scatter | solution.py:345
  1389.1 46.8 %reduce-scatter.12.cloned.1.call-done = bf16[2,128,2048]{2,1,0:T(8,128)(2,1)} async-done(((bf16[2,1024,2048]{2,1,0:T(8,128)(2,1)}), bf16[2,128,2048]{2,1,0:T(8,128)(2,1)}) %reduce-scatter.12.cloned.1.call-update) | async-done | bytes 1048592 | tf_op jit(solution)/shard_map/reduce_scatter | solution.py:348
  1446.7 26.2 fusion.83
  1473.0 26.2 fusion.84
  1562.5 42.5 all-reduce.4
  1622.9 187.3 %reduce-scatter.14.cloned.1.call-done = f32[64,2048]{1,0:T(8,128)} async-done(((f32[2048,2048]{1,0:T(8,128)}), f32[64,2048]{1,0:T(8,128)}) %reduce-scatter.14.cloned.1.call-update) | async-done | bytes 524304 | tf_op jit(solution)/shard_map/reduce_scatter | solution.py:379
  1810.3 187.1 %reduce-scatter.16.cloned.1.call-done = f32[64,2048]{1,0:T(8,128)} async-done(((f32[2048,2048]{1,0:T(8,128)}), f32[64,2048]{1,0:T(8,128)}) %reduce-scatter.16.cloned.1.call-update) | async-done | bytes 524304 | tf_op jit(solution)/shard_map/reduce_scatter | solution.py:380
  1997.4 187.2 %reduce-scatter.18.cloned.1.call-done = f32[64,2048]{1,0:T(8,128)} async-done(((f32[2048,2048]{1,0:T(8,128)}), f32[64,2048]{1,0:T(8,128)}) %reduce-scatter.18.cloned.1.call-update) | async-done | bytes 524304 | tf_op jit(solution)/shard_map/reduce_scatter | solution.py:381
  2184.6 707.2 %reduce-scatter.22.cloned.1.call-done = f32[64,8192]{1,0:T(8,128)} async-done(((f32[2048,8192]{1,0:T(8,128)}), f32[64,8192]{1,0:T(8,128)}) %reduce-scatter.22.cloned.1.call-update) | async-done | bytes 2097168 | tf_op jit(solution)/shard_map/reduce_scatter | solution.py:318
  2891.8 713.0 %reduce-scatter.24.cloned.1.call-done = f32[64,8192]{1,0:T(8,128)} async-done(((f32[2048,8192]{1,0:T(8,128)}), f32[64,8192]{1,0:T(8,128)}) %reduce-scatter.24.cloned.1.call-update) | async-done | bytes 2097168 | tf_op jit(solution)/shard_map/reduce_scatter | solution.py:319
  3604.8 713.1 %reduce-scatter.26.cloned.1.call-done = f32[256,2048]{1,0:T(8,128)} async-done(((f32[8192,2048]{1,0:T(8,128)}), f32[256,2048]{1,0:T(8,128)}) %reduce-scatter.26.cloned.1.call-update) | async-done | bytes 2097168 | tf_op jit(solution)/shard_map/reduce_scatter | solution.py:320
  (315 shorter events, 586.3 us)
Async XLA Ops:
  7.2 84.1 %all-gather.18.cloned.1.call-start = ((), (), s32[]{:S(2)}) async-start(), calls=%async_computation.13 | async-start | bytes 8650752 | tf_op jit(solution)/shard_map/all_gather | solution.py:211
  7.9 162.3 %all-gather.14.cloned.1.call-start = ((), (), s32[]{:S(2)}) async-start(), calls=%async_computation.11 | async-start | bytes 8650752 | tf_op jit(solution)/shard_map/all_gather | solution.py:212
  8.7 240.5 %all-gather.10.cloned.1.call-start = ((), (), s32[]{:S(2)}) async-start(), calls=%async_computation.9 | async-start | bytes 8650752 | tf_op jit(solution)/shard_map/all_gather | solution.py:213
  9.4 296.6 %all-gather.16.cloned.1.call-start = ((), (), s32[]{:S(2)}) async-start(), calls=%async_computation.12 | async-start | bytes 9437184 | tf_op jit(solution)/shard_map/all_gather | solution.py:265
  54.4 138.1 %copy-start.32 = (f32[2048]{0:T(1024)}, f32[2048]{0:T(1024)S(1)}, u32[]{:S(2)}) copy-start(f32[2048]{0:T(1024)S(1)} %convert_element_type.130) | copy-start | bytes 24580
  57.2 133.5 %copy-start.28 = (f32[2,128,32]{1,2,0:T(8,128)}, f32[2,128,32]{1,2,0:T(8,128)S(1)}, u32[]{:S(2)}) copy-start(f32[2,128,32]{1,2,0:T(8,128)S(1)} %get-tuple-element.615) | copy-start | bytes 98308
  57.2 133.5 %copy-start.30 = (f32[2,128,32]{1,2,0:T(8,128)}, f32[2,128,32]{1,2,0:T(8,128)S(1)}, u32[]{:S(2)}) copy-start(f32[2,128,32]{1,2,0:T(8,128)S(1)} %get-tuple-element.616) | copy-start | bytes 98308
  58.8 133.7 %copy-start.36 = (f32[256]{0:T(256)}, f32[256]{0:T(256)S(1)}, u32[]{:S(2)}) copy-start(f32[256]{0:T(256)S(1)} %get-tuple-element.624) | copy-start | bytes 3076
  192.4 171.9 %all-gather.12.cloned.1.call-start = ((), (), s32[]{:S(2)}) async-start(), calls=%async_computation.10 | async-start | bytes 9437184 | tf_op jit(solution)/shard_map/all_gather | solution.py:266
  256.5 188.0 %all-gather.20.cloned.1.call-start = ((), (), s32[]{:S(2)}) async-start(), calls=%async_computation.14 | async-start | bytes 8650752 | tf_op jit(solution)/shard_map/all_gather | solution.py:214
  257.1 383.6 %all-gather.22.cloned.1.call-start = ((), (), s32[]{:S(2)}) async-start(), calls=%async_computation.15 | async-start | bytes 34603008 | tf_op jit(solution)/shard_map/all_gather | solution.py:275
  257.8 578.7 %all-gather.24.cloned.1.call-start = ((), (), s32[]{:S(2)}) async-start(), calls=%async_computation.16 | async-start | bytes 34603008 | tf_op jit(solution)/shard_map/all_gather | solution.py:276
  258.6 773.8 %all-gather.26.cloned.1.call-start = ((), (), s32[]{:S(2)}) async-start(), calls=%async_computation.17 | async-start | bytes 34603008 | tf_op jit(solution)/shard_map/all_gather | solution.py:277
  259.3 1101.4 %reduce-scatter.10.cloned.1.call-start = ((), (), s32[]{:S(2)}) async-start(), calls=%async_computation.18 | async-start | bytes 9437184 | tf_op jit(solution)/shard_map/reduce_scatter | solution.py:345
  451.9 384.7 %copy-start.13 = (bf16[256,2048]{1,0:T(8,128)(2,1)}, bf16[256,2048]{1,0:T(8,128)(2,1)S(1)}, u32[]{:S(2)}) copy-start(bf16[256,2048]{1,0:T(8,128)(2,1)S(1)} %multiply_convert_fusion.3) | copy-start | bytes 3145732
  658.6 373.8 %copy-start.16 = (bf16[2,128,2048]{2,1,0:T(8,128)(2,1)S(1)}, bf16[2,128,2048]{2,1,0:T(8,128)(2,1)}, u32[]{:S(2)}) copy-start(bf16[2,128,2048]{2,1,0:T(8,128)(2,1)} %param.22) | copy-start | bytes 3145732
  1291.1 144.8 %reduce-scatter.12.cloned.1.call-start = ((), (), s32[]{:S(2)}) async-start(), calls=%async_computation.19 | async-start | bytes 9437184 | tf_op jit(solution)/shard_map/reduce_scatter | solution.py:348
  1291.9 331.1 %reduce-scatter.20.cloned.1.call-start = ((), (), s32[]{:S(2)}) async-start(), calls=%async_computation.23 | async-start | bytes 17301504 | tf_op jit(solution)/shard_map/reduce_scatter | solution.py:382
  1305.2 505.1 %reduce-scatter.14.cloned.1.call-start = ((), (), s32[]{:S(2)}) async-start(), calls=%async_computation.20 | async-start | bytes 17301504 | tf_op jit(solution)/shard_map/reduce_scatter | solution.py:379
  1378.5 618.9 %reduce-scatter.16.cloned.1.call-start = ((), (), s32[]{:S(2)}) async-start(), calls=%async_computation.21 | async-start | bytes 17301504 | tf_op jit(solution)/shard_map/reduce_scatter | solution.py:380
  1388.8 795.8 %reduce-scatter.18.cloned.1.call-start = ((), (), s32[]{:S(2)}) async-start(), calls=%async_computation.22 | async-start | bytes 17301504 | tf_op jit(solution)/shard_map/reduce_scatter | solution.py:381
  1445.5 1446.3 %reduce-scatter.22.cloned.1.call-start = ((), (), s32[]{:S(2)}) async-start(), calls=%async_computation.24 | async-start | bytes 69206016 | tf_op jit(solution)/shard_map/reduce_scatter | solution.py:318
  1472.9 2131.8 %reduce-scatter.24.cloned.1.call-start = ((), (), s32[]{:S(2)}) async-start(), calls=%async_computation.25 | async-start | bytes 69206016 | tf_op jit(solution)/shard_map/reduce_scatter | solution.py:319
  1499.2 2818.6 %reduce-scatter.26.cloned.1.call-start = ((), (), s32[]{:S(2)}) async-start(), calls=%async_computation.26 | async-start | bytes 69206016 | tf_op jit(solution)/shard_map/reduce_scatter | solution.py:320
  (46 other events, 729.7 us)
Sparse Core Ops, SparseCore 0:
  10.9 80.3 all-gather.17
  94.1 76.0 all-gather.13
  173.0 76.0 all-gather.9
  251.4 54.5 all-gather.15
  308.3 55.9 all-gather.11
  367.0 77.4 all-gather.19
  447.3 193.3 all-gather.21
  643.6 192.9 all-gather.23
  839.4 192.9 all-gather.25
  1291.2 69.4 reduce-scatter.9
  1364.6 71.2 reduce-scatter.11
  1438.6 184.2 reduce-scatter.19
  1625.8 184.4 reduce-scatter.13
  1813.0 184.3 reduce-scatter.15
  2000.1 184.4 reduce-scatter.17
  2187.4 704.3 reduce-scatter.21
  2894.6 710.1 reduce-scatter.23
  3607.6 710.2 reduce-scatter.25
where the time goes:
time: 4340 us; the launch traced here: 4330 us
  waiting for transfers between devices  3610 us (83%)
  matrix products  423 us (10%)
  local copies, waits for them, and re-layouts  141 us (3%)
  blocking collectives  85.7 us (2%)
    reduce_scatter x1, waiting for transfers between devices, layer_gathered(): lax.psum_scatter(mlp_terms[3], ('dp', 'seq'), scatter_dimension=0, tiled=...  713 us
    reduce_scatter x1, waiting for transfers between devices, layer_gathered(): lax.psum_scatter(mlp_terms[2], ('dp', 'seq'), scatter_dimension=0, tiled=...  713 us
    reduce_scatter x1, waiting for transfers between devices, layer_gathered(): lax.psum_scatter(mlp_terms[1], ('dp', 'seq'), scatter_dimension=0, tiled=...  707 us
    all_gather x1, waiting for transfers between devices, layer_gathered(): lax.all_gather(w_gate, ('dp', 'seq'), axis=0, tiled=True)  189 us
    reduce_scatter x1, waiting for transfers between devices, layer_gathered(): lax.psum_scatter(attention_terms[1], ('dp', 'seq'), scatter_dimension=0,...  187 us
    reduce_scatter x1, waiting for transfers between devices, layer_gathered(): lax.psum_scatter(attention_terms[3], ('dp', 'seq'), scatter_dimension=0,...  187 us
    reduce_scatter x1, waiting for transfers between devices, layer_gathered(): lax.psum_scatter(attention_terms[2], ('dp', 'seq'), scatter_dimension=0,...  187 us
    all_gather x1, waiting for transfers between devices, layer_gathered(): lax.all_gather(w_up, ('dp', 'seq'), axis=0, tiled=True)  178 us
  transfers between devices with their start and end apart: 18, of which 18 were waited for; matrix products, arithmetic and copies ran while one was open for 8% of the time, Pallas kernels for 0%

commit v1 on v0

v1 whole, which is shorter than its diff:
```python
import functools

import jax
import jax.numpy as jnp
from jax import lax
from jax.experimental import pallas as pl
from jax.experimental.pallas import tpu as pltpu
from jax.sharding import PartitionSpec as P

H = 32
HD = 64
PAIR = 2 * HD

rope_base = 130000.0
norm_eps = 1e-05

bf16 = jnp.bfloat16
f32 = jnp.float32
MESH = pl.DeviceIdType.MESH
ANY = pl.BlockSpec(memory_space=pl.ANY)
VMEM = pl.BlockSpec(memory_space=pltpu.VMEM)
DMA = pltpu.SemaphoreType.DMA
MIB = 1 << 20


def plane():
    dp, s = lax.axis_index("dp"), lax.axis_index("seq")
    core, xb, yb = lax.rem(s, 2), lax.rem(lax.div(s, 2), 2), lax.div(s, 4)
    at = lambda y, x, c: y * 4 + x * 2 + c
    return dict(
        dp=dp,
        me=s,
        sib=at(yb, xb, 1 - core),
        xp=at(yb, 1 - xb, core),
        yp=at(1 - yb, xb, core),
        dg=at(1 - yb, 1 - xb, core),
        xs=at(yb, 1 - xb, 1 - core),
        ys=at(1 - yb, xb, 1 - core),
        ds=at(1 - yb, 1 - xb, 1 - core),
    )


def greet(p, names):
    barrier = pltpu.get_barrier_semaphore()
    for name in names:
        pl.semaphore_signal(barrier, inc=1, device_id=(p["dp"], p[name]), device_id_type=MESH)
    pl.semaphore_wait(barrier, len(names))


def remote(p, src, dst, send, recv, i, to):
    return pltpu.make_async_remote_copy(
        src_ref=src,
        dst_ref=dst,
        send_sem=send.at[i],
        recv_sem=recv.at[i],
        device_id=(p["dp"], p[to]),
        device_id_type=MESH,
    )


GATHER_SEMS = 25


def gather_start(p, src, out, send, recv, base):
    quarter = src.shape[0] // 4
    part = lambda ref, k: ref.at[pl.ds(k * quarter, quarter)]
    mine = out.at[p["me"]]
    sent = {}
    for j in range(4):
        kx, ky = j, (j + 2) % 4
        sent["x", kx] = remote(p, part(src, kx), part(mine, kx), send, recv, base + kx, "xp")
        sent["y", ky] = remote(p, part(src, ky), part(mine, ky), send, recv, base + 4 + ky, "yp")
        sent["x", kx].start()
        sent["y", ky].start()
    sent["s"] = remote(p, src, mine, send, recv, base + 8, "sib")
    sent["s"].start()
    return sent


def gather_finish(p, sent, src, out, send, recv, base):
    quarter = src.shape[0] // 4
    part = lambda ref, k: ref.at[pl.ds(k * quarter, quarter)]
    passed = []

    def forward(owner, k, i, to):
        ref = part(out.at[p[owner]], k)
        copy = remote(p, ref, ref, send, recv, base + i, to)
        copy.start()
        return copy

    for j in range(4):
        kx, ky = j, (j + 2) % 4
        sent["x", kx].wait_recv()
        if j < 2:
            sent["far", kx] = forward("xp", kx, 9 + kx, "yp")
        passed.append(forward("xp", kx, 13 + kx, "sib"))
        sent["y", ky].wait_recv()
        if j < 2:
            sent["far", ky] = forward("yp", ky, 9 + ky, "xp")
        passed.append(forward("yp", ky, 17 + ky, "sib"))
    for k in (0, 2, 1, 3):
        sent["far", k].wait_recv()
        passed.append(forward("dg", k, 21 + k, "sib"))
    sent["s"].wait_recv()
    for copy in passed:
        copy.wait_recv()
    for copy in list(sent.values()) + passed:
        copy.wait_send()


def gather_kernel(count, *refs):
    sources, outs = refs[:count], refs[count : 2 * count]
    send, recv, local = refs[2 * count :]
    p = plane()
    greet(p, ("sib", "xp", "yp"))
    sent, kept = [], []
    for i in range(count):
        sent.append(gather_start(p, sources[i], outs[i], send, recv, i * GATHER_SEMS))
        kept.append(pltpu.make_async_copy(sources[i], outs[i].at[p["me"]], local.at[i]))
        kept[i].start()
    for i in range(count):
        gather_finish(p, sent[i], sources[i], outs[i], send, recv, i * GATHER_SEMS)
    for copy in kept:
        copy.wait()


def gather_plane(arrays, shards, collective_id):
    if shards != 8:
        return [lax.all_gather(a, "seq") for a in arrays]
    count = len(arrays)
    return pl.pallas_call(
        functools.partial(gather_kernel, count),
        out_shape=[jax.ShapeDtypeStruct((8,) + a.shape, a.dtype) for a in arrays],
        in_specs=[ANY] * count,
        out_specs=[ANY] * count,
        scratch_shapes=[DMA((GATHER_SEMS * count,)), DMA((GATHER_SEMS * count,)), DMA((count,))],
        compiler_params=pltpu.CompilerParams(collective_id=collective_id, has_side_effects=True),
    )(*arrays)


def exchange_kernel(count, *refs):
    sources, outs = refs[:count], refs[count : 2 * count]
    send, recv, local = refs[2 * count :]
    p = plane()
    names = ("dg", "ds", "xp", "yp", "xs", "ys", "sib")
    greet(p, names)
    copies = []
    for i in range(count):
        for j, name in enumerate(names):
            copies.append(
                remote(
                    p, sources[i].at[p[name]], outs[i].at[p["me"]], send, recv, i * 7 + j, name
                )
            )
            copies[-1].start()
        copies.append(
            pltpu.make_async_copy(sources[i].at[p["me"]], outs[i].at[p["me"]], local.at[i])
        )
        copies[-1].start()
    for copy in copies:
        copy.wait()


def exchange_plane(arrays, shards, collective_id):
    if shards != 8:
        return [lax.all_to_all(a, "seq", split_axis=0, concat_axis=0) for a in arrays]
    count = len(arrays)
    return pl.pallas_call(
        functools.partial(exchange_kernel, count),
        out_shape=[jax.ShapeDtypeStruct(a.shape, a.dtype) for a in arrays],
        in_specs=[ANY] * count,
        out_specs=[ANY] * count,
        scratch_shapes=[DMA((7 * count,)), DMA((7 * count,)), DMA((count,))],
        compiler_params=pltpu.CompilerParams(collective_id=collective_id, has_side_effects=True),
    )(*arrays)


BLOCK = 16


def over_rows(rows, step):
    @pl.loop(0, rows // BLOCK)
    def _(i):
        step(pl.ds(pl.multiple_of(i * BLOCK, BLOCK), BLOCK))


def scatter_scratch(rows, width):
    return [
        pltpu.VMEM((4, rows, width), bf16),
        pltpu.VMEM((4, rows, width), bf16),
        pltpu.VMEM((2, rows // 2, width), bf16),
        pltpu.VMEM((2, rows, width), bf16),
        DMA((12,)),
        DMA((12,)),
        DMA((4,)),
    ]


def scatter_plane(p, terms, kept, paired, far, final, send, recv, local):
    rows = terms.shape[1]
    half = rows // 2
    low, high = pl.ds(0, half), pl.ds(half, half)
    order = ((3, "dg", "ds"), (1, "xp", "xs"), (2, "yp", "ys"), (0, "me", "sib"))
    loads, pairs, sends = {}, {}, []
    for i, own, other in order:
        loads[i] = pltpu.make_async_copy(terms.at[p[own]], kept.at[i], local.at[i])
        loads[i].start()
        pairs[i] = remote(p, terms.at[p[other]], paired.at[i], send, recv, i, "sib")
        pairs[i].start()

    def add_pair(i):
        loads[i].wait()
        pairs[i].wait_recv()

        def step(at):
            kept[i, at, :] = (kept[i, at, :].astype(f32) + paired[i, at, :].astype(f32)).astype(
                bf16
            )

        over_rows(rows, step)

    def put(src, dst, i, to):
        copy = remote(p, src, dst, send, recv, i, to)
        copy.start()
        sends.append(copy)
        return copy

    add_pair(3)
    far_x = put(kept.at[3, low], far.at[0], 4, "xp")
    far_y = put(kept.at[3, high], far.at[1], 5, "yp")
    add_pair(1)
    near = [put(kept.at[1, low], final.at[0, low], 6, "xp")]
    add_pair(2)
    near.append(put(kept.at[2, high], final.at[1, high], 7, "yp"))
    far_x.wait_recv()

    def step_x(at):
        kept[2, at, :] = (kept[2, at, :].astype(f32) + far[0, at, :].astype(f32)).astype(bf16)

    over_rows(half, step_x)
    near.append(put(kept.at[2, low], final.at[1, low], 8, "yp"))
    far_y.wait_recv()

    def step_y(at):
        up = pl.ds(pl.multiple_of(at.start + half, BLOCK), BLOCK)
        kept[1, up, :] = (kept[1, up, :].astype(f32) + far[1, at, :].astype(f32)).astype(bf16)

    over_rows(half, step_y)
    near.append(put(kept.at[1, high], final.at[0, high], 9, "xp"))
    loads[0].wait()
    pairs[0].wait_recv()
    for copy in near:
        copy.wait_recv()
    return sends + list(pairs.values())


def total(kept, paired, final, at):
    return (kept[0, at, :].astype(f32) + paired[0, at, :].astype(f32)) + (
        final[0, at, :].astype(f32) + final[1, at, :].astype(f32)
    )


def forward_kernel(
    terms, tokens, gain, hidden, normed, kept, paired, far, final, send, recv, local, mine, gsend, grecv
):
    p = plane()
    greet(p, ("sib", "xp", "yp"))
    sends = scatter_plane(p, terms, kept, paired, far, final, send, recv, local)

    def step(at):
        h = tokens[at, :].astype(f32) + total(kept, paired, final, at)
        hidden[at, :] = h
        scale = lax.rsqrt(jnp.mean(h * h, axis=-1, keepdims=True) + norm_eps)
        mine[at, :] = (h * scale * gain[...]).astype(bf16)

    over_rows(tokens.shape[0], step)
    sent = gather_start(p, mine, normed, gsend, grecv, 0)
    own = pltpu.make_async_copy(mine, normed.at[p["me"]], local.at[0])
    own.start()
    gather_finish(p, sent, mine, normed, gsend, grecv, 0)
    own.wait()
    for copy in sends:
        copy.wait_send()


def reduce_plane(terms):
    rows = terms.shape[1]
    return lax.psum_scatter(terms, "seq", scatter_dimension=0, tiled=False).astype(f32).reshape(
        rows, terms.shape[2]
    )


def rms_scale(values):
    return lax.rsqrt(jnp.mean(values * values, axis=-1, keepdims=True) + norm_eps)


def forward_plane(terms, tokens, gain, collective_id):
    shards, rows, width = terms.shape
    if shards != 8:
        hidden = tokens.astype(f32) + reduce_plane(terms)
        normed = (hidden * rms_scale(hidden) * gain).astype(bf16)
        return hidden, lax.all_gather(normed, "seq")
    return pl.pallas_call(
        forward_kernel,
        out_shape=[
            jax.ShapeDtypeStruct((rows, width), f32),
            jax.ShapeDtypeStruct((8, rows, width), bf16),
        ],
        in_specs=[ANY, VMEM, VMEM],
        out_specs=[VMEM, ANY],
        scratch_shapes=scatter_scratch(rows, width)
        + [pltpu.VMEM((rows, width), bf16), DMA((GATHER_SEMS,)), DMA((GATHER_SEMS,))],
        compiler_params=pltpu.CompilerParams(
            collective_id=collective_id, has_side_effects=True, vmem_limit_bytes=40 * MIB
        ),
    )(terms, tokens, gain)


def middle_kernel(
    terms,
    cotangent,
    hidden,
    gain,
    grad_hidden,
    gain_term,
    branch,
    kept,
    paired,
    far,
    final,
    send,
    recv,
    local,
    mine,
    gsend,
    grecv,
):
    p = plane()
    greet(p, ("sib", "xp", "yp"))
    sends = scatter_plane(p, terms, kept, paired, far, final, send, recv, local)
    gain_term[...] = jnp.zeros_like(gain_term)

    def step(at):
        g = total(kept, paired, final, at)
        h = hidden[at, :]
        scale = lax.rsqrt(jnp.mean(h * h, axis=-1, keepdims=True) + norm_eps)
        weighted = g * gain[...]
        inner = jnp.mean(weighted * h, axis=-1, keepdims=True)
        out = cotangent[at, :].astype(f32) + scale * weighted - h * (scale * scale * scale * inner)
        grad_hidden[at, :] = out
        mine[at, :] = out.astype(bf16)
        gain_term[...] += jnp.sum(g * h * scale, axis=0, keepdims=True)

    over_rows(hidden.shape[0], step)
    sent = gather_start(p, mine, branch, gsend, grecv, 0)
    own = pltpu.make_async_copy(mine, branch.at[p["me"]], local.at[0])
    own.start()
    gather_finish(p, sent, mine, branch, gsend, grecv, 0)
    own.wait()
    for copy in sends:
        copy.wait_send()


def norm_back(values, scale, gain, grad):
    weighted = grad * gain
    inner = jnp.mean(weighted * values, axis=-1, keepdims=True)
    return (
        scale * weighted - values * (scale * scale * scale) * inner,
        jnp.sum(grad * values * scale, axis=0, keepdims=True),
    )


def middle_plane(terms, cotangent, hidden, gain, collective_id):
    shards, rows, width = terms.shape
    if shards != 8:
        back, gain_term = norm_back(hidden, rms_scale(hidden), gain, reduce_plane(terms))
        grad_hidden = cotangent.astype(f32) + back
        return grad_hidden, gain_term, lax.all_gather(grad_hidden.astype(bf16), "seq")
    return pl.pallas_call(
        middle_kernel,
        out_shape=[
            jax.ShapeDtypeStruct((rows, width), f32),
            jax.ShapeDtypeStruct((1, width), f32),
            jax.ShapeDtypeStruct((8, rows, width), bf16),
        ],
        in_specs=[ANY, VMEM, VMEM, VMEM],
        out_specs=[VMEM, VMEM, ANY],
        scratch_shapes=scatter_scratch(rows, width)
        + [pltpu.VMEM((rows, width), bf16), DMA((GATHER_SEMS,)), DMA((GATHER_SEMS,))],
        compiler_params=pltpu.CompilerParams(
            collective_id=collective_id, has_side_effects=True, vmem_limit_bytes=44 * MIB
        ),
    )(terms, cotangent, hidden, gain)


def last_kernel(
    terms,
    out_terms,
    tokens,
    hidden,
    grad_hidden,
    gain,
    grad_tokens,
    gain_term,
    out_tokens,
    *scratch,
):
    p = plane()
    greet(p, ("sib", "xp", "yp"))
    kept, paired, far, final, send, recv, local = scratch[:7]
    sends = scatter_plane(p, terms, kept, paired, far, final, send, recv, local)
    gain_term[...] = jnp.zeros_like(gain_term)

    def step(at):
        g = total(kept, paired, final, at)
        t = tokens[at, :].astype(f32)
        scale = lax.rsqrt(jnp.mean(t * t, axis=-1, keepdims=True) + norm_eps)
        weighted = g * gain[...]
        inner = jnp.mean(weighted * t, axis=-1, keepdims=True)
        grad_tokens[at, :] = (
            grad_hidden[at, :] + scale * weighted - t * (scale * scale * scale * inner)
        ).astype(bf16)
        gain_term[...] += jnp.sum(g * t * scale, axis=0, keepdims=True)

    over_rows(tokens.shape[0], step)
    kept, paired, far, final, send, recv, local = scratch[7:]
    sends += scatter_plane(p, out_terms, kept, paired, far, final, send, recv, local)

    def step_out(at):
        out_tokens[at, :] = (hidden[at, :] + total(kept, paired, final, at)).astype(bf16)

    over_rows(tokens.shape[0], step_out)
    for copy in sends:
        copy.wait_send()


def last_plane(terms, out_terms, tokens, hidden, grad_hidden, gain, collective_id):
    shards, rows, width = terms.shape
    if shards != 8:
        values = tokens.astype(f32)
        back, gain_term = norm_back(values, rms_scale(values), gain, reduce_plane(terms))
        return (
            (grad_hidden + back).astype(bf16),
            gain_term,
            (hidden + reduce_plane(out_terms)).astype(bf16),
        )
    return pl.pallas_call(
        last_kernel,
        out_shape=[
            jax.ShapeDtypeStruct((rows, width), bf16),
            jax.ShapeDtypeStruct((1, width), f32),
            jax.ShapeDtypeStruct((rows, width), bf16),
        ],
        in_specs=[ANY, ANY, VMEM, VMEM, VMEM, VMEM],
        out_specs=[VMEM, VMEM, VMEM],
        scratch_shapes=scatter_scratch(rows, width) * 2,
        compiler_params=pltpu.CompilerParams(
            collective_id=collective_id, has_side_effects=True, vmem_limit_bytes=48 * MIB
        ),
    )(terms, out_terms, tokens, hidden, grad_hidden, gain)


def swap_halves(v, first):
    width = v.shape[-1]
    return jnp.where(first, pltpu.roll(v, width - HD // 2, 1), pltpu.roll(v, HD // 2, 1))


def dot_t(a, b):
    return lax.dot_general(a, b, (((1,), (1,)), ((), ())), preferred_element_type=f32)


def dot(a, b):
    return jnp.dot(a, b, preferred_element_type=f32)


def allowed_pairs(start, keys, queries, offset):
    key = lax.broadcasted_iota(jnp.int32, (keys, queries), 0)
    query = lax.broadcasted_iota(jnp.int32, (keys, queries), 1) + offset
    return (key >= start) & (key <= query)


def attend_kernel(pre, cos, sin, starts, rotated, attended, stats):
    shards, _, shard_len, _ = pre.shape
    length = shards * shard_len
    block = min(256, length)
    per = block // shard_len
    pre_all = pre[...].reshape(length, 3 * PAIR)
    lane = lax.broadcasted_iota(jnp.int32, (length, PAIR), 1)
    first = lax.rem(lane, HD) < HD // 2
    cos_all, sin_all = cos[...].reshape(length, PAIR), sin[...].reshape(length, PAIR)

    def rotate(v):
        return v * cos_all + swap_halves(v, first) * sin_all

    query = rotate(pre_all[:, :PAIR]).astype(bf16)
    key = rotate(pre_all[:, PAIR : 2 * PAIR]).astype(bf16)
    value = pre_all[:, 2 * PAIR :]
    value_t = value.T.astype(bf16)
    rotated[:, 0, :, :PAIR] = query.reshape(shards, shard_len, PAIR)
    rotated[:, 0, :, PAIR : 2 * PAIR] = key.reshape(shards, shard_len, PAIR)
    rotated[:, 0, :, 2 * PAIR :] = value.astype(bf16).reshape(shards, shard_len, PAIR)
    left = lax.broadcasted_iota(jnp.int32, (block, PAIR), 1) < HD
    top = lax.broadcasted_iota(jnp.int32, (PAIR, block), 0) < HD
    scaled = query * jnp.asarray(0.125, bf16)
    for i in range(length // block):
        keys = (i + 1) * block
        start = starts[0, :, i * block : (i + 1) * block]
        mask = allowed_pairs(start, keys, block, i * block)
        here = scaled[i * block : (i + 1) * block]
        results = []
        for h in range(2):
            own = jnp.where(left if h == 0 else ~left, here, jnp.zeros_like(here))
            scores = jnp.where(mask, dot_t(key[:keys], own), -1e30)
            peak = jnp.max(scores, axis=0, keepdims=True)
            shifted = jnp.exp(scores - peak)
            summed = jnp.sum(shifted, axis=0, keepdims=True)
            probs = (shifted * (1.0 / summed)).astype(bf16)
            results.append(dot(value_t[:, :keys], probs))
            stats[0, 0, h : h + 1, i * block : (i + 1) * block] = peak + jnp.log(summed)
        merged = jnp.where(top, results[0], results[1]).T.astype(bf16)
        attended[i * per : (i + 1) * per, 0, :, :] = merged.reshape(per, shard_len, PAIR)


def attend(pre, cos, sin, starts):
    shards, rows, shard_len, width = pre.shape
    pairs = width // (3 * PAIR)
    length = shards * shard_len
    wide = pl.BlockSpec((shards, 1, shard_len, 3 * PAIR), lambda r, p: (0, r, 0, p))
    narrow = pl.BlockSpec((shards, 1, shard_len, PAIR), lambda r, p: (0, r, 0, p))
    table = pl.BlockSpec((shards, 1, shard_len, PAIR), lambda r, p: (0, r, 0, 0))
    return pl.pallas_call(
        attend_kernel,
        grid=(rows, pairs),
        out_shape=[
            jax.ShapeDtypeStruct(pre.shape, bf16),
            jax.ShapeDtypeStruct((shards, rows, shard_len, pairs * PAIR), bf16),
            jax.ShapeDtypeStruct((rows, pairs, 2, length), f32),
        ],
        in_specs=[wide, table, table, pl.BlockSpec((1, 1, length), lambda r, p: (r, 0, 0))],
        out_specs=[wide, narrow, pl.BlockSpec((1, 1, 2, length), lambda r, p: (r, p, 0, 0))],
        compiler_params=pltpu.CompilerParams(vmem_limit_bytes=48 * MIB),
        cost_estimate=pl.CostEstimate(
            flops=rows * pairs * 2 * length * length * 256 * 2,
            bytes_accessed=pre.size * 8,
            transcendentals=rows * pairs * length * length,
        ),
    )(pre, cos, sin, starts)


def attend_back_kernel(rotated, grad, cos, sin, starts, stats, result, key_acc, value_acc):
    shards, _, shard_len, _ = rotated.shape
    length = shards * shard_len
    block = min(256, length)
    per = block // shard_len
    all_in = rotated[...].reshape(length, 3 * PAIR)
    query, key, value = all_in[:, :PAIR], all_in[:, PAIR : 2 * PAIR], all_in[:, 2 * PAIR :]
    grad_all = grad[...].reshape(length, PAIR)
    key_t = key.astype(f32).T.astype(bf16)
    left = lax.broadcasted_iota(jnp.int32, (block, PAIR), 1) < HD
    top = lax.broadcasted_iota(jnp.int32, (PAIR, block), 0) < HD
    first = lax.rem(lax.broadcasted_iota(jnp.int32, (length, PAIR), 1), HD) < HD // 2
    key_acc[...] = jnp.zeros_like(key_acc)
    value_acc[...] = jnp.zeros_like(value_acc)

    for i in range(length // block):
        keys = (i + 1) * block
        at = slice(i * block, (i + 1) * block)
        start = starts[0, :, at]
        mask = allowed_pairs(start, keys, block, i * block)
        results = []
        for h in range(2):
            side = left if h == 0 else ~left
            own = jnp.where(side, query[at], jnp.zeros_like(query[at]))
            own_grad = jnp.where(side, grad_all[at], jnp.zeros_like(grad_all[at]))
            scores = dot_t(key[:keys], own * jnp.asarray(0.125, bf16))
            probs = jnp.exp(jnp.where(mask, scores - stats[0, 0, h : h + 1, at], -1e30))
            grad_probs = dot_t(value[:keys], own_grad)
            inner = jnp.sum(probs * grad_probs, axis=0, keepdims=True)
            grad_scores = (probs * (grad_probs - inner) * 0.125).astype(bf16)
            key_acc[:keys, :] += dot(grad_scores, own)
            value_acc[:keys, :] += dot(probs.astype(bf16), own_grad)
            results.append(dot(key_t[:, :keys], grad_scores))
        merged = jnp.where(top, results[0], results[1]).T
        cos_here = cos[i * per : (i + 1) * per].reshape(block, PAIR)
        sin_here = sin[i * per : (i + 1) * per].reshape(block, PAIR)
        turned = merged * cos_here - swap_halves(merged, first[:block]) * sin_here
        result[i * per : (i + 1) * per, 0, :, :PAIR] = turned.astype(bf16).reshape(
            per, shard_len, PAIR
        )
    cos_all, sin_all = cos[...].reshape(length, PAIR), sin[...].reshape(length, PAIR)
    key_grad = key_acc[...]
    turned = key_grad * cos_all - swap_halves(key_grad, first) * sin_all
    result[:, 0, :, PAIR : 2 * PAIR] = turned.astype(bf16).reshape(shards, shard_len, PAIR)
    result[:, 0, :, 2 * PAIR :] = value_acc[...].astype(bf16).reshape(shards, shard_len, PAIR)


def attend_back(rotated, grad, cos, sin, starts, stats):
    shards, rows, shard_len, width = rotated.shape
    pairs = width // (3 * PAIR)
    length = shards * shard_len
    wide = pl.BlockSpec((shards, 1, shard_len, 3 * PAIR), lambda r, p: (0, r, 0, p))
    narrow = pl.BlockSpec((shards, 1, shard_len, PAIR), lambda r, p: (0, r, 0, p))
    table = pl.BlockSpec((shards, 1, shard_len, PAIR), lambda r, p: (0, r, 0, 0))
    return pl.pallas_call(
        attend_back_kernel,
        grid=(rows, pairs),
        out_shape=jax.ShapeDtypeStruct(rotated.shape, bf16),
        in_specs=[
            wide,
            narrow,
            table,
            table,
            pl.BlockSpec((1, 1, length), lambda r, p: (r, 0, 0)),
            pl.BlockSpec((1, 1, 2, length), lambda r, p: (r, p, 0, 0)),
        ],
        out_specs=wide,
        scratch_shapes=[pltpu.VMEM((length, PAIR), f32), pltpu.VMEM((length, PAIR), f32)],
        compiler_params=pltpu.CompilerParams(vmem_limit_bytes=48 * MIB),
        cost_estimate=pl.CostEstimate(
            flops=rows * pairs * 5 * length * length * 256 * 2,
            bytes_accessed=rotated.size * 6,
            transcendentals=rows * pairs * length * length,
        ),
    )(rotated, grad, cos, sin, starts, stats)


def rope_tables(doc_ids, shards):
    rows, length = doc_ids.shape
    places = lax.broadcasted_iota(jnp.int32, doc_ids.shape, 1)
    earlier = jnp.concatenate([doc_ids[:, :1], doc_ids[:, :-1]], axis=1)
    starts = lax.cummax(jnp.where(doc_ids != earlier, places, 0), axis=1)
    positions = (places - starts).astype(f32)
    frequency = rope_base ** (-(jnp.arange(HD // 2, dtype=f32) * 2.0 / HD))
    angles = positions[..., None] * frequency
    cos, sin = jnp.cos(angles), jnp.sin(angles)
    lay = lambda v: jnp.moveaxis(
        jnp.concatenate(v, axis=-1).reshape(rows, shards, length // shards, PAIR), 0, 1
    )
    return lay([cos] * 4), lay([-sin, sin, -sin, sin]), starts


def layer(
    groups,
    shards,
    tokens,
    doc_ids,
    cotangent,
    norm1_gain,
    w_query,
    w_key,
    w_value,
    w_out,
    norm2_gain,
    w_gate,
    w_up,
    w_down,
):
    rows, shard_len, width = tokens.shape
    count = rows * shard_len
    held = w_query.shape[0]
    hidden_held = w_down.shape[0]
    hidden_here = groups * hidden_held
    whole_heads = held % HD == 0
    outer, inner = (groups, held) if whole_heads else (1, width // shards)
    pairs = width // shards // PAIR
    flat = lambda v: v.reshape(shards * count, v.shape[-1])
    split = lambda v: v.reshape(shards, count, v.shape[-1])

    gains = lax.all_gather(
        jnp.stack([norm1_gain, norm2_gain]), ("dp", "seq"), axis=1, tiled=True
    ).astype(f32)
    gain_one, gain_two = gains[:1], gains[1:]

    def by_head(w):
        blocks = w.reshape(held, outer, shards, inner)
        return jnp.moveaxis(blocks, 2, 0).reshape(shards, held, pairs, PAIR)

    def by_unit(w):
        return jnp.moveaxis(w.reshape(held, groups, shards, hidden_held), 2, 0).reshape(
            shards, held, hidden_here
        )

    heads = jnp.stack([by_head(w) for w in (w_query, w_key, w_value)], axis=3)
    heads = heads.reshape(shards, held, 3 * pairs * PAIR)
    units = jnp.concatenate([by_unit(w_gate), by_unit(w_up)], axis=-1)
    heads, units = exchange_plane([heads, units], shards, 1)
    heads = heads.reshape(shards * held, heads.shape[-1])
    units = units.reshape(shards * held, units.shape[-1])
    qkv_weight = lax.all_gather(heads, "dp", axis=0, tiled=True)
    if whole_heads:
        out_weight = lax.all_gather(w_out, "dp", axis=0, tiled=True)
    else:
        whole = lax.all_gather(w_out, ("dp", "seq"), axis=0, tiled=True)
        out_weight = lax.dynamic_slice_in_dim(whole, lax.axis_index("seq") * inner, inner, 0)
    unit_weight = lax.all_gather(units, "dp", axis=0, tiled=True)
    down_weight = lax.all_gather(w_down, "dp", axis=0, tiled=True)

    own_tokens = tokens.reshape(count, width)
    own_cotangent = cotangent.reshape(count, width)
    inputs = own_tokens.astype(f32)
    own_normed = (inputs * rms_scale(inputs) * gain_one).astype(bf16)
    normed_one, cot = [flat(v) for v in gather_plane([own_normed, own_cotangent], shards, 2)]

    cos, sin, starts = rope_tables(doc_ids, shards)
    starts = starts[:, None, :]
    by_row = lambda v: v.reshape(shards, rows, shard_len, v.shape[-1])
    pre = by_row(dot(normed_one, qkv_weight))
    rotated, attended, stats = attend(pre, cos, sin, starts)
    attended = flat(attended)
    hidden, normed_two = forward_plane(
        split(dot(attended, out_weight).astype(bf16)), own_tokens, gain_two, 3
    )
    normed_two = flat(normed_two)

    gate_pre = dot(normed_two, unit_weight[:, :hidden_here])
    up_pre = dot(normed_two, unit_weight[:, hidden_here:])
    sigmoid = jax.nn.sigmoid(gate_pre)
    silu = gate_pre * sigmoid
    activated = (silu * up_pre).astype(bf16)
    out_terms = split(dot(activated, down_weight).astype(bf16))
    grad_act = dot_t(cot, down_weight)
    grad_gate_pre = (grad_act * up_pre * sigmoid * (1.0 + gate_pre * (1.0 - sigmoid))).astype(bf16)
    grad_up_pre = (grad_act * silu).astype(bf16)
    grad_units = jnp.concatenate([grad_gate_pre, grad_up_pre], axis=-1)
    middle_terms = split(dot_t(grad_units, unit_weight).astype(bf16))
    unit_terms = dot(normed_two.T, grad_units).astype(bf16)
    down_terms = dot(activated.T, cot).astype(bf16)
    unit_sums = lax.psum_scatter(unit_terms, "dp", scatter_dimension=0, tiled=True)
    down_sums = lax.psum_scatter(down_terms, "dp", scatter_dimension=0, tiled=True)

    grad_hidden, gain_two_term, branch = middle_plane(
        middle_terms, own_cotangent, hidden, gain_two, 4
    )
    branch = flat(branch)
    out_w_terms = dot(attended.T, branch).astype(bf16)
    if whole_heads:
        grad_out = lax.psum_scatter(out_w_terms, "dp", scatter_dimension=0, tiled=True)
    else:
        placed = lax.dynamic_update_slice_in_dim(
            jnp.zeros((width, width), bf16), out_w_terms, lax.axis_index("seq") * inner, 0
        )
        grad_out = lax.psum_scatter(placed, ("dp", "seq"), scatter_dimension=0, tiled=True)
    grad_attended = by_row(dot_t(branch, out_weight).astype(bf16))
    grad_pre = flat(attend_back(rotated, grad_attended, cos, sin, starts, stats))
    last_terms = split(dot_t(grad_pre, qkv_weight).astype(bf16))
    head_terms = dot(normed_one.T, grad_pre).astype(bf16)
    head_sums = lax.psum_scatter(head_terms, "dp", scatter_dimension=0, tiled=True)

    grad_tokens, gain_one_term, out_tokens = last_plane(
        last_terms, out_terms, own_tokens, hidden, grad_hidden, gain_one, 5
    )
    head_sums, unit_sums = exchange_plane(
        [head_sums.reshape(shards, held, -1), unit_sums.reshape(shards, held, -1)], shards, 6
    )

    head_sums = head_sums.reshape(shards, held, pairs, 3, PAIR)

    def heads_back(i):
        blocks = head_sums[:, :, :, i, :].reshape(shards, held, outer, inner)
        return jnp.moveaxis(blocks, 0, 2).reshape(held, width).astype(f32)

    def units_back(i):
        blocks = unit_sums[:, :, i * hidden_here : (i + 1) * hidden_here]
        blocks = blocks.reshape(shards, held, groups, hidden_held)
        return jnp.moveaxis(blocks, 0, 2).reshape(held, -1).astype(f32)

    gain_sums = lax.psum_scatter(
        jnp.concatenate([gain_one_term, gain_two_term]),
        ("dp", "seq"),
        scatter_dimension=1,
        tiled=True,
    )
    return (
        out_tokens.reshape(tokens.shape),
        grad_tokens.reshape(tokens.shape),
        gain_sums[0],
        heads_back(0),
        heads_back(1),
        heads_back(2),
        grad_out.astype(f32),
        gain_sums[1],
        units_back(0),
        units_back(1),
        down_sums.astype(f32),
    )


def solution(mesh):
    both = ("dp", "seq")
    return jax.shard_map(
        functools.partial(layer, mesh.shape["dp"], mesh.shape["seq"]),
        mesh=mesh,
        in_specs=(
            P("dp", "seq", None),
            P("dp", None),
            P("dp", "seq", None),
            P(both),
            P(both, None),
            P(both, None),
            P(both, None),
            P(both, None),
            P(both),
            P(both, None),
            P(both, None),
            P(both, None),
        ),
        out_specs=(
            P("dp", "seq", None),
            P("dp", "seq", None),
            P(both),
            P(both, None),
            P(both, None),
            P(both, None),
            P(both, None),
            P(both),
            P(both, None),
            P(both, None),
            P(both, None),
        ),
        check_vma=False,
    )
```

time: 4340 us -> 1200 us (0.28)
  waiting for transfers between devices: 3610 us -> 437 us
  Pallas kernels: 0 us -> 441 us
  matrix products: 423 us -> 180 us
  local copies, waits for them, and re-layouts: 141 us -> 53.7 us
  blocking collectives: 85.7 us -> 41.1 us
    reduce_scatter x9 -> x4, waiting for transfers between devices: 2810 us -> 307 us  [the longest x1 147 us: layer(): lax.psum_scatter(unit_terms, 'dp', scatter_dimension=0, tiled=True)]
    all_gather x9 -> x4, waiting for transfers between devices: 798 us -> 51.6 us  [the longest x1 51.6 us: layer(): unit_weight = lax.all_gather(units, 'dp', axis=0, tiled=True)]
    pallas_call x0 -> x8, Pallas kernels: none -> 441 us  [the longest x1 84.1 us: last_plane(): pl.pallas_call(last_kernel, out_shape=[jax.ShapeDtypeStruct((rows, width)...]
    dot_general x39 -> x13, matrix products: 423 us -> 180 us  [the longest x9 126 us: dot(): return jnp.dot(a, b, preferred_element_type=f32)]
    unnamed x2 -> x0, blocking collectives: 85.7 us -> none
    unnamed x18 -> x10, waiting for transfers between devices: 5.49 us -> 78 us
    dynamic_slice x27 -> x0, local copies, waits for them, and re-layouts: 45 us -> none  [the longest x10 40.3 us: key_slice(): piece = lax.dynamic_slice_in_dim(source, block_start, block_size, 1)]
  transfers between devices with their start and end apart: 18 -> 9, of which waited for: 18 -> 6; matrix products, arithmetic and copies ran while one was open for 8% -> 9% of each run, Pallas kernels for 0% -> 15%
where the time goes in v1:
time: 1200 us
  Pallas kernels  441 us (37%)
  waiting for transfers between devices  437 us (36%)
  matrix products  180 us (15%)
  local copies, waits for them, and re-layouts  53.7 us (4%)
  blocking collectives  41.1 us (3%)
  other arithmetic  26.7 us (2%)
  between operations  14.7 us (1%)
    reduce_scatter x1, waiting for transfers between devices, layer(): lax.psum_scatter(unit_terms, 'dp', scatter_dimension=0, tiled=True)  147 us
    dot_general x9, matrix products, dot(): return jnp.dot(a, b, preferred_element_type=f32)  126 us
    pallas_call x1, Pallas kernels, last_plane(): pl.pallas_call(last_kernel, out_shape=[jax.ShapeDtypeStruct((rows, width)...  84.1 us
    pallas_call x1, Pallas kernels, middle_plane(): pl.pallas_call(middle_kernel, out_shape=[jax.ShapeDtypeStruct((rows, widt...  81.3 us
    pallas_call x1, Pallas kernels, forward_plane(): pl.pallas_call(forward_kernel, out_shape=[jax.ShapeDtypeStruct((rows, wid...  80.4 us
    unnamed x10, waiting for transfers between devices  78 us
    pallas_call x1, Pallas kernels, gather_plane(): pl.pallas_call(functools.partial(gather_kernel, count), out_shape=[jax.Sh...  77.4 us
    reduce_scatter x1, waiting for transfers between devices, layer(): lax.psum_scatter(down_terms, 'dp', scatter_dimension=0, tiled=True)  76 us
  transfers between devices with their start and end apart: 9, of which 6 were waited for; matrix products, arithmetic and copies ran while one was open for 9% of the time, Pallas kernels for 15%

profile of v1, /device:TPU:0, one launch (start us, length us, event | category | flops | bytes accessed | tf_op | source)
XLA Modules:
  0.0 1195.4 jit_solution(1617142204614252863)
XLA Ops:
  24.7 36.9 %shard_map.204 = (bf16[8,64,768]{2,1,0:T(8,128)(2,1)}, bf16[8,64,2048]{2,1,0:T(8,128)(2,1)}) custom-call(bf16[8,64,768]{2,1,0:T(8,128)(2,1)} %reshape.232.refs_0_, bf16[8,64,2048]{2,1,0:T(8,128)(2,1)} %pad_maximum_fusion.3.refs_1_), custom_call_target="tpu_custom_call" | custom-call | tf_op jit(solution)/shard_map/pallas_call | solution.py:168
  64.9 41.1 %all-gather = bf16[32,64,2]{1,2,0:T(2,128)(2,1)S(1)} all-gather(bf16[1,64,2]{1,2,0:T(2,128)(2,1)S(1)} %maximum_bitcast_fusion.2), channel_id=1, replica_groups=mesh['dp'=4,'seq'=8] {'dp','seq'}, dimensions={0}, use_global_device_ids=true | all-gather | bytes 8448 | tf_op jit(solution)/shard_map/all_gather | solution.py:669
  108.3 77.4 %shard_map.203 = (bf16[8,256,2048]{2,1,0:T(8,128)(2,1)}, bf16[8,256,2048]{2,1,0:T(8,128)(2,1)}) custom-call(bf16[256,2048]{1,0:T(8,128)(2,1)} %multiply_convert_fusion.3.refs_0_, bf16[256,2048]{1,0:T(8,128)(2,1)} %bitcast.117), custom_call_target="tpu_custom_call" | custom-call | tf_op jit(solution)/shard_map/pallas_call | solution.py:131
  192.1 12.0 %fusion.5.pre = f32[8,2,128,768]{3,2,1,0:T(8,128)} fusion(bf16[8,2,128,2048]{3,2,1,0:T(8,128)(2,1)} %bitcast.164, bf16[2048,768]{1,0:T(8,128)(2,1)} %all-gather.6.cloned.1.call-done), kind=kOutput, calls=%fused_computation.17 | convolution fusion | flops 6442450944 | bytes 17825792 | tf_op jit(solution)/shard_map/dot_general | solution.py:473
  204.1 22.6 %shard_map.205 = (bf16[8,2,128,768]{3,2,1,0:T(8,128)(2,1)}, bf16[8,2,128,256]{3,2,1,0:T(8,128)(2,1)S(1)}, f32[2,2,2,1024]{3,2,1,0:T(2,128)S(1)}) custom-call(f32[8,2,128,768]{3,2,1,0:T(8,128)} %fusion.5.pre, f32[8,2,128,128]{3,2,1,0:T(8,128)S(1)} %get-tuple-element.62.cos, f32[8,2,128,128]{3,2,1,0:T(8,128)S(1)} %copy-done.5, s32[2,1,1024]{2,1,0:T(1,128)S(1)} %bitcast.122), custom_call_target="tpu_custom_call" | custom-call | flops 4294967296 | bytes 12582912 | tf_op jit(solution)/shard_map/pallas_call | solution.py:531
  233.5 80.4 %shard_map.206 = (f32[256,2048]{1,0:T(8,128)S(1)}, bf16[8,256,2048]{2,1,0:T(8,128)(2,1)S(1)}) custom-call(bf16[8,256,2048]{2,1,0:T(8,128)(2,1)} %bitcast.128, bf16[256,2048]{1,0:T(8,128)(2,1)S(1)} %bitcast.113, f32[1,2048]{1,0:T(1,128)S(1)} %get-tuple-element.57.gain), custom_call_target="tpu_custom_call" | custom-call | tf_op jit(solution)/shard_map/pallas_call | solution.py:303
  318.6 15.1 %fusion.16 = f32[2048,1024]{0,1:T(8,128)} fusion(bf16[2048,2048]{1,0:T(8,128)(2,1)} %bitcast.166, bf16[1024,2048]{1,0:T(8,128)(2,1)} %all-gather.8.cloned.1.call-done), kind=kOutput, calls=%fused_computation.59 | convolution fusion | flops 8589934592 | bytes 20971520 | tf_op jit(solution)/shard_map/dot_general | solution.py:469
  333.7 51.6 %all-gather.12.cloned.1.call-done = bf16[2048,2048]{1,0:T(8,128)(2,1)} async-done(((bf16[512,2048]{1,0:T(8,128)(2,1)}), bf16[2048,2048]{1,0:T(8,128)(2,1)}) %all-gather.12.cloned.1.call-update) | async-done | bytes 8388624 | tf_op jit(solution)/shard_map/all_gather | solution.py:695
  385.3 14.7 %fusion.1 = f32[2048,1024]{0,1:T(8,128)} fusion(bf16[2048,2048]{1,0:T(8,128)(2,1)} %bitcast.124, bf16[2048,2048]{1,0:T(8,128)(2,1)} %all-gather.12.cloned.1.call-done), kind=kOutput, calls=%fused_computation.11 | convolution fusion | flops 8589934592 | bytes 20971520 | tf_op jit(solution)/shard_map/dot_general | solution.py:473
  399.9 22.6 %multiply_convert_fusion = (bf16[2048,1024]{0,1:T(8,128)(2,1)}, bf16[2048,1024]{0,1:T(8,128)(2,1)}, bf16[2048,1024]{0,1:T(8,128)(2,1)}) fusion(f32[2048,1024]{0,1:T(8,128)} %fusion.1, f32[2048,1024]{0,1:T(8,128)} %fusion.16, bf16[2048,2048]{1,0:T(8,128)(2,1)} %bitcast.125, bf16[2048,2048]{1,0:T(8,128)(2,1)} %all-gather.12.cloned.1.call-done), kind=kOutput, calls=%fused_computation.1 | convolution fusion | flops 8621391872 | bytes 41943040 | tf_op jit(solution)/shard_map/dot_general | solution.py:473
  422.5 23.8 %convolution_convert_fusion.3 = bf16[2048,2048]{1,0:T(8,128)(2,1)} fusion(bf16[2048,2048]{1,0:T(8,128)(2,1)} %all-gather.12.cloned.1.call-done, bf16[2048,1024]{0,1:T(8,128)(2,1)} %get-tuple-element.52, bf16[2048,1024]{0,1:T(8,128)(2,1)} %get-tuple-element.51), kind=kOutput, calls=%fused_computation.9 | convolution fusion | flops 17200840704 | bytes 25165824 | tf_op jit(solution)/shard_map/dot_general | solution.py:469
  446.3 81.3 %shard_map.207 = (f32[256,2048]{1,0:T(8,128)S(1)}, f32[1,2048]{1,0:T(1,128)S(1)}, bf16[8,256,2048]{2,1,0:T(8,128)(2,1)}) custom-call(bf16[8,256,2048]{2,1,0:T(8,128)(2,1)} %bitcast.133, bf16[256,2048]{1,0:T(8,128)(2,1)S(1)} %bitcast.118, f32[256,2048]{1,0:T(8,128)S(1)} %copy-done.2, f32[1,2048]{1,0:T(1,128)S(1)} %get-tuple-element.57.gain), custom_call_target="tpu_custom_call" | custom-call | tf_op jit(solution)/shard_map/pallas_call | solution.py:379
  534.2 23.5 %shard_map.208 = bf16[8,2,128,768]{3,2,1,0:T(8,128)(2,1)} custom-call(bf16[8,2,128,768]{3,2,1,0:T(8,128)(2,1)} %get-tuple-element.30.rotated, bf16[8,2,128,256]{3,2,1,0:T(8,128)(2,1)S(1)} %bitcast.127, f32[8,2,128,128]{3,2,1,0:T(8,128)S(1)} %get-tuple-element.62.cos, f32[8,2,128,128]{3,2,1,0:T(8,128)S(1)} %copy-done.6, s32[2,1,1024]{2,1,0:T(1,128)S(1)} %bitcast.123, ...), custom_call_target="tpu_custom_call" | custom-call | flops 10737418240 | bytes 9437184 | tf_op jit(solution)/shard_map/pallas_call | solution.py:604
  557.8 14.0 %convolution_convert_fusion.1 = bf16[2048,2048]{1,0:T(8,128)(2,1)} fusion(bf16[2048,1024]{0,1:T(8,128)(2,1)} %get-tuple-element.50, bf16[1024,2048]{1,0:T(8,128)(2,1)S(1)} %copy-done.15), kind=kOutput, calls=%fused_computation.7 | convolution fusion | flops 8594128896 | bytes 16777216 | tf_op jit(solution)/shard_map/dot_general | solution.py:473
  580.9 84.1 %shard_map.209 = (bf16[256,2048]{1,0:T(8,128)(2,1)S(1)}, f32[1,2048]{1,0:T(1,128)S(1)}, bf16[256,2048]{1,0:T(8,128)(2,1)S(1)}) custom-call(bf16[8,256,2048]{2,1,0:T(8,128)(2,1)} %bitcast.132, bf16[8,256,2048]{2,1,0:T(8,128)(2,1)} %bitcast.131, bf16[256,2048]{1,0:T(8,128)(2,1)S(1)} %bitcast.114, f32[256,2048]{1,0:T(8,128)S(1)} %copy-done.2, ...), custom_call_target="tpu_custom_call" | custom-call | tf_op jit(solution)/shard_map/pallas_call | solution.py:447
  674.1 14.0 %convolution_convert_fusion.5 = bf16[1024,2048]{1,0:T(8,128)(2,1)} fusion(bf16[2048,1024]{0,1:T(8,128)(2,1)} %get-tuple-element.50, bf16[2048,2048]{1,0:T(8,128)(2,1)} %bitcast.167), kind=kOutput, calls=%fused_computation.15 | convolution fusion | flops 8592031744 | bytes 16777216 | tf_op jit(solution)/shard_map/dot_general | solution.py:473
  688.2 11.4 convolution_convert_fusion.6
  699.6 23.8 %convolution_convert_fusion = bf16[2048,2048]{1,0:T(8,128)(2,1)} fusion(bf16[2048,2048]{1,0:T(8,128)(2,1)} %bitcast.126, bf16[2048,1024]{0,1:T(8,128)(2,1)} %get-tuple-element.52, bf16[2048,1024]{0,1:T(8,128)(2,1)} %get-tuple-element.51), kind=kOutput, calls=%fused_computation.6 | convolution fusion | flops 17200840704 | bytes 25165824 | tf_op jit(solution)/shard_map/dot_general | solution.py:473
  723.5 76.0 %reduce-scatter.16.cloned.1.call-done = f32[64,2]{1,0:T(8,128)} async-done(((f32[2048,2]{1,0:T(8,128)}), f32[64,2]{1,0:T(8,128)}) %reduce-scatter.16.cloned.1.call-update) | async-done | bytes 528
  801.6 23.9 %reduce-scatter.12.cloned.1.call-done = bf16[64,2048]{1,0:T(8,128)(2,1)} async-done(((bf16[256,2048]{1,0:T(8,128)(2,1)}), bf16[64,2048]{1,0:T(8,128)(2,1)}) %reduce-scatter.12.cloned.1.call-update) | async-done | bytes 262160 | tf_op jit(solution)/shard_map/reduce_scatter | solution.py:737
  827.2 76.0 %reduce-scatter.14.cloned.1.call-done = bf16[256,2048]{1,0:T(8,128)(2,1)} async-done(((bf16[1024,2048]{1,0:T(8,128)(2,1)}), bf16[256,2048]{1,0:T(8,128)(2,1)}) %reduce-scatter.14.cloned.1.call-update) | async-done | bytes 1048592 | tf_op jit(solution)/shard_map/reduce_scatter | solution.py:729
  905.9 60.4 %reduce-scatter.8.cloned.1.call-done = bf16[512,768]{1,0:T(8,128)(2,1)} async-done(((bf16[2048,768]{1,0:T(8,128)(2,1)}), bf16[512,768]{1,0:T(8,128)(2,1)}) %reduce-scatter.8.cloned.1.call-update) | async-done | bytes 786448 | tf_op jit(solution)/shard_map/reduce_scatter | solution.py:747
  966.3 147.0 %reduce-scatter.10.cloned.1.call-done = bf16[512,2048]{1,0:T(8,128)(2,1)} async-done(((bf16[2048,2048]{1,0:T(8,128)(2,1)}), bf16[512,2048]{1,0:T(8,128)(2,1)}) %reduce-scatter.10.cloned.1.call-update) | async-done | bytes 2097168 | tf_op jit(solution)/shard_map/reduce_scatter | solution.py:728
  1113.4 35.3 %shard_map.210 = (bf16[8,64,768]{2,1,0:T(8,128)(2,1)}, bf16[8,64,2048]{2,1,0:T(8,128)(2,1)}) custom-call(bf16[8,64,768]{2,1,0:T(8,128)(2,1)} %bitcast.156, bf16[8,64,2048]{2,1,0:T(8,128)(2,1)} %bitcast.147), custom_call_target="tpu_custom_call" | custom-call | tf_op jit(solution)/shard_map/pallas_call | solution.py:168
  (130 shorter events, 112.0 us)
Async XLA Ops:
  7.2 9.8 copy-start.12
  7.2 184.9 %all-gather.6.cloned.1.call-start = ((), (), s32[]{:S(2)}) async-start(), calls=%async_computation.5 | async-start | bytes 3932160 | tf_op jit(solution)/shard_map/all_gather | solution.py:689
  18.4 45.3 %copy-start.14 = (s32[2,1024]{1,0:T(2,128)S(1)}, s32[2,1024]{1,0:T(2,128)}, u32[]{:S(2)}) copy-start(s32[2,1024]{1,0:T(2,128)} %param.13) | copy-start | bytes 24580
  18.4 46.5 %copy-start.17 = (bf16[64]{0:T(256)(128)(2,1)S(1)}, bf16[64]{0:T(256)(128)(2,1)}, u32[]{:S(2)}) copy-start(bf16[64]{0:T(256)(128)(2,1)} %param.20) | copy-start | bytes 388
  18.4 46.5 %copy-start.18 = (bf16[64]{0:T(256)(128)(2,1)S(1)}, bf16[64]{0:T(256)(128)(2,1)}, u32[]{:S(2)}) copy-start(bf16[64]{0:T(256)(128)(2,1)} %param.15) | copy-start | bytes 388
  20.0 86.2 %copy-start = (bf16[2,128,2048]{2,1,0:T(8,128)(2,1)S(1)}, bf16[2,128,2048]{2,1,0:T(8,128)(2,1)}, u32[]{:S(2)}) copy-start(bf16[2,128,2048]{2,1,0:T(8,128)(2,1)} %param.12) | copy-start | bytes 3145732
  61.6 165.1 %all-gather.10.cloned.1.call-start = ((), (), s32[]{:S(2)}) async-start(), calls=%async_computation.7 | async-start | bytes 1310720 | tf_op jit(solution)/shard_map/all_gather | solution.py:691
  62.3 256.2 %all-gather.8.cloned.1.call-start = ((), (), s32[]{:S(2)}) async-start(), calls=%async_computation.6 | async-start | bytes 5242880 | tf_op jit(solution)/shard_map/all_gather | solution.py:696
  63.1 322.2 %all-gather.12.cloned.1.call-start = ((), (), s32[]{:S(2)}) async-start(), calls=%async_computation.8 | async-start | bytes 10485760 | tf_op jit(solution)/shard_map/all_gather | solution.py:695
  63.7 735.8 %reduce-scatter.16.cloned.1.call-start = ((), (), s32[]{:S(2)}) async-start(), calls=%async_computation.13 | async-start | bytes 1081344
  192.1 12.0 %copy-start.5 = (f32[8,2,128,128]{3,2,1,0:T(8,128)S(1)}, f32[8,2,128,128]{3,2,1,0:T(8,128)}, u32[]{:S(2)}) copy-start(f32[8,2,128,128]{3,2,1,0:T(8,128)} %get-tuple-element.63.sin) | copy-start | bytes 3145732
  422.5 23.8 %copy-start.2 = (f32[256,2048]{1,0:T(8,128)S(1)}, f32[256,2048]{1,0:T(8,128)}, u32[]{:S(2)}) copy-start(f32[256,2048]{1,0:T(8,128)} %copy-done.1) | copy-start | bytes 6291460
  422.5 23.8 %copy-start.3 = (bf16[2,128,2048]{2,1,0:T(8,128)(2,1)S(1)}, bf16[2,128,2048]{2,1,0:T(8,128)(2,1)}, u32[]{:S(2)}) copy-start(bf16[2,128,2048]{2,1,0:T(8,128)(2,1)} %param.14) | copy-start | bytes 3145732
  446.3 81.3 %copy-start.13 = (bf16[256,2048]{1,0:T(8,128)(2,1)S(1)}, bf16[256,2048]{1,0:T(8,128)(2,1)}, u32[]{:S(2)}) copy-start(bf16[256,2048]{1,0:T(8,128)(2,1)} %all-gather.10.cloned.1.call-done) | copy-start | bytes 3145732
  527.6 6.6 copy-start.4
  534.2 23.5 %copy-start.15 = (bf16[1024,2048]{1,0:T(8,128)(2,1)S(1)}, bf16[1024,2048]{1,0:T(8,128)(2,1)}, u32[]{:S(2)}) copy-start(bf16[1024,2048]{1,0:T(8,128)(2,1)} %all-gather.8.cloned.1.call-done) | copy-start | bytes 12582916
  557.8 14.0 %copy-start.16 = (bf16[2048,768]{1,0:T(8,128)(2,1)S(1)}, bf16[2048,768]{1,0:T(8,128)(2,1)}, u32[]{:S(2)}) copy-start(bf16[2048,768]{1,0:T(8,128)(2,1)} %all-gather.6.cloned.1.call-done) | copy-start | bytes 9437188
  557.8 14.0 %copy-start.19 = (bf16[8,2,128,768]{3,2,1,0:T(8,128)(2,1)S(1)}, bf16[8,2,128,768]{3,2,1,0:T(8,128)(2,1)}, u32[]{:S(2)}) copy-start(bf16[8,2,128,768]{3,2,1,0:T(8,128)(2,1)} %shard_map.208) | copy-start | bytes 9437188
  571.8 9.1 copy-start.10
  667.3 158.1 %reduce-scatter.12.cloned.1.call-start = ((), (), s32[]{:S(2)}) async-start(), calls=%async_computation.11 | async-start | bytes 1310720 | tf_op jit(solution)/shard_map/reduce_scatter | solution.py:737
  674.1 229.1 %reduce-scatter.14.cloned.1.call-start = ((), (), s32[]{:S(2)}) async-start(), calls=%async_computation.12 | async-start | bytes 5242880 | tf_op jit(solution)/shard_map/reduce_scatter | solution.py:729
  688.2 278.2 %reduce-scatter.8.cloned.1.call-start = ((), (), s32[]{:S(2)}) async-start(), calls=%async_computation.9 | async-start | bytes 3932160 | tf_op jit(solution)/shard_map/reduce_scatter | solution.py:747
  699.6 413.8 %reduce-scatter.10.cloned.1.call-start = ((), (), s32[]{:S(2)}) async-start(), calls=%async_computation.10 | async-start | bytes 10485760 | tf_op jit(solution)/shard_map/reduce_scatter | solution.py:728
  1175.5 11.0 copy-start.8
  (5 other events, 12.7 us)
Sparse Core Ops, SparseCore 0:
  61.7 63.8 all-gather.5
  127.1 26.6 all-gather.9
  155.4 80.2 all-gather.7
  237.1 148.1 all-gather.11
  667.4 132.0 reduce-scatter.15
  802.3 23.0 reduce-scatter.11
  827.7 75.4 reduce-scatter.13
  905.6 60.7 reduce-scatter.7
  968.8 144.4 reduce-scatter.9

commit v2 on v1

--- a/solution.py
+++ b/solution.py
@@ -21,6 +21,10 @@
 VMEM = pl.BlockSpec(memory_space=pltpu.VMEM)
 DMA = pltpu.SemaphoreType.DMA
 MIB = 1 << 20
+
+
+def lasting(us):
+    return pl.CostEstimate(flops=0, transcendentals=0, bytes_accessed=int(us * 3_500_000))
 
 
 def plane():
@@ -135,6 +139,7 @@
         out_specs=[ANY] * count,
         scratch_shapes=[DMA((GATHER_SEMS * count,)), DMA((GATHER_SEMS * count,)), DMA((count,))],
         compiler_params=pltpu.CompilerParams(collective_id=collective_id, has_side_effects=True),
+        cost_estimate=lasting(40 * count),
     )(*arrays)
 
 
@@ -172,6 +177,7 @@
         out_specs=[ANY] * count,
         scratch_shapes=[DMA((7 * count,)), DMA((7 * count,)), DMA((count,))],
         compiler_params=pltpu.CompilerParams(collective_id=collective_id, has_side_effects=True),
+        cost_estimate=lasting(35),
     )(*arrays)
 
 
@@ -196,21 +202,34 @@
     ]
 
 
-def scatter_plane(p, terms, kept, paired, far, final, send, recv, local):
-    rows = terms.shape[1]
+class FromMemory:
+    def __init__(self, p, terms, kept, paired, send, recv, local):
+        self.loads, self.pairs = {}, {}
+        for i, own, other in ORDER:
+            self.loads[i] = pltpu.make_async_copy(terms.at[p[own]], kept.at[i], local.at[i])
+            self.loads[i].start()
+            self.pairs[i] = remote(p, terms.at[p[other]], paired.at[i], send, recv, i, "sib")
+            self.pairs[i].start()
+
+    def ready(self, i):
+        self.loads[i].wait()
+        self.pairs[i].wait_recv()
+
+    def finish(self):
+        for copy in self.pairs.values():
+            copy.wait_send()
+
+
+ORDER = ((3, "dg", "ds"), (1, "xp", "xs"), (2, "yp", "ys"), (0, "me", "sib"))
+
+
+def scatter_plane(p, source, rows, kept, paired, far, final, send, recv, meanwhile=None):
     half = rows // 2
     low, high = pl.ds(0, half), pl.ds(half, half)
-    order = ((3, "dg", "ds"), (1, "xp", "xs"), (2, "yp", "ys"), (0, "me", "sib"))
-    loads, pairs, sends = {}, {}, []
-    for i, own, other in order:
-        loads[i] = pltpu.make_async_copy(terms.at[p[own]], kept.at[i], local.at[i])
-        loads[i].start()
-        pairs[i] = remote(p, terms.at[p[other]], paired.at[i], send, recv, i, "sib")
-        pairs[i].start()
+    sends = []
 
     def add_pair(i):
-        loads[i].wait()
-        pairs[i].wait_recv()
+        source.ready(i)
 
         def step(at):
             kept[i, at, :] = (kept[i, at, :].astype(f32) + paired[i, at, :].astype(f32)).astype(
@@ -247,11 +266,12 @@
 
     over_rows(half, step_y)
     near.append(put(kept.at[1, high], final.at[0, high], 9, "xp"))
-    loads[0].wait()
-    pairs[0].wait_recv()
+    source.ready(0)
+    if meanwhile is not None:
+        meanwhile()
     for copy in near:
         copy.wait_recv()
-    return sends + list(pairs.values())
+    return sends
 
 
 def total(kept, paired, final, at):
@@ -265,7 +285,8 @@
 ):
     p = plane()
     greet(p, ("sib", "xp", "yp"))
-    sends = scatter_plane(p, terms, kept, paired, far, final, send, recv, local)
+    source = FromMemory(p, terms, kept, paired, send, recv, local)
+    sends = scatter_plane(p, source, tokens.shape[0], kept, paired, far, final, send, recv)
 
     def step(at):
         h = tokens[at, :].astype(f32) + total(kept, paired, final, at)
@@ -279,6 +300,7 @@
     own.start()
     gather_finish(p, sent, mine, normed, gsend, grecv, 0)
     own.wait()
+    source.finish()
     for copy in sends:
         copy.wait_send()
 
@@ -313,52 +335,8 @@
         compiler_params=pltpu.CompilerParams(
             collective_id=collective_id, has_side_effects=True, vmem_limit_bytes=40 * MIB
         ),
+        cost_estimate=lasting(80),
     )(terms, tokens, gain)
-
-
-def middle_kernel(
-    terms,
-    cotangent,
-    hidden,
-    gain,
-    grad_hidden,
-    gain_term,
-    branch,
-    kept,
-    paired,
-    far,
-    final,
-    send,
-    recv,
-    local,
-    mine,
-    gsend,
-    grecv,
-):
-    p = plane()
-    greet(p, ("sib", "xp", "yp"))
-    sends = scatter_plane(p, terms, kept, paired, far, final, send, recv, local)
-    gain_term[...] = jnp.zeros_like(gain_term)
-
-    def step(at):
-        g = total(kept, paired, final, at)
-        h = hidden[at, :]
-        scale = lax.rsqrt(jnp.mean(h * h, axis=-1, keepdims=True) + norm_eps)
-        weighted = g * gain[...]
-        inner = jnp.mean(weighted * h, axis=-1, keepdims=True)
-        out = cotangent[at, :].astype(f32) + scale * weighted - h * (scale * scale * scale * inner)
-        grad_hidden[at, :] = out
-        mine[at, :] = out.astype(bf16)
-        gain_term[...] += jnp.sum(g * h * scale, axis=0, keepdims=True)
-
-    over_rows(hidden.shape[0], step)
-    sent = gather_start(p, mine, branch, gsend, grecv, 0)
-    own = pltpu.make_async_copy(mine, branch.at[p["me"]], local.at[0])
-    own.start()
-    gather_finish(p, sent, mine, branch, gsend, grecv, 0)
-    own.wait()
-    for copy in sends:
-        copy.wait_send()
 
 
 def norm_back(values, scale, gain, grad):
@@ -368,96 +346,6 @@
         scale * weighted - values * (scale * scale * scale) * inner,
         jnp.sum(grad * values * scale, axis=0, keepdims=True),
     )
-
-
-def middle_plane(terms, cotangent, hidden, gain, collective_id):
-    shards, rows, width = terms.shape
-    if shards != 8:
-        back, gain_term = norm_back(hidden, rms_scale(hidden), gain, reduce_plane(terms))
-        grad_hidden = cotangent.astype(f32) + back
-        return grad_hidden, gain_term, lax.all_gather(grad_hidden.astype(bf16), "seq")
-    return pl.pallas_call(
-        middle_kernel,
-        out_shape=[
-            jax.ShapeDtypeStruct((rows, width), f32),
-            jax.ShapeDtypeStruct((1, width), f32),
-            jax.ShapeDtypeStruct((8, rows, width), bf16),
-        ],
-        in_specs=[ANY, VMEM, VMEM, VMEM],
-        out_specs=[VMEM, VMEM, ANY],
-        scratch_shapes=scatter_scratch(rows, width)
-        + [pltpu.VMEM((rows, width), bf16), DMA((GATHER_SEMS,)), DMA((GATHER_SEMS,))],
-        compiler_params=pltpu.CompilerParams(
-            collective_id=collective_id, has_side_effects=True, vmem_limit_bytes=44 * MIB
-        ),
-    )(terms, cotangent, hidden, gain)
-
-
-def last_kernel(
-    terms,
-    out_terms,
-    tokens,
-    hidden,
-    grad_hidden,
-    gain,
-    grad_tokens,
-    gain_term,
-    out_tokens,
-    *scratch,
-):
-    p = plane()
-    greet(p, ("sib", "xp", "yp"))
-    kept, paired, far, final, send, recv, local = scratch[:7]
-    sends = scatter_plane(p, terms, kept, paired, far, final, send, recv, local)
-    gain_term[...] = jnp.zeros_like(gain_term)
-
-    def step(at):
-        g = total(kept, paired, final, at)
-        t = tokens[at, :].astype(f32)
-        scale = lax.rsqrt(jnp.mean(t * t, axis=-1, keepdims=True) + norm_eps)
-        weighted = g * gain[...]
-        inner = jnp.mean(weighted * t, axis=-1, keepdims=True)
-        grad_tokens[at, :] = (
-            grad_hidden[at, :] + scale * weighted - t * (scale * scale * scale * inner)
-        ).astype(bf16)
-        gain_term[...] += jnp.sum(g * t * scale, axis=0, keepdims=True)
-
-    over_rows(tokens.shape[0], step)
-    kept, paired, far, final, send, recv, local = scratch[7:]
-    sends += scatter_plane(p, out_terms, kept, paired, far, final, send, recv, local)
-
-    def step_out(at):
-        out_tokens[at, :] = (hidden[at, :] + total(kept, paired, final, at)).astype(bf16)
-
-    over_rows(tokens.shape[0], step_out)
-    for copy in sends:
-        copy.wait_send()
-
-
-def last_plane(terms, out_terms, tokens, hidden, grad_hidden, gain, collective_id):
-    shards, rows, width = terms.shape
-    if shards != 8:
-        values = tokens.astype(f32)
-        back, gain_term = norm_back(values, rms_scale(values), gain, reduce_plane(terms))
-        return (
-            (grad_hidden + back).astype(bf16),
-            gain_term,
-            (hidden + reduce_plane(out_terms)).astype(bf16),
-        )
-    return pl.pallas_call(
-        last_kernel,
-        out_shape=[
-            jax.ShapeDtypeStruct((rows, width), bf16),
-            jax.ShapeDtypeStruct((1, width), f32),
-            jax.ShapeDtypeStruct((rows, width), bf16),
-        ],
-        in_specs=[ANY, ANY, VMEM, VMEM, VMEM, VMEM],
-        out_specs=[VMEM, VMEM, VMEM],
-        scratch_shapes=scatter_scratch(rows, width) * 2,
-        compiler_params=pltpu.CompilerParams(
-            collective_id=collective_id, has_side_effects=True, vmem_limit_bytes=48 * MIB
-        ),
-    )(terms, out_terms, tokens, hidden, grad_hidden, gain)
 
 
 def swap_halves(v, first):
@@ -639,6 +527,806 @@
     return lay([cos] * 4), lay([-sin, sin, -sin, sin]), starts
 
 
+class LineSum:
+    def __init__(self, p, view, land, send, recv, base):
+        self.p, self.view, self.land = p, view, land
+        self.send, self.recv, self.base = send, recv, base
+        self.z = p["dp"]
+        self.inward = 1 - 2 * lax.div(self.z, 2)
+        self.end = (self.z == 0) | (self.z == 3)
+
+    def copy(self, src, slot, i, to):
+        return pltpu.make_async_remote_copy(
+            src_ref=src,
+            dst_ref=self.land.at[slot],
+            send_sem=self.send.at[self.base + i],
+            recv_sem=self.recv.at[self.base + slot],
+            device_id=(to, self.p["me"]),
+            device_id_type=MESH,
+        )
+
+    def arrived(self, slot):
+        self.copy(self.land.at[slot], slot, 0, self.z).wait_recv()
+
+    def first(self):
+        self.first_far()
+        self.first_rest()
+
+    def first_far(self):
+        z, inward = self.z, self.inward
+
+        @pl.when(self.end)
+        def _():
+            near, far = z + inward, z + 3 * inward
+            self.copy(self.view(far), near, 0, near).start()
+
+    def first_rest(self):
+        z, inward = self.z, self.inward
+
+        @pl.when(self.end)
+        def _():
+            near, mid = z + inward, z + 2 * inward
+            self.copy(self.view(mid), z, 1, mid).start()
+            self.copy(self.view(near), z, 2, near).start()
+
+        @pl.when(jnp.logical_not(self.end))
+        def _():
+            inner, outer = z + inward, z - inward
+            self.copy(self.view(inner), z, 0, inner).start()
+            self.copy(self.view(outer), z, 1, outer).start()
+
+    def second(self, acc, extra, local, i):
+        @pl.when(jnp.logical_not(self.end))
+        def _():
+            far = self.z + 2 * self.inward
+            own = pltpu.make_async_copy(self.view(far), acc, local.at[i])
+            own.start()
+            self.arrived(self.z)
+            other = pltpu.make_async_copy(self.land.at[self.z], extra, local.at[i + 1])
+            other.start()
+            own.wait()
+            other.wait()
+
+            def step(at):
+                acc[at, :] = (acc[at, :].astype(f32) + extra[at, :].astype(f32)).astype(bf16)
+
+            over_rows(acc.shape[0], step)
+            self.copy(acc, self.z, 2, far).start()
+
+    def total(self, parts, local, i):
+        z, inward = self.z, self.inward
+        self.arrived(z + inward)
+        self.arrived(z + 2 * inward)
+        loads = [
+            pltpu.make_async_copy(src, parts.at[k], local.at[i + k])
+            for k, src in enumerate(
+                (self.view(z), self.land.at[z + inward], self.land.at[z + 2 * inward])
+            )
+        ]
+        for load in loads:
+            load.start()
+        for load in loads:
+            load.wait()
+        rows = parts.shape[1]
+        three = lambda at: (parts[0, at, :].astype(f32) + parts[1, at, :].astype(f32)) + parts[
+            2, at, :
+        ].astype(f32)
+
+        @pl.when(self.end)
+        def _():
+            def step(at):
+                parts[0, at, :] = three(at).astype(bf16)
+
+            over_rows(rows, step)
+
+        @pl.when(jnp.logical_not(self.end))
+        def _():
+            self.arrived(z - inward)
+            load = pltpu.make_async_copy(self.land.at[z - inward], parts.at[3], local.at[i + 3])
+            load.start()
+            load.wait()
+
+            def step(at):
+                parts[0, at, :] = (three(at) + parts[3, at, :].astype(f32)).astype(bf16)
+
+            over_rows(rows, step)
+
+    def finish(self):
+        for i in range(3):
+            self.copy(self.land.at[0], 0, i, self.z).wait_send()
+
+
+CHUNKS = 4
+EARLY = 3
+
+
+class Local:
+    def __init__(self, sems):
+        self.sems, self.used = sems, 0
+
+    def take(self, count=1):
+        self.used += count
+        return self.used - count
+
+
+def feed_kernel(
+    normed,
+    cot,
+    units,
+    down,
+    own_cot,
+    hidden,
+    gain,
+    grad_hidden,
+    gain_term,
+    branch,
+    out_terms,
+    unit_sums,
+    down_sums,
+    unit_terms,
+    down_terms,
+    kept_units,
+    kept_acts,
+    unit_land,
+    down_land,
+    x,
+    c,
+    w,
+    d,
+    unit_stage,
+    act_stage,
+    unit_t,
+    act_t,
+    unit_grad,
+    down_grad,
+    unit_acc,
+    down_acc,
+    unit_parts,
+    down_parts,
+    turned,
+    kept,
+    paired,
+    far,
+    final,
+    send,
+    recv,
+    gsend,
+    grecv,
+    zsend,
+    zrecv,
+    local,
+):
+    p = plane()
+    barrier = pltpu.get_barrier_semaphore()
+    others = [(p["dp"], p[name]) for name in ("sib", "xp", "yp")]
+    for k in range(1, 4):
+        others.append((lax.rem(p["dp"] + k, 4), p["me"]))
+    for where in others:
+        pl.semaphore_signal(barrier, inc=1, device_id=where, device_id_type=MESH)
+    sems = Local(local)
+    x_sem, c_sem, w_sem, d_sem = sems.take(8), sems.take(8), sems.take(2), sems.take(8)
+    us_sem, as_sem, ug_sem, dg_sem = (sems.take() for _ in range(4))
+    ub_sem, ab_sem, out_sem, last_w, last_d = (
+        sems.take(2),
+        sems.take(2),
+        sems.take(2),
+        sems.take(),
+        sems.take(16),
+    )
+    z_sem, own_sem, turn_sem = sems.take(8), sems.take(), sems.take(2)
+    shards, rows, width = normed.shape
+    chunk = w.shape[3]
+    part = chunk // 2
+    piece = down.shape[2]
+
+    def move(src, dst, i):
+        return pltpu.make_async_copy(src, dst, local.at[i])
+
+    def w_load(j):
+        return move(units.at[:, :, pl.ds(j * chunk, chunk)], w.at[j % 2], w_sem + j % 2)
+
+    def d_load(j):
+        return [
+            move(down.at[k, j], d.at[j % 2, pl.ds(k * piece, piece)], d_sem + 4 * (j % 2) + k)
+            for k in range(4)
+        ]
+
+    def start_chunk(j):
+        w_load(j).start()
+        for load in d_load(j):
+            load.start()
+
+    start_chunk(0)
+    for s in range(shards):
+        move(normed.at[s], x.at[s], x_sem + s).start()
+        move(cot.at[s], c.at[s], c_sem + s).start()
+    pl.semaphore_wait(barrier, len(others))
+
+    line = {}
+    for j in range(EARLY):
+        line[j] = (
+            LineSum(
+                p,
+                lambda owner, j=j: unit_terms.at[
+                    j, :, pl.ds(pl.multiple_of(owner * chunk, chunk), chunk)
+                ],
+                unit_land.at[j],
+                zsend,
+                zrecv,
+                8 * j,
+            ),
+            LineSum(
+                p,
+                lambda owner, j=j: down_terms.at[
+                    j, pl.ds(pl.multiple_of(owner * piece, piece), piece)
+                ],
+                down_land.at[j],
+                zsend,
+                zrecv,
+                8 * j + 4,
+            ),
+        )
+
+    def pass_on(j):
+        line[j][0].second(unit_acc.at[j], unit_parts.at[0], local, z_sem)
+        line[j][1].second(down_acc.at[j], down_parts.at[0], local, z_sem + 2)
+
+    for j in range(CHUNKS):
+        slot = j % 2
+        w_load(j).wait()
+        for load in d_load(j):
+            load.wait()
+        if j + 1 < CHUNKS:
+            start_chunk(j + 1)
+        if j > 0:
+            move(unit_stage, kept_units.at[:, :, pl.ds(0, chunk)], us_sem).wait()
+            move(act_stage, kept_acts.at[:, :, pl.ds(0, part)], as_sem).wait()
+
+        @pl.loop(0, shards)
+        def _(s):
+            if j == 0:
+                move(normed.at[s], x.at[s], x_sem + s).wait()
+                move(cot.at[s], c.at[s], c_sem + s).wait()
+            pre = dot(x[s], w[slot].reshape(shards * rows, chunk))
+            grad_act = dot_t(c[s], d[slot])
+            gate, up = pre[:, :part], pre[:, part:]
+            sigmoid = 1.0 / (1.0 + jnp.exp(-gate))
+            silu = gate * sigmoid
+            act = (silu * up).astype(bf16).astype(f32)
+            grad_gate = (grad_act * up * sigmoid * (1.0 + gate * (1.0 - sigmoid))).astype(bf16)
+            grad_up = (grad_act * silu).astype(bf16)
+            at = pl.ds(pl.multiple_of(s * rows, rows), rows)
+            act_stage[s] = act.astype(bf16)
+            unit_stage[s, :, :part] = grad_gate
+            unit_stage[s, :, part:] = grad_up
+            act_t[:, at] = act.T.astype(bf16)
+            unit_t[:part, at] = grad_gate.astype(f32).T.astype(bf16)
+            unit_t[part:, at] = grad_up.astype(f32).T.astype(bf16)
+
+        move(unit_stage, kept_units.at[:, :, pl.ds(j * chunk, chunk)], us_sem).start()
+        move(act_stage, kept_acts.at[:, :, pl.ds(j * part, part)], as_sem).start()
+
+        @pl.loop(0, width // 256)
+        def _(n):
+            at = pl.ds(pl.multiple_of(n * 256, 256), 256)
+            unit_grad[:, at] = dot(unit_t[...], x[:, :, at].reshape(shards * rows, 256)).astype(
+                bf16
+            )
+            down_grad[:, at] = dot(act_t[...], c[:, :, at].reshape(shards * rows, 256)).astype(
+                bf16
+            )
+
+        keep_unit = move(unit_grad, unit_terms.at[j], ug_sem)
+        keep_down = move(down_grad, down_terms.at[j], dg_sem)
+        keep_unit.start()
+        keep_down.start()
+        keep_unit.wait()
+        keep_down.wait()
+        if j < EARLY:
+            for sums in line[j]:
+                sums.first()
+        if j >= 2:
+            pass_on(j - 2)
+    move(unit_stage, kept_units.at[:, :, pl.ds(0, chunk)], us_sem).wait()
+    move(act_stage, kept_acts.at[:, :, pl.ds(0, part)], as_sem).wait()
+
+    load_w = move(units, x, last_w)
+    load_w.start()
+    load_d = [
+        move(down.at[k, j], c.at[j, pl.ds(k * piece, piece)], last_d + 4 * j + k)
+        for j in range(CHUNKS)
+        for k in range(4)
+    ]
+    for load in load_d:
+        load.start()
+
+    class Computed:
+        names = [name for i, own, other in ORDER for name in (other, own)]
+
+        def __init__(self):
+            self.pairs, self.done = {}, 0
+            self.load(0).start()
+
+        def load(self, k):
+            return move(
+                kept_units.at[p[self.names[k]]],
+                unit_t.at[pl.ds(k % 2 * rows, rows)],
+                ub_sem + k % 2,
+            )
+
+        def compute(self, out):
+            k = self.done
+            self.load(k).wait()
+            if k + 1 < len(self.names):
+                self.load(k + 1).start()
+            if k == 0:
+                load_w.wait()
+
+            @pl.loop(0, shards)
+            def _(n):
+                at = pl.ds(pl.multiple_of(n * rows, rows), rows)
+                out[:, at] = dot_t(unit_t[k % 2 * rows : (k % 2 + 1) * rows], x[n]).astype(bf16)
+
+            self.done += 1
+
+        def ready(self, i):
+            k = self.done // 2
+            stage = unit_grad.at[pl.ds(k % 2 * rows, rows)]
+            if k >= 2:
+                self.pairs[ORDER[k - 2][0]].wait_send()
+            self.compute(stage)
+            self.pairs[i] = remote(p, stage, paired.at[i], send, recv, i, "sib")
+            self.pairs[i].start()
+            self.compute(kept.at[i])
+            self.pairs[i].wait_recv()
+
+        def finish(self):
+            for i, _, _ in ORDER[2:]:
+                self.pairs[i].wait_send()
+
+    def act_load(s):
+        slot = lax.rem(s, 2)
+        half = pl.multiple_of(slot * (width // 2), width // 2)
+        return move(kept_acts.at[s], act_t.at[:, pl.ds(half, width // 2)], ab_sem + slot)
+
+    def out_store(s):
+        slot = lax.rem(s, 2)
+        at = pl.ds(pl.multiple_of(slot * rows, rows), rows)
+        return move(unit_grad.at[at], out_terms.at[s], out_sem + slot)
+
+    def forward_terms():
+        source.finish()
+        for load in load_d:
+            load.wait()
+        act_load(0).start()
+
+        @pl.loop(0, shards)
+        def _(s):
+            act_load(s).wait()
+
+            @pl.when(s + 1 < shards)
+            def _():
+                act_load(s + 1).start()
+
+            @pl.when(s >= 2)
+            def _():
+                out_store(s - 2).wait()
+
+            slot = lax.rem(s, 2)
+            to = pl.ds(pl.multiple_of(slot * rows, rows), rows)
+
+            @pl.loop(0, width // 256)
+            def _(n):
+                at = pl.ds(pl.multiple_of(n * 256, 256), 256)
+                summed = jnp.zeros((rows, 256), f32)
+                for j in range(CHUNKS):
+                    base = pl.multiple_of(slot * (width // 2) + j * part, part)
+                    summed = summed + dot(act_t[:, pl.ds(base, part)], c[j, :, at])
+                unit_grad[to, at] = summed.astype(bf16)
+
+            out_store(s).start()
+
+        out_store(shards - 2).wait()
+        out_store(shards - 1).wait()
+        pass_on(2)
+
+    source = Computed()
+    sends = scatter_plane(
+        p, source, rows, kept, paired, far, final, send, recv, meanwhile=forward_terms
+    )
+    gain_term[...] = jnp.zeros_like(gain_term)
+
+    def step(at):
+        g = total(kept, paired, final, at)
+        h = hidden[at, :]
+        scale = lax.rsqrt(jnp.mean(h * h, axis=-1, keepdims=True) + norm_eps)
+        weighted = g * gain[...]
+        inner = jnp.mean(weighted * h, axis=-1, keepdims=True)
+        out = own_cot[at, :].astype(f32) + scale * weighted - h * (scale * scale * scale * inner)
+        grad_hidden[at, :] = out
+        down_grad[at, :] = out.astype(bf16)
+        gain_term[...] += jnp.sum(g * h * scale, axis=0, keepdims=True)
+
+    over_rows(rows, step)
+    sent = gather_start(p, down_grad, branch, gsend, grecv, 0)
+    own = move(down_grad, branch.at[p["me"]], own_sem)
+    own.start()
+
+    def sum_up(j):
+        line[j][0].total(unit_parts, local, z_sem)
+
+        @pl.loop(0, chunk // 128)
+        def _(n):
+            at = pl.ds(pl.multiple_of(n * 128, 128), 128)
+            turned[:, at] = unit_parts[0, at, :].astype(f32).T.astype(bf16)
+
+        line[j][1].total(down_parts, local, z_sem + 4)
+        out = [move(turned, unit_sums.at[j], turn_sem), move(down_parts.at[0], down_sums.at[j], turn_sem + 1)]
+        for copy in out:
+            copy.start()
+        for copy in out:
+            copy.wait()
+
+    sum_up(0)
+    gather_finish(p, sent, down_grad, branch, gsend, grecv, 0)
+    own.wait()
+    sum_up(1)
+    sum_up(2)
+    for j in range(EARLY):
+        for sums in line[j]:
+            sums.finish()
+    for copy in sends:
+        copy.wait_send()
+
+
+def feed_plane(normed, cot, units, down, own_cot, hidden, gain, collective_id):
+    shards, rows, width = normed.shape
+    wide = units.shape[1]
+    chunk = wide // CHUNKS
+    part = chunk // 2
+    piece = down.shape[0] // 16
+    sds = jax.ShapeDtypeStruct
+    return pl.pallas_call(
+        feed_kernel,
+        out_shape=[
+            sds((rows, width), f32),
+            sds((1, width), f32),
+            sds((shards, rows, width), bf16),
+            sds((shards, rows, width), bf16),
+            sds((EARLY, chunk, chunk), bf16),
+            sds((EARLY, piece, width), bf16),
+            sds((CHUNKS, chunk, width), bf16),
+            sds((CHUNKS, part, width), bf16),
+            sds((shards, rows, wide), bf16),
+            sds((shards, rows, wide // 2), bf16),
+            sds((EARLY, 4, chunk, chunk), bf16),
+            sds((EARLY, 4, piece, width), bf16),
+        ],
+        in_specs=[ANY] * 4 + [VMEM] * 3,
+        out_specs=[VMEM, VMEM] + [ANY] * 10,
+        scratch_shapes=[
+            pltpu.VMEM((shards, rows, width), bf16),
+            pltpu.VMEM((shards, rows, width), bf16),
+            pltpu.VMEM((2, shards, rows, chunk), bf16),
+            pltpu.VMEM((2, part, width), bf16),
+            pltpu.VMEM((shards, rows, chunk), bf16),
+            pltpu.VMEM((shards, rows, part), bf16),
+            pltpu.VMEM((chunk, shards * rows), bf16),
+            pltpu.VMEM((part, shards * rows), bf16),
+            pltpu.VMEM((chunk, width), bf16),
+            pltpu.VMEM((part, width), bf16),
+            pltpu.VMEM((EARLY, chunk, chunk), bf16),
+            pltpu.VMEM((EARLY, piece, width), bf16),
+            pltpu.VMEM((4, chunk, chunk), bf16),
+            pltpu.VMEM((4, piece, width), bf16),
+            pltpu.VMEM((chunk, chunk), bf16),
+        ]
+        + scatter_scratch(rows, width)[:6]
+        + [
+            DMA((GATHER_SEMS,)),
+            DMA((GATHER_SEMS,)),
+            DMA((8 * EARLY,)),
+            DMA((8 * EARLY,)),
+            DMA((72,)),
+        ],
+        compiler_params=pltpu.CompilerParams(
+            collective_id=collective_id, has_side_effects=True, vmem_limit_bytes=62 * MIB
+        ),
+        cost_estimate=lasting(160),
+    )(
+        normed,
+        cot,
+        units.reshape(shards, rows, wide),
+        down.reshape(4, CHUNKS, piece, width),
+        own_cot,
+        hidden,
+        gain,
+    )
+
+
+def tail_kernel(
+    devices,
+    terms,
+    out_terms,
+    unit_terms,
+    down_terms,
+    head_terms,
+    wo_terms,
+    unit_sums,
+    tokens,
+    hidden,
+    grad_hidden,
+    gain,
+    gain_two_term,
+    grad_tokens,
+    out_tokens,
+    gain_sums,
+    down_sum,
+    wo_sum,
+    units_out,
+    heads_out,
+    unit_sum,
+    head_sum,
+    unit_land,
+    down_land,
+    head_land,
+    wo_land,
+    gain_one_term,
+    gain_mine,
+    gain_land,
+    unit_acc,
+    down_acc,
+    head_acc,
+    wo_acc,
+    unit_parts,
+    down_parts,
+    head_parts,
+    turned,
+    zsend,
+    zrecv,
+    esend,
+    erecv,
+    gsend,
+    grecv,
+    local,
+    *scratch,
+):
+    p = plane()
+    names = ("dg", "ds", "xp", "yp", "xs", "ys", "sib")
+    mine = p["dp"] * 8 + p["me"]
+    barrier = pltpu.get_barrier_semaphore()
+
+    def other(k):
+        to = lax.rem(mine + k, devices)
+        return dict(device_id=(lax.div(to, 8), lax.rem(to, 8)), device_id_type=MESH), to
+
+    @pl.loop(1, devices)
+    def _(k):
+        pl.semaphore_signal(barrier, inc=1, **other(k)[0])
+
+    pl.semaphore_wait(barrier, devices - 1)
+    chunk = unit_terms.shape[1]
+    piece = down_terms.shape[1] // 4
+    rows = tokens.shape[0]
+    held = units_out.shape[2]
+    line = [
+        LineSum(p, lambda owner: head_terms.at[owner], head_land, zsend, zrecv, 0),
+        LineSum(
+            p,
+            lambda owner: unit_terms.at[
+                EARLY, :, pl.ds(pl.multiple_of(owner * chunk, chunk), chunk)
+            ],
+            unit_land,
+            zsend,
+            zrecv,
+            4,
+        ),
+        LineSum(
+            p,
+            lambda owner: down_terms.at[EARLY, pl.ds(pl.multiple_of(owner * piece, piece), piece)],
+            down_land,
+            zsend,
+            zrecv,
+            8,
+        ),
+        LineSum(p, lambda owner: wo_terms.at[owner], wo_land, zsend, zrecv, 12),
+    ]
+    for sums in line:
+        sums.first_far()
+    for sums in line:
+        sums.first_rest()
+    kept, paired, far, final, send, recv, loads = scratch[:7]
+    source = FromMemory(p, terms, kept, paired, send, recv, loads)
+    copies = []
+
+    def exchange(i, block, out):
+        for j, name in enumerate(names):
+            copies.append(remote(p, block(p[name]), out, esend, erecv, i * 7 + j, name))
+            copies[-1].start()
+        copies.append(pltpu.make_async_copy(block(p["me"]), out, local.at[i]))
+        copies[-1].start()
+
+    sends = scatter_plane(p, source, rows, kept, paired, far, final, send, recv)
+    gain_one_term[...] = jnp.zeros_like(gain_one_term)
+
+    def step(at):
+        g = total(kept, paired, final, at)
+        t = tokens[at, :].astype(f32)
+        scale = lax.rsqrt(jnp.mean(t * t, axis=-1, keepdims=True) + norm_eps)
+        weighted = g * gain[...]
+        inner = jnp.mean(weighted * t, axis=-1, keepdims=True)
+        grad_tokens[at, :] = (
+            grad_hidden[at, :] + scale * weighted - t * (scale * scale * scale * inner)
+        ).astype(bf16)
+        gain_one_term[...] += jnp.sum(g * t * scale, axis=0, keepdims=True)
+
+    over_rows(rows, step)
+    line[0].second(head_acc, head_parts.at[0], local, 8)
+    line[1].second(unit_acc, unit_parts.at[0], local, 8)
+    line[2].second(down_acc, down_parts.at[0], local, 8)
+    line[3].second(wo_acc, down_parts.at[1], local, 8)
+    gain_mine[...] = jnp.zeros_like(gain_mine)
+    for k in range(devices):
+        at = slice(k * held, (k + 1) * held)
+        gain_mine[k, 0:1, :held] = gain_one_term[:, at]
+        gain_mine[k, 1:2, :held] = gain_two_term[:, at]
+
+    def gain_copy(k):
+        where, to = other(k)
+        return pltpu.make_async_remote_copy(
+            src_ref=gain_mine.at[to],
+            dst_ref=gain_land.at[k],
+            send_sem=gsend.at[k],
+            recv_sem=grecv.at[k],
+            **where,
+        )
+
+    @pl.loop(1, devices)
+    def _(k):
+        gain_copy(k).start()
+
+    def rows_of(ref):
+        return lambda s: ref.at[pl.ds(pl.multiple_of(s * held, held), held)]
+
+    for j in range(EARLY):
+        exchange(j, rows_of(unit_sums.at[j]), units_out.at[j, p["me"]])
+    kept, paired, far, final, send, recv, loads = scratch[7:]
+    source_out = FromMemory(p, out_terms, kept, paired, send, recv, loads)
+    sends += scatter_plane(p, source_out, rows, kept, paired, far, final, send, recv)
+
+    def step_out(at):
+        out_tokens[at, :] = (hidden[at, :] + total(kept, paired, final, at)).astype(bf16)
+
+    over_rows(rows, step_out)
+    gain_land[0] = gain_mine[mine]
+
+    @pl.loop(1, devices)
+    def _(k):
+        gain_copy(k).wait()
+
+    gain_sums[...] = jnp.sum(gain_land[...], axis=0)
+
+    def store(src, dst, i):
+        copy = pltpu.make_async_copy(src, dst, local.at[i])
+        copy.start()
+        copy.wait()
+
+    line[0].total(head_parts, local, 8)
+    store(head_parts.at[0], head_sum, 8)
+    exchange(EARLY + 1, rows_of(head_sum), heads_out.at[p["me"]])
+    line[1].total(unit_parts, local, 8)
+
+    @pl.loop(0, chunk // 128)
+    def _(n):
+        at = pl.ds(pl.multiple_of(n * 128, 128), 128)
+        turned[:, at] = unit_parts[0, at, :].astype(f32).T.astype(bf16)
+
+    store(turned, unit_sum, 8)
+    exchange(EARLY, rows_of(unit_sum), units_out.at[EARLY, p["me"]])
+    line[2].total(down_parts, local, 8)
+    store(down_parts.at[0], down_sum, 8)
+    line[3].total(down_parts, local, 8)
+    store(down_parts.at[0], wo_sum, 8)
+    for copy in copies:
+        copy.wait()
+    for sums in line:
+        sums.finish()
+    source.finish()
+    source_out.finish()
+    for copy in sends:
+        copy.wait_send()
+
+
+def tail_plane(
+    groups,
+    shards,
+    terms,
+    out_terms,
+    unit_terms,
+    down_terms,
+    head_terms,
+    wo_terms,
+    unit_sums,
+    tokens,
+    hidden,
+    grad_hidden,
+    gain,
+    gain_two_term,
+    collective_id,
+):
+    rows, width = tokens.shape
+    devices = groups * shards
+    chunk, piece = unit_terms.shape[1], down_terms.shape[1] // 4
+    held = width // devices
+    span, heads_wide = head_terms.shape[1:]
+    wo_rows = wo_terms.shape[1]
+    sds = jax.ShapeDtypeStruct
+    unit, down_, head, wo_ = (
+        (chunk, chunk),
+        (piece, width),
+        (span, heads_wide),
+        (wo_rows, width),
+    )
+    return pl.pallas_call(
+        functools.partial(tail_kernel, devices),
+        out_shape=[
+            sds((rows, width), bf16),
+            sds((rows, width), bf16),
+            sds((8, 128), f32),
+            sds(down_, bf16),
+            sds(wo_, bf16),
+            sds((CHUNKS, shards, held, chunk), bf16),
+            sds((shards, held, heads_wide), bf16),
+            sds(unit, bf16),
+            sds(head, bf16),
+            sds((4,) + unit, bf16),
+            sds((4,) + down_, bf16),
+            sds((4,) + head, bf16),
+            sds((4,) + wo_, bf16),
+        ],
+        in_specs=[ANY] * 7 + [VMEM] * 5,
+        out_specs=[VMEM] * 3 + [ANY] * 10,
+        scratch_shapes=[
+            pltpu.VMEM((1, width), f32),
+            pltpu.VMEM((devices, 8, 128), f32),
+            pltpu.VMEM((devices, 8, 128), f32),
+            pltpu.VMEM(unit, bf16),
+            pltpu.VMEM(down_, bf16),
+            pltpu.VMEM(head, bf16),
+            pltpu.VMEM(wo_, bf16),
+            pltpu.VMEM((4,) + unit, bf16),
+            pltpu.VMEM((4,) + down_, bf16),
+            pltpu.VMEM((4,) + head, bf16),
+            pltpu.VMEM(unit, bf16),
+            DMA((16,)),
+            DMA((16,)),
+            DMA((35,)),
+            DMA((35,)),
+            DMA((devices,)),
+            DMA((devices,)),
+            DMA((12,)),
+        ]
+        + scatter_scratch(rows, width) * 2,
+        compiler_params=pltpu.CompilerParams(
+            collective_id=collective_id, has_side_effects=True, vmem_limit_bytes=60 * MIB
+        ),
+        cost_estimate=lasting(120),
+    )(
+        terms,
+        out_terms,
+        unit_terms,
+        down_terms,
+        head_terms,
+        wo_terms,
+        unit_sums,
+        tokens,
+        hidden,
+        grad_hidden,
+        gain,
+        gain_two_term,
+    )
+
+
 def layer(
     groups,
     shards,
@@ -675,15 +1363,16 @@
         blocks = w.reshape(held, outer, shards, inner)
         return jnp.moveaxis(blocks, 2, 0).reshape(shards, held, pairs, PAIR)
 
-    def by_unit(w):
-        return jnp.moveaxis(w.reshape(held, groups, shards, hidden_held), 2, 0).reshape(
-            shards, held, hidden_here
-        )
+    chunks = CHUNKS if shards == 8 else 1
+    piece = hidden_held // chunks
+
+    def by_unit(gate, up):
+        blocks = jnp.stack([gate, up]).reshape(2, held, groups, shards, chunks, piece)
+        return jnp.transpose(blocks, (3, 1, 4, 0, 2, 5)).reshape(shards, held, 2 * hidden_here)
 
     heads = jnp.stack([by_head(w) for w in (w_query, w_key, w_value)], axis=3)
     heads = heads.reshape(shards, held, 3 * pairs * PAIR)
-    units = jnp.concatenate([by_unit(w_gate), by_unit(w_up)], axis=-1)
-    heads, units = exchange_plane([heads, units], shards, 1)
+    heads, units = exchange_plane([heads, by_unit(w_gate, w_up)], shards, 1)
     heads = heads.reshape(shards * held, heads.shape[-1])
     units = units.reshape(shards * held, units.shape[-1])
     qkv_weight = lax.all_gather(heads, "dp", axis=0, tiled=True)
@@ -699,7 +1388,8 @@
     own_cotangent = cotangent.reshape(count, width)
     inputs = own_tokens.astype(f32)
     own_normed = (inputs * rms_scale(inputs) * gain_one).astype(bf16)
-    normed_one, cot = [flat(v) for v in gather_plane([own_normed, own_cotangent], shards, 2)]
+    normed_split, cot_split = gather_plane([own_normed, own_cotangent], shards, 2)
+    normed_one = flat(normed_split)
 
     cos, sin, starts = rope_tables(doc_ids, shards)
     starts = starts[:, None, :]
@@ -710,77 +1400,131 @@
     hidden, normed_two = forward_plane(
         split(dot(attended, out_weight).astype(bf16)), own_tokens, gain_two, 3
     )
-    normed_two = flat(normed_two)
-
-    gate_pre = dot(normed_two, unit_weight[:, :hidden_here])
-    up_pre = dot(normed_two, unit_weight[:, hidden_here:])
-    sigmoid = jax.nn.sigmoid(gate_pre)
-    silu = gate_pre * sigmoid
-    activated = (silu * up_pre).astype(bf16)
-    out_terms = split(dot(activated, down_weight).astype(bf16))
-    grad_act = dot_t(cot, down_weight)
-    grad_gate_pre = (grad_act * up_pre * sigmoid * (1.0 + gate_pre * (1.0 - sigmoid))).astype(bf16)
-    grad_up_pre = (grad_act * silu).astype(bf16)
-    grad_units = jnp.concatenate([grad_gate_pre, grad_up_pre], axis=-1)
-    middle_terms = split(dot_t(grad_units, unit_weight).astype(bf16))
-    unit_terms = dot(normed_two.T, grad_units).astype(bf16)
-    down_terms = dot(activated.T, cot).astype(bf16)
-    unit_sums = lax.psum_scatter(unit_terms, "dp", scatter_dimension=0, tiled=True)
-    down_sums = lax.psum_scatter(down_terms, "dp", scatter_dimension=0, tiled=True)
-
-    grad_hidden, gain_two_term, branch = middle_plane(
-        middle_terms, own_cotangent, hidden, gain_two, 4
-    )
+
+    if shards == 8:
+        (
+            grad_hidden,
+            gain_two_term,
+            branch,
+            out_terms,
+            unit_sums,
+            _,
+            unit_terms,
+            down_terms,
+            *_,
+        ) = fed = feed_plane(
+            normed_two, cot_split, unit_weight, down_weight, own_cotangent, hidden, gain_two, 4
+        )
+        down_sums = fed[5]
+    else:
+        cot = flat(cot_split)
+        normed_two = flat(normed_two)
+        gate_weight, up_weight = unit_weight[:, :hidden_here], unit_weight[:, hidden_here:]
+        gate_pre, up_pre = dot(normed_two, gate_weight), dot(normed_two, up_weight)
+        sigmoid = jax.nn.sigmoid(gate_pre)
+        silu = gate_pre * sigmoid
+        activated = (silu * up_pre).astype(bf16)
+        out_terms = split(dot(activated, down_weight).astype(bf16))
+        grad_act = dot_t(cot, down_weight)
+        grad_gate_pre = grad_act * up_pre * sigmoid * (1.0 + gate_pre * (1.0 - sigmoid))
+        grad_up_pre = grad_act * silu
+        grad_units = jnp.concatenate([grad_gate_pre, grad_up_pre], axis=-1).astype(bf16)
+        middle_terms = split(dot_t(grad_units, unit_weight).astype(bf16))
+        unit_sums = lax.psum_scatter(
+            dot(normed_two.T, grad_units).astype(bf16), "dp", scatter_dimension=0, tiled=True
+        )
+        down_sums = lax.psum_scatter(
+            dot(activated.T, cot).astype(bf16), "dp", scatter_dimension=0, tiled=True
+        )
+        back, gain_two_term = norm_back(
+            hidden, rms_scale(hidden), gain_two, reduce_plane(middle_terms)
+        )
+        grad_hidden = own_cotangent.astype(f32) + back
+        branch = lax.all_gather(grad_hidden.astype(bf16), "seq")
+
     branch = flat(branch)
     out_w_terms = dot(attended.T, branch).astype(bf16)
-    if whole_heads:
-        grad_out = lax.psum_scatter(out_w_terms, "dp", scatter_dimension=0, tiled=True)
-    else:
-        placed = lax.dynamic_update_slice_in_dim(
-            jnp.zeros((width, width), bf16), out_w_terms, lax.axis_index("seq") * inner, 0
-        )
-        grad_out = lax.psum_scatter(placed, ("dp", "seq"), scatter_dimension=0, tiled=True)
     grad_attended = by_row(dot_t(branch, out_weight).astype(bf16))
     grad_pre = flat(attend_back(rotated, grad_attended, cos, sin, starts, stats))
     last_terms = split(dot_t(grad_pre, qkv_weight).astype(bf16))
     head_terms = dot(normed_one.T, grad_pre).astype(bf16)
-    head_sums = lax.psum_scatter(head_terms, "dp", scatter_dimension=0, tiled=True)
-
-    grad_tokens, gain_one_term, out_tokens = last_plane(
-        last_terms, out_terms, own_tokens, hidden, grad_hidden, gain_one, 5
-    )
-    head_sums, unit_sums = exchange_plane(
-        [head_sums.reshape(shards, held, -1), unit_sums.reshape(shards, held, -1)], shards, 6
-    )
-
-    head_sums = head_sums.reshape(shards, held, pairs, 3, PAIR)
-
-    def heads_back(i):
-        blocks = head_sums[:, :, :, i, :].reshape(shards, held, outer, inner)
+
+    if shards == 8:
+        (
+            grad_tokens,
+            out_tokens,
+            gain_sums,
+            down_last,
+            grad_out,
+            units_back,
+            heads_back,
+            *_,
+        ) = tail_plane(
+            groups,
+            shards,
+            last_terms,
+            out_terms,
+            unit_terms,
+            down_terms,
+            head_terms.reshape(groups, -1, head_terms.shape[-1]),
+            out_w_terms.reshape(groups, -1, width),
+            unit_sums,
+            own_tokens,
+            hidden,
+            grad_hidden,
+            gain_one,
+            gain_two_term,
+            5,
+        )
+        grad_norms = gain_sums[:2, :held]
+        down_sums = jnp.concatenate([down_sums, down_last[None]]).reshape(hidden_held, width)
+    else:
+        if whole_heads:
+            grad_out = lax.psum_scatter(out_w_terms, "dp", scatter_dimension=0, tiled=True)
+        else:
+            placed = lax.dynamic_update_slice_in_dim(
+                jnp.zeros((width, width), bf16), out_w_terms, lax.axis_index("seq") * inner, 0
+            )
+            grad_out = lax.psum_scatter(placed, ("dp", "seq"), scatter_dimension=0, tiled=True)
+        back, gain_one_term = norm_back(
+            inputs, rms_scale(inputs), gain_one, reduce_plane(last_terms)
+        )
+        grad_tokens = (grad_hidden + back).astype(bf16)
+        out_tokens = (hidden + reduce_plane(out_terms)).astype(bf16)
+        head_sums = lax.psum_scatter(head_terms, "dp", scatter_dimension=0, tiled=True)
+        heads_back, units_back = exchange_plane(
+            [head_sums.reshape(shards, held, -1), unit_sums.reshape(shards, held, -1)], shards, 6
+        )
+        grad_norms = lax.psum_scatter(
+            jnp.concatenate([gain_one_term, gain_two_term]),
+            ("dp", "seq"),
+            scatter_dimension=1,
+            tiled=True,
+        )
+
+    heads_back = heads_back.reshape(shards, held, pairs, 3, PAIR)
+    units_back = units_back.reshape(chunks, shards, held, 2, groups, piece)
+
+    def head_grad(i):
+        blocks = heads_back[:, :, :, i, :].reshape(shards, held, outer, inner)
         return jnp.moveaxis(blocks, 0, 2).reshape(held, width).astype(f32)
 
-    def units_back(i):
-        blocks = unit_sums[:, :, i * hidden_here : (i + 1) * hidden_here]
-        blocks = blocks.reshape(shards, held, groups, hidden_held)
-        return jnp.moveaxis(blocks, 0, 2).reshape(held, -1).astype(f32)
-
-    gain_sums = lax.psum_scatter(
-        jnp.concatenate([gain_one_term, gain_two_term]),
-        ("dp", "seq"),
-        scatter_dimension=1,
-        tiled=True,
-    )
+    def unit_grad(i):
+        return (
+            jnp.transpose(units_back[:, :, :, i], (2, 3, 1, 0, 4)).reshape(held, -1).astype(f32)
+        )
+
     return (
         out_tokens.reshape(tokens.shape),
         grad_tokens.reshape(tokens.shape),
-        gain_sums[0],
-        heads_back(0),
-        heads_back(1),
-        heads_back(2),
+        grad_norms[0],
+        head_grad(0),
+        head_grad(1),
+        head_grad(2),
         grad_out.astype(f32),
-        gain_sums[1],
-        units_back(0),
-        units_back(1),
+        grad_norms[1],
+        unit_grad(0),
+        unit_grad(1),
         down_sums.astype(f32),
     )
 

time: 1200 us -> 909 us (0.76)
  waiting for transfers between devices: 437 us -> 68.2 us
  Pallas kernels: 441 us -> 628 us
  matrix products: 180 us -> 49.6 us
  local copies, waits for them, and re-layouts: 53.7 us -> 71.1 us
    reduce_scatter x4 -> x0, waiting for transfers between devices: 307 us -> none  [the longest x1 147 us: layer(): lax.psum_scatter(unit_terms, 'dp', scatter_dimension=0, tiled=True)]
    pallas_call x2, Pallas kernels: 165 us -> 387 us  [the longest x1 201 us: feed_plane(): pl.pallas_call(feed_kernel, out_shape=[sds((rows, width), f32), sds((1, w...]
    dot_general x9 -> x4, matrix products: 126 us -> 38 us  [dot(): return jnp.dot(a, b, preferred_element_type=f32)]
    unnamed x10 -> x4, waiting for transfers between devices: 78 us -> 1.92 us
    dot_general x4 -> x2, matrix products: 54.5 us -> 11.5 us  [dot_t(): lax.dot_general(a, b, (((1,), (1,)), ((), ())), preferred_element_type=f32)]
    pallas_call x2 -> x1, Pallas kernels: 72.2 us -> 36.9 us  [exchange_plane(): pl.pallas_call(functools.partial(exchange_kernel, count), out_shape=[jax....]
    all_gather x1, waiting for transfers between devices: 51.6 us -> 66.3 us  [layer(): unit_weight = lax.all_gather(units, 'dp', axis=0, tiled=True)]
  transfers between devices with their start and end apart: 9 -> 4, of which waited for: 6 -> 1; matrix products, arithmetic and copies ran while one was open for 9% -> 3% of each run, Pallas kernels for 15% -> 20%
where the time goes in v2:
time: 909 us; the launch traced here: 902 us
  Pallas kernels  628 us (69%)
  local copies, waits for them, and re-layouts  71.1 us (8%)
  waiting for transfers between devices  68.2 us (8%)
  matrix products  49.6 us (5%)
  blocking collectives  41.1 us (5%)
  other arithmetic  30.4 us (3%)
  between operations  14.4 us (2%)
    pallas_call x1, Pallas kernels, feed_plane(): pl.pallas_call(feed_kernel, out_shape=[sds((rows, width), f32), sds((1, w...  201 us
    pallas_call x1, Pallas kernels, tail_plane(): pl.pallas_call(functools.partial(tail_kernel, devices), out_shape=[sds((r...  185 us
    pallas_call x1, Pallas kernels, forward_plane(): pl.pallas_call(forward_kernel, out_shape=[jax.ShapeDtypeStruct((rows, wid...  80.4 us
    pallas_call x1, Pallas kernels, gather_plane(): pl.pallas_call(functools.partial(gather_kernel, count), out_shape=[jax.Sh...  77.4 us
    all_gather x1, waiting for transfers between devices, layer(): unit_weight = lax.all_gather(units, 'dp', axis=0, tiled=True)  66.3 us
    all_gather x1, blocking collectives, layer(): lax.all_gather(jnp.stack([norm1_gain, norm2_gain]), ('dp', 'seq'), axis=1...  41.1 us
    dot_general x4, matrix products, dot(): return jnp.dot(a, b, preferred_element_type=f32)  38 us
    pallas_call x1, Pallas kernels, exchange_plane(): pl.pallas_call(functools.partial(exchange_kernel, count), out_shape=[jax....  36.9 us
  transfers between devices with their start and end apart: 4, of which 1 were waited for; matrix products, arithmetic and copies ran while one was open for 3% of the time, Pallas kernels for 20%

profile of v2, /device:TPU:0, one launch (start us, length us, event | category | flops | bytes accessed | tf_op | source)
XLA Modules:
  0.0 902.5 jit_solution(702669362009041312)
XLA Ops:
  25.3 5.5 maximum_bitcast_fusion
  30.8 7.7 reshape.227.refs_1_
  38.5 36.9 %shard_map.204 = (bf16[8,64,768]{2,1,0:T(8,128)(2,1)}, bf16[8,64,2048]{2,1,0:T(8,128)(2,1)}) custom-call(bf16[8,64,768]{2,1,0:T(8,128)(2,1)} %reshape.226.refs_0_, bf16[8,64,2048]{2,1,0:T(8,128)(2,1)} %reshape.227.refs_1_), custom_call_target="tpu_custom_call" | custom-call | bytes 122500000 | tf_op jit(solution)/shard_map/pallas_call | solution.py:173
  78.7 41.1 %all-gather = bf16[32,64,2]{1,2,0:T(2,128)(2,1)S(1)} all-gather(bf16[1,64,2]{1,2,0:T(2,128)(2,1)S(1)} %maximum_bitcast_fusion.3), channel_id=1, replica_groups=mesh['dp'=4,'seq'=8] {'dp','seq'}, dimensions={0}, use_global_device_ids=true | all-gather | bytes 8448 | tf_op jit(solution)/shard_map/all_gather | solution.py:1357
  121.5 77.4 %shard_map.203 = (bf16[8,256,2048]{2,1,0:T(8,128)(2,1)}, bf16[8,256,2048]{2,1,0:T(8,128)(2,1)}) custom-call(bf16[256,2048]{1,0:T(8,128)(2,1)} %multiply_convert_fusion.refs_0_, bf16[256,2048]{1,0:T(8,128)(2,1)} %bitcast.117), custom_call_target="tpu_custom_call" | custom-call | bytes 280000000 | tf_op jit(solution)/shard_map/pallas_call | solution.py:135
  198.9 3.7 fusion.5
  205.7 12.3 %fusion.pre = f32[8,2,128,768]{3,2,1,0:T(8,128)} fusion(bf16[8,2,128,2048]{3,2,1,0:T(8,128)(2,1)} %bitcast.136, bf16[2048,768]{1,0:T(8,128)(2,1)} %all-gather.6.cloned.1.call-done), kind=kOutput, calls=%fused_computation.6 | convolution fusion | flops 6442450944 | bytes 17825792 | tf_op jit(solution)/shard_map/dot_general | solution.py:361
  218.0 22.6 %shard_map.205 = (bf16[8,2,128,768]{3,2,1,0:T(8,128)(2,1)}, bf16[8,2,128,256]{3,2,1,0:T(8,128)(2,1)S(1)}, f32[2,2,2,1024]{3,2,1,0:T(2,128)S(1)}) custom-call(f32[8,2,128,768]{3,2,1,0:T(8,128)} %fusion.pre, f32[8,2,128,128]{3,2,1,0:T(8,128)S(1)} %copy-done.5, f32[8,2,128,128]{3,2,1,0:T(8,128)S(1)} %copy-done.7, s32[2,1,1024]{2,1,0:T(1,128)S(1)} %bitcast.107), custom_call_target="tpu_custom_call" | custom-call | flops 4294967296 | bytes 12582912 | tf_op jit(solution)/shard_map/pallas_call | solution.py:419
  240.6 7.2 convolution_convert_fusion.1
  247.8 80.4 %shard_map.206 = (f32[256,2048]{1,0:T(8,128)S(1)}, bf16[8,256,2048]{2,1,0:T(8,128)(2,1)S(1)}) custom-call(bf16[8,256,2048]{2,1,0:T(8,128)(2,1)} %bitcast.110, bf16[256,2048]{1,0:T(8,128)(2,1)S(1)} %bitcast.104, f32[1,2048]{1,0:T(1,128)S(1)} %get-tuple-element.66.gain), custom_call_target="tpu_custom_call" | custom-call | bytes 280000000 | tf_op jit(solution)/shard_map/pallas_call | solution.py:325
  332.8 66.3 %all-gather.10.cloned.1.call-done = bf16[2048,2048]{1,0:T(8,128)(2,1)} async-done(((bf16[512,2048]{1,0:T(8,128)(2,1)}), bf16[2048,2048]{1,0:T(8,128)(2,1)}) %all-gather.10.cloned.1.call-update) | async-done | bytes 8388624 | tf_op jit(solution)/shard_map/all_gather | solution.py:1384
  399.1 201.4 %shard_map.207 = (f32[256,2048]{1,0:T(8,128)}, f32[1,2048]{1,0:T(1,128)}, bf16[8,256,2048]{2,1,0:T(8,128)(2,1)}, bf16[8,256,2048]{2,1,0:T(8,128)(2,1)}, bf16[3,5...) custom-call(bf16[8,256,2048]{2,1,0:T(8,128)(2,1)} %copy-done.3, ...), custom_call_target="tpu_custom_call" | custom-call | bytes 560000000 | tf_op jit(solution)/shard_map/pallas_call | solution.py:989
  600.5 6.9 convolution_convert_fusion.3
  609.8 23.8 %shard_map.208 = bf16[8,2,128,768]{3,2,1,0:T(8,128)(2,1)} custom-call(bf16[8,2,128,768]{3,2,1,0:T(8,128)(2,1)} %get-tuple-element.37.rotated, bf16[8,2,128,256]{3,2,1,0:T(8,128)(2,1)S(1)} %bitcast.109, f32[8,2,128,128]{3,2,1,0:T(8,128)S(1)} %copy-done.6, f32[8,2,128,128]{3,2,1,0:T(8,128)S(1)} %copy-done.8, s32[2,1,1024]{2,1,0:T(1,128)S(1)} %bitcast.108, ...), custom_call_target="tpu_custom_call" | custom-call | flops 10737418240 | bytes 9437184 | tf_op jit(solution)/shard_map/pallas_call | solution.py:492
  633.6 11.6 %convolution_convert_fusion.2 = bf16[2048,768]{1,0:T(8,128)(2,1)} fusion(bf16[2048,2048]{1,0:T(8,128)(2,1)} %bitcast.137, bf16[2048,768]{1,0:T(8,128)(2,1)} %bitcast.140), kind=kOutput, calls=%fused_computation.5 | convolution fusion | flops 6444023808 | bytes 14680064 | tf_op jit(solution)/shard_map/dot_general | solution.py:361
  645.2 9.1 %convolution_convert_fusion = bf16[2048,2048]{1,0:T(8,128)(2,1)} fusion(bf16[2048,768]{1,0:T(8,128)(2,1)S(1)} %bitcast.141, bf16[2048,768]{1,0:T(8,128)(2,1)S(1)} %copy-done.22), kind=kOutput, calls=%fused_computation | convolution fusion | flops 6446645248 | bytes 14680064 | tf_op jit(solution)/shard_map/dot_general | solution.py:357
  654.4 185.1 %shard_map.209 = (bf16[256,2048]{1,0:T(8,128)(2,1)}, bf16[256,2048]{1,0:T(8,128)(2,1)}, f32[8,128]{1,0:T(8,128)}, bf16[64,2048]{1,0:T(8,128)(2,1)}, bf16[64,2048...) custom-call(bf16[8,256,2048]{2,1,0:T(8,128)(2,1)} %bitcast.114, ...), custom_call_target="tpu_custom_call" | custom-call | bytes 420000000 | tf_op jit(solution)/shard_map/pallas_call | solution.py:1270
  845.5 5.1 fusion.2
  858.4 7.8 reshape.246
  866.2 4.9 convert_bitcast_fusion
  871.0 4.7 copy.73
  875.8 5.5 reshape.251
  881.2 6.9 copy.72
  888.1 5.6 reshape.250
  (114 shorter events, 48.6 us)
Async XLA Ops:
  7.2 4.0 copy-start.19
  7.2 198.5 %all-gather.6.cloned.1.call-start = ((), (), s32[]{:S(2)}) async-start(), calls=%async_computation | async-start | bytes 3932160 | tf_op jit(solution)/shard_map/all_gather | solution.py:1378
  11.9 4.3 copy-start.12
  38.5 39.0 %copy-start.21 = (s32[2,1024]{1,0:T(2,128)S(1)}, s32[2,1024]{1,0:T(2,128)}, u32[]{:S(2)}) copy-start(s32[2,1024]{1,0:T(2,128)} %param.13) | copy-start | bytes 24580
  38.5 40.2 %copy-start.23 = (bf16[64]{0:T(256)(128)(2,1)S(1)}, bf16[64]{0:T(256)(128)(2,1)}, u32[]{:S(2)}) copy-start(bf16[64]{0:T(256)(128)(2,1)} %param.20) | copy-start | bytes 388
  38.5 40.2 %copy-start.24 = (bf16[64]{0:T(256)(128)(2,1)S(1)}, bf16[64]{0:T(256)(128)(2,1)}, u32[]{:S(2)}) copy-start(bf16[64]{0:T(256)(128)(2,1)} %param.15) | copy-start | bytes 388
  38.5 81.4 %copy-start = (bf16[2,128,2048]{2,1,0:T(8,128)(2,1)S(1)}, bf16[2,128,2048]{2,1,0:T(8,128)(2,1)}, u32[]{:S(2)}) copy-start(bf16[2,128,2048]{2,1,0:T(8,128)(2,1)} %param.12) | copy-start | bytes 3145732
  75.4 165.1 %all-gather.8.cloned.1.call-start = ((), (), s32[]{:S(2)}) async-start(), calls=%async_computation.1 | async-start | bytes 1310720 | tf_op jit(solution)/shard_map/all_gather | solution.py:1380
  76.2 256.6 %all-gather.12.cloned.1.call-start = ((), (), s32[]{:S(2)}) async-start(), calls=%async_computation.3 | async-start | bytes 5242880 | tf_op jit(solution)/shard_map/all_gather | solution.py:1385
  76.9 322.1 %all-gather.10.cloned.1.call-start = ((), (), s32[]{:S(2)}) async-start(), calls=%async_computation.2 | async-start | bytes 10485760 | tf_op jit(solution)/shard_map/all_gather | solution.py:1384
  120.2 82.4 %copy-start.20 = (f32[1,2048]{1,0:T(1,128)}, f32[1,2048]{1,0:T(1,128)S(1)}, u32[]{:S(2)}) copy-start(f32[1,2048]{1,0:T(1,128)S(1)} %get-tuple-element.67.gain) | copy-start | bytes 24580
  120.2 127.6 %copy-start.9 = (f32[1,2048]{1,0:T(1,128)}, f32[1,2048]{1,0:T(1,128)S(1)}, u32[]{:S(2)}) copy-start(f32[1,2048]{1,0:T(1,128)S(1)} %get-tuple-element.66.gain) | copy-start | bytes 24580
  205.7 12.3 %copy-start.5 = (f32[8,2,128,128]{3,2,1,0:T(8,128)S(1)}, f32[8,2,128,128]{3,2,1,0:T(8,128)}, u32[]{:S(2)}) copy-start(f32[8,2,128,128]{3,2,1,0:T(8,128)} %get-tuple-element.73.cos) | copy-start | bytes 3145732
  205.7 12.3 %copy-start.7 = (f32[8,2,128,128]{3,2,1,0:T(8,128)S(1)}, f32[8,2,128,128]{3,2,1,0:T(8,128)}, u32[]{:S(2)}) copy-start(f32[8,2,128,128]{3,2,1,0:T(8,128)} %get-tuple-element.74.sin) | copy-start | bytes 3145732
  240.6 7.2 copy-start.1
  399.1 201.4 %copy-start.2 = (bf16[8,2,128,256]{3,2,1,0:T(8,128)(2,1)S(1)}, bf16[8,2,128,256]{3,2,1,0:T(8,128)(2,1)}, u32[]{:S(2)}) copy-start(bf16[8,2,128,256]{3,2,1,0:T(8,128)(2,1)} %copy-done.1) | copy-start | bytes 3145732
  600.5 6.9 copy-start.10
  600.5 6.9 copy-start.16
  633.6 11.6 %copy-start.22 = (bf16[2048,768]{1,0:T(8,128)(2,1)S(1)}, bf16[2048,768]{1,0:T(8,128)(2,1)}, u32[]{:S(2)}) copy-start(bf16[2048,768]{1,0:T(8,128)(2,1)} %all-gather.6.cloned.1.call-done) | copy-start | bytes 9437188
  633.6 11.6 %copy-start.25 = (bf16[8,2,128,768]{3,2,1,0:T(8,128)(2,1)S(1)}, bf16[8,2,128,768]{3,2,1,0:T(8,128)(2,1)}, u32[]{:S(2)}) copy-start(bf16[8,2,128,768]{3,2,1,0:T(8,128)(2,1)} %shard_map.208) | copy-start | bytes 9437188
  654.4 188.2 %copy-start.18 = (bf16[3,64,2048]{2,1,0:T(8,128)(2,1)S(1)}, bf16[3,64,2048]{2,1,0:T(8,128)(2,1)}, u32[]{:S(2)}) copy-start(bf16[3,64,2048]{2,1,0:T(8,128)(2,1)} %get-tuple-element.57) | copy-start | bytes 2359300
  839.4 5.7 copy-start.17
  888.1 5.6 copy-start.15
  888.1 6.6 copy-start.14
  (6 other events, 13.9 us)
Sparse Core Ops, SparseCore 0:
  75.5 63.7 all-gather.5
  140.9 26.6 all-gather.7
  169.1 80.2 all-gather.11
  250.9 148.1 all-gather.9

commit v3 on v2

--- a/solution.py
+++ b/solution.py
@@ -81,35 +81,47 @@
     return sent
 
 
-def gather_finish(p, sent, src, out, send, recv, base):
-    quarter = src.shape[0] // 4
-    part = lambda ref, k: ref.at[pl.ds(k * quarter, quarter)]
+def gather_pass(p, ref, send, recv, i, to):
+    copy = remote(p, ref, ref, send, recv, i, to)
+    copy.start()
+    return copy
+
+
+def gather_forward(p, sent, out, send, recv, base):
+    quarter = out.shape[1] // 4
+    part = lambda owner, k: out.at[p[owner], pl.ds(k * quarter, quarter)]
     passed = []
-
-    def forward(owner, k, i, to):
-        ref = part(out.at[p[owner]], k)
-        copy = remote(p, ref, ref, send, recv, base + i, to)
-        copy.start()
-        return copy
-
     for j in range(4):
         kx, ky = j, (j + 2) % 4
         sent["x", kx].wait_recv()
         if j < 2:
-            sent["far", kx] = forward("xp", kx, 9 + kx, "yp")
-        passed.append(forward("xp", kx, 13 + kx, "sib"))
+            sent["far", kx] = gather_pass(p, part("xp", kx), send, recv, base + 9 + kx, "yp")
+        passed.append(gather_pass(p, part("xp", kx), send, recv, base + 13 + kx, "sib"))
         sent["y", ky].wait_recv()
         if j < 2:
-            sent["far", ky] = forward("yp", ky, 9 + ky, "xp")
-        passed.append(forward("yp", ky, 17 + ky, "sib"))
-    for k in (0, 2, 1, 3):
-        sent["far", k].wait_recv()
-        passed.append(forward("dg", k, 21 + k, "sib"))
+            sent["far", ky] = gather_pass(p, part("yp", ky), send, recv, base + 9 + ky, "xp")
+        passed.append(gather_pass(p, part("yp", ky), send, recv, base + 17 + ky, "sib"))
+
+    def last():
+        for k in (0, 2, 1, 3):
+            sent["far", k].wait_recv()
+            passed.append(gather_pass(p, part("dg", k), send, recv, base + 21 + k, "sib"))
+
+    return passed, last
+
+
+def gather_wait(sent, late):
+    passed, last = late
+    last()
     sent["s"].wait_recv()
     for copy in passed:
         copy.wait_recv()
     for copy in list(sent.values()) + passed:
         copy.wait_send()
+
+
+def gather_finish(p, sent, out, send, recv, base):
+    gather_wait(sent, gather_forward(p, sent, out, send, recv, base))
 
 
 def gather_kernel(count, *refs):
@@ -123,7 +135,7 @@
         kept.append(pltpu.make_async_copy(sources[i], outs[i].at[p["me"]], local.at[i]))
         kept[i].start()
     for i in range(count):
-        gather_finish(p, sent[i], sources[i], outs[i], send, recv, i * GATHER_SEMS)
+        gather_finish(p, sent[i], outs[i], send, recv, i * GATHER_SEMS)
     for copy in kept:
         copy.wait()
 
@@ -280,31 +292,6 @@
     )
 
 
-def forward_kernel(
-    terms, tokens, gain, hidden, normed, kept, paired, far, final, send, recv, local, mine, gsend, grecv
-):
-    p = plane()
-    greet(p, ("sib", "xp", "yp"))
-    source = FromMemory(p, terms, kept, paired, send, recv, local)
-    sends = scatter_plane(p, source, tokens.shape[0], kept, paired, far, final, send, recv)
-
-    def step(at):
-        h = tokens[at, :].astype(f32) + total(kept, paired, final, at)
-        hidden[at, :] = h
-        scale = lax.rsqrt(jnp.mean(h * h, axis=-1, keepdims=True) + norm_eps)
-        mine[at, :] = (h * scale * gain[...]).astype(bf16)
-
-    over_rows(tokens.shape[0], step)
-    sent = gather_start(p, mine, normed, gsend, grecv, 0)
-    own = pltpu.make_async_copy(mine, normed.at[p["me"]], local.at[0])
-    own.start()
-    gather_finish(p, sent, mine, normed, gsend, grecv, 0)
-    own.wait()
-    source.finish()
-    for copy in sends:
-        copy.wait_send()
-
-
 def reduce_plane(terms):
     rows = terms.shape[1]
     return lax.psum_scatter(terms, "seq", scatter_dimension=0, tiled=False).astype(f32).reshape(
@@ -314,29 +301,6 @@
 
 def rms_scale(values):
     return lax.rsqrt(jnp.mean(values * values, axis=-1, keepdims=True) + norm_eps)
-
-
-def forward_plane(terms, tokens, gain, collective_id):
-    shards, rows, width = terms.shape
-    if shards != 8:
-        hidden = tokens.astype(f32) + reduce_plane(terms)
-        normed = (hidden * rms_scale(hidden) * gain).astype(bf16)
-        return hidden, lax.all_gather(normed, "seq")
-    return pl.pallas_call(
-        forward_kernel,
-        out_shape=[
-            jax.ShapeDtypeStruct((rows, width), f32),
-            jax.ShapeDtypeStruct((8, rows, width), bf16),
-        ],
-        in_specs=[ANY, VMEM, VMEM],
-        out_specs=[VMEM, ANY],
-        scratch_shapes=scatter_scratch(rows, width)
-        + [pltpu.VMEM((rows, width), bf16), DMA((GATHER_SEMS,)), DMA((GATHER_SEMS,))],
-        compiler_params=pltpu.CompilerParams(
-            collective_id=collective_id, has_side_effects=True, vmem_limit_bytes=40 * MIB
-        ),
-        cost_estimate=lasting(80),
-    )(terms, tokens, gain)
 
 
 def norm_back(values, scale, gain, grad):
@@ -367,34 +331,33 @@
     return (key >= start) & (key <= query)
 
 
-def attend_kernel(pre, cos, sin, starts, rotated, attended, stats):
+def attend_pair(pre, cos, sin, starts, rotated, attended, stats, r, pair):
     shards, _, shard_len, _ = pre.shape
     length = shards * shard_len
     block = min(256, length)
     per = block // shard_len
-    pre_all = pre[...].reshape(length, 3 * PAIR)
-    lane = lax.broadcasted_iota(jnp.int32, (length, PAIR), 1)
-    first = lax.rem(lane, HD) < HD // 2
-    cos_all, sin_all = cos[...].reshape(length, PAIR), sin[...].reshape(length, PAIR)
-
-    def rotate(v):
-        return v * cos_all + swap_halves(v, first) * sin_all
-
-    query = rotate(pre_all[:, :PAIR]).astype(bf16)
-    key = rotate(pre_all[:, PAIR : 2 * PAIR]).astype(bf16)
-    value = pre_all[:, 2 * PAIR :]
+    lanes = lambda i: pl.ds(pl.multiple_of((pair * 3 + i) * PAIR, PAIR), PAIR)
+    first = lax.rem(lax.broadcasted_iota(jnp.int32, (length, PAIR), 1), HD) < HD // 2
+    cos_all, sin_all = cos[:, r].reshape(length, PAIR), sin[:, r].reshape(length, PAIR)
+
+    def rotate(i):
+        v = pre[:, r, :, lanes(i)].reshape(length, PAIR)
+        return (v * cos_all + swap_halves(v, first) * sin_all).astype(bf16)
+
+    query, key = rotate(0), rotate(1)
+    value = pre[:, r, :, lanes(2)].reshape(length, PAIR)
     value_t = value.T.astype(bf16)
-    rotated[:, 0, :, :PAIR] = query.reshape(shards, shard_len, PAIR)
-    rotated[:, 0, :, PAIR : 2 * PAIR] = key.reshape(shards, shard_len, PAIR)
-    rotated[:, 0, :, 2 * PAIR :] = value.astype(bf16).reshape(shards, shard_len, PAIR)
+    for i, v in enumerate((query, key, value.astype(bf16))):
+        rotated[:, r, :, lanes(i)] = v.reshape(shards, shard_len, PAIR)
     left = lax.broadcasted_iota(jnp.int32, (block, PAIR), 1) < HD
     top = lax.broadcasted_iota(jnp.int32, (PAIR, block), 0) < HD
     scaled = query * jnp.asarray(0.125, bf16)
+    here_lanes = pl.ds(pl.multiple_of(pair * PAIR, PAIR), PAIR)
     for i in range(length // block):
         keys = (i + 1) * block
-        start = starts[0, :, i * block : (i + 1) * block]
-        mask = allowed_pairs(start, keys, block, i * block)
-        here = scaled[i * block : (i + 1) * block]
+        at = slice(i * block, (i + 1) * block)
+        mask = allowed_pairs(starts[:, at], keys, block, i * block)
+        here = scaled[at]
         results = []
         for h in range(2):
             own = jnp.where(left if h == 0 else ~left, here, jnp.zeros_like(here))
@@ -404,9 +367,15 @@
             summed = jnp.sum(shifted, axis=0, keepdims=True)
             probs = (shifted * (1.0 / summed)).astype(bf16)
             results.append(dot(value_t[:, :keys], probs))
-            stats[0, 0, h : h + 1, i * block : (i + 1) * block] = peak + jnp.log(summed)
+            stats[r, pair, h : h + 1, at] = peak + jnp.log(summed)
         merged = jnp.where(top, results[0], results[1]).T.astype(bf16)
-        attended[i * per : (i + 1) * per, 0, :, :] = merged.reshape(per, shard_len, PAIR)
+        attended[i * per : (i + 1) * per, r, :, here_lanes] = merged.reshape(
+            per, shard_len, PAIR
+        )
+
+
+def attend_kernel(pre, cos, sin, starts, rotated, attended, stats):
+    attend_pair(pre, cos, sin, starts[0], rotated, attended, stats, 0, 0)
 
 
 def attend(pre, cos, sin, starts):
@@ -636,24 +605,12 @@
             self.copy(self.land.at[0], 0, i, self.z).wait_send()
 
 
-CHUNKS = 4
-EARLY = 3
-
-
-class Local:
-    def __init__(self, sems):
-        self.sems, self.used = sems, 0
-
-    def take(self, count=1):
-        self.used += count
-        return self.used - count
-
-
 def feed_kernel(
     normed,
     cot,
     units,
     down,
+    w_down,
     own_cot,
     hidden,
     gain,
@@ -669,6 +626,8 @@
     kept_acts,
     unit_land,
     down_land,
+    late_units,
+    late_down,
     x,
     c,
     w,
@@ -694,6 +653,8 @@
     grecv,
     zsend,
     zrecv,
+    lsend,
+    lrecv,
     local,
 ):
     p = plane()
@@ -704,13 +665,13 @@
     for where in others:
         pl.semaphore_signal(barrier, inc=1, device_id=where, device_id_type=MESH)
     sems = Local(local)
-    x_sem, c_sem, w_sem, d_sem = sems.take(8), sems.take(8), sems.take(2), sems.take(8)
+    x_sem, c_sem, w_sem, d_sem = sems.take(8), sems.take(8), sems.take(2), sems.take(2)
     us_sem, as_sem, ug_sem, dg_sem = (sems.take() for _ in range(4))
     ub_sem, ab_sem, out_sem, last_w, last_d = (
         sems.take(2),
         sems.take(2),
         sems.take(2),
-        sems.take(),
+        sems.take(32),
         sems.take(16),
     )
     z_sem, own_sem, turn_sem = sems.take(8), sems.take(), sems.take(2)
@@ -718,22 +679,34 @@
     chunk = w.shape[3]
     part = chunk // 2
     piece = down.shape[2]
+    all_units = lambda j: units.at[j] if j < EARLY else late_units
+    all_down = lambda j: down.at[j] if j < EARLY else late_down
+    late = (
+        LineGather(
+            p, units.at[EARLY, p["dp"]], late_units, lsend, lrecv, 0, local.at[sems.take()]
+        ),
+        LineGather(
+            p,
+            w_down.at[pl.ds(EARLY * piece, piece)],
+            late_down,
+            lsend,
+            lrecv,
+            1,
+            local.at[sems.take()],
+        ),
+    )
 
     def move(src, dst, i):
         return pltpu.make_async_copy(src, dst, local.at[i])
 
-    def w_load(j):
-        return move(units.at[:, :, pl.ds(j * chunk, chunk)], w.at[j % 2], w_sem + j % 2)
-
-    def d_load(j):
-        return [
-            move(down.at[k, j], d.at[j % 2, pl.ds(k * piece, piece)], d_sem + 4 * (j % 2) + k)
-            for k in range(4)
-        ]
+    def chunk_loads(j):
+        return (
+            move(all_units(j), w.at[j % 2], w_sem + j % 2),
+            move(all_down(j), d.at[j % 2], d_sem + j % 2),
+        )
 
     def start_chunk(j):
-        w_load(j).start()
-        for load in d_load(j):
+        for load in chunk_loads(j):
             load.start()
 
     start_chunk(0)
@@ -741,6 +714,8 @@
         move(normed.at[s], x.at[s], x_sem + s).start()
         move(cot.at[s], c.at[s], c_sem + s).start()
     pl.semaphore_wait(barrier, len(others))
+    for gather in late:
+        gather.start()
 
     line = {}
     for j in range(EARLY):
@@ -773,10 +748,13 @@
 
     for j in range(CHUNKS):
         slot = j % 2
-        w_load(j).wait()
-        for load in d_load(j):
+        if j == EARLY:
+            for gather in late:
+                gather.finish()
+            start_chunk(j)
+        for load in chunk_loads(j):
             load.wait()
-        if j + 1 < CHUNKS:
+        if j + 1 < EARLY:
             start_chunk(j + 1)
         if j > 0:
             move(unit_stage, kept_units.at[:, :, pl.ds(0, chunk)], us_sem).wait()
@@ -788,7 +766,7 @@
                 move(normed.at[s], x.at[s], x_sem + s).wait()
                 move(cot.at[s], c.at[s], c_sem + s).wait()
             pre = dot(x[s], w[slot].reshape(shards * rows, chunk))
-            grad_act = dot_t(c[s], d[slot])
+            grad_act = dot_t(c[s], d[slot].reshape(part, width))
             gate, up = pre[:, :part], pre[:, part:]
             sigmoid = 1.0 / (1.0 + jnp.exp(-gate))
             silu = gate * sigmoid
@@ -822,6 +800,11 @@
         keep_down.start()
         keep_unit.wait()
         keep_down.wait()
+        for gather in late:
+            if j == 0:
+                gather.second()
+            if j == 1:
+                gather.third()
         if j < EARLY:
             for sums in line[j]:
                 sums.first()
@@ -830,59 +813,45 @@
     move(unit_stage, kept_units.at[:, :, pl.ds(0, chunk)], us_sem).wait()
     move(act_stage, kept_acts.at[:, :, pl.ds(0, part)], as_sem).wait()
 
-    load_w = move(units, x, last_w)
-    load_w.start()
+    load_w = [
+        move(
+            all_units(j).at[k // 2, pl.ds(k % 2 * rows, rows)],
+            x.at[k, :, pl.ds(j * chunk, chunk)],
+            last_w + 8 * j + k,
+        )
+        for j in range(CHUNKS)
+        for k in range(shards)
+    ]
     load_d = [
-        move(down.at[k, j], c.at[j, pl.ds(k * piece, piece)], last_d + 4 * j + k)
+        move(all_down(j).at[k], c.at[j, pl.ds(k * piece, piece)], last_d + 4 * j + k)
         for j in range(CHUNKS)
         for k in range(4)
     ]
-    for load in load_d:
+    for load in load_w + load_d:
         load.start()
 
-    class Computed:
-        names = [name for i, own, other in ORDER for name in (other, own)]
-
-        def __init__(self):
-            self.pairs, self.done = {}, 0
-            self.load(0).start()
-
-        def load(self, k):
-            return move(
-                kept_units.at[p[self.names[k]]],
-                unit_t.at[pl.ds(k % 2 * rows, rows)],
-                ub_sem + k % 2,
-            )
-
-        def compute(self, out):
-            k = self.done
-            self.load(k).wait()
-            if k + 1 < len(self.names):
-                self.load(k + 1).start()
-            if k == 0:
-                load_w.wait()
-
-            @pl.loop(0, shards)
-            def _(n):
-                at = pl.ds(pl.multiple_of(n * rows, rows), rows)
-                out[:, at] = dot_t(unit_t[k % 2 * rows : (k % 2 + 1) * rows], x[n]).astype(bf16)
-
-            self.done += 1
-
-        def ready(self, i):
-            k = self.done // 2
-            stage = unit_grad.at[pl.ds(k % 2 * rows, rows)]
-            if k >= 2:
-                self.pairs[ORDER[k - 2][0]].wait_send()
-            self.compute(stage)
-            self.pairs[i] = remote(p, stage, paired.at[i], send, recv, i, "sib")
-            self.pairs[i].start()
-            self.compute(kept.at[i])
-            self.pairs[i].wait_recv()
-
-        def finish(self):
-            for i, _, _ in ORDER[2:]:
-                self.pairs[i].wait_send()
+    order = [name for _, own, far_name in ORDER for name in (far_name, own)]
+
+    def load_kept(k):
+        return move(
+            kept_units.at[p[order[k]]], unit_t.at[pl.ds(k % 2 * rows, rows)], ub_sem + k % 2
+        )
+
+    load_kept(0).start()
+
+    def produce(name, out):
+        k = order.index(name)
+        load_kept(k).wait()
+        if k + 1 < len(order):
+            load_kept(k + 1).start()
+        if k == 0:
+            for load in load_w:
+                load.wait()
+
+        @pl.loop(0, shards)
+        def _(n):
+            at = pl.ds(pl.multiple_of(n * rows, rows), rows)
+            out[:, at] = dot_t(unit_t[k % 2 * rows : (k % 2 + 1) * rows], x[n]).astype(bf16)
 
     def act_load(s):
         slot = lax.rem(s, 2)
@@ -930,7 +899,7 @@
         out_store(shards - 1).wait()
         pass_on(2)
 
-    source = Computed()
+    source = Produced(p, produce, unit_grad, kept, paired, send, recv)
     sends = scatter_plane(
         p, source, rows, kept, paired, far, final, send, recv, meanwhile=forward_terms
     )
@@ -968,7 +937,7 @@
             copy.wait()
 
     sum_up(0)
-    gather_finish(p, sent, down_grad, branch, gsend, grecv, 0)
+    gather_finish(p, sent, branch, gsend, grecv, 0)
     own.wait()
     sum_up(1)
     sum_up(2)
@@ -979,12 +948,12 @@
         copy.wait_send()
 
 
-def feed_plane(normed, cot, units, down, own_cot, hidden, gain, collective_id):
+def feed_plane(normed, cot, units, down, w_down, own_cot, hidden, gain, collective_id):
     shards, rows, width = normed.shape
-    wide = units.shape[1]
-    chunk = wide // CHUNKS
+    chunk = units.shape[3]
+    wide = chunk * CHUNKS
     part = chunk // 2
-    piece = down.shape[0] // 16
+    piece = down.shape[2]
     sds = jax.ShapeDtypeStruct
     return pl.pallas_call(
         feed_kernel,
@@ -1001,14 +970,16 @@
             sds((shards, rows, wide // 2), bf16),
             sds((EARLY, 4, chunk, chunk), bf16),
             sds((EARLY, 4, piece, width), bf16),
+            sds((4, width // 4, chunk), bf16),
+            sds((4, piece, width), bf16),
         ],
-        in_specs=[ANY] * 4 + [VMEM] * 3,
-        out_specs=[VMEM, VMEM] + [ANY] * 10,
+        in_specs=[ANY] * 5 + [VMEM] * 3,
+        out_specs=[VMEM, VMEM] + [ANY] * 12,
         scratch_shapes=[
             pltpu.VMEM((shards, rows, width), bf16),
             pltpu.VMEM((shards, rows, width), bf16),
-            pltpu.VMEM((2, shards, rows, chunk), bf16),
-            pltpu.VMEM((2, part, width), bf16),
+            pltpu.VMEM((2, 4, width // 4, chunk), bf16),
+            pltpu.VMEM((2, 4, piece, width), bf16),
             pltpu.VMEM((shards, rows, chunk), bf16),
             pltpu.VMEM((shards, rows, part), bf16),
             pltpu.VMEM((chunk, shards * rows), bf16),
@@ -1027,7 +998,9 @@
             DMA((GATHER_SEMS,)),
             DMA((8 * EARLY,)),
             DMA((8 * EARLY,)),
-            DMA((72,)),
+            DMA((2 * LINE_SEMS,)),
+            DMA((2 * LINE_SEMS,)),
+            DMA((100,)),
         ],
         compiler_params=pltpu.CompilerParams(
             collective_id=collective_id, has_side_effects=True, vmem_limit_bytes=62 * MIB
@@ -1036,8 +1009,9 @@
     )(
         normed,
         cot,
-        units.reshape(shards, rows, wide),
-        down.reshape(4, CHUNKS, piece, width),
+        units,
+        down,
+        w_down,
         own_cot,
         hidden,
         gain,
@@ -1327,6 +1301,463 @@
     )
 
 
+LINE_SEMS = 5
+
+
+class LineGather:
+    def __init__(self, p, src, out, send, recv, base, own=None):
+        self.p, self.src, self.out = p, src, out
+        self.send, self.recv, self.base = send, recv, base * LINE_SEMS
+        self.z = p["dp"]
+        self.inward = 1 - 2 * lax.div(self.z, 2)
+        self.end = (self.z == 0) | (self.z == 3)
+        self.own = None if own is None else pltpu.make_async_copy(src, out.at[self.z], own)
+
+    def copy(self, src, owner, i, to):
+        return pltpu.make_async_remote_copy(
+            src_ref=src,
+            dst_ref=self.out.at[owner],
+            send_sem=self.send.at[self.base + i],
+            recv_sem=self.recv.at[self.base + owner],
+            device_id=(to, self.p["me"]),
+            device_id_type=MESH,
+        )
+
+    def arrived(self, owner):
+        self.copy(self.src, owner, 0, self.z).wait_recv()
+
+    def start(self):
+        z, inward = self.z, self.inward
+        if self.own is not None:
+            self.own.start()
+        self.copy(self.src, z, 0, z + inward).start()
+
+        @pl.when(jnp.logical_not(self.end))
+        def _():
+            self.copy(self.src, z, 1, z - inward).start()
+
+    def second(self):
+        z, inward = self.z, self.inward
+
+        @pl.when(jnp.logical_not(self.end))
+        def _():
+            outer, inner = z - inward, z + inward
+            self.arrived(inner)
+            self.copy(self.out.at[inner], inner, 2, outer).start()
+            self.arrived(outer)
+            self.copy(self.out.at[outer], outer, 3, inner).start()
+
+    def third(self):
+        z, inward = self.z, self.inward
+
+        @pl.when(jnp.logical_not(self.end))
+        def _():
+            far = z + 2 * inward
+            self.arrived(far)
+            self.copy(self.out.at[far], far, 4, z - inward).start()
+
+    def finish(self):
+        z, inward = self.z, self.inward
+
+        @pl.when(self.end)
+        def _():
+            for k in range(1, 4):
+                self.arrived(z + k * inward)
+
+        if self.own is not None:
+            self.own.wait()
+        self.copy(self.src, 0, 0, z).wait_send()
+
+        @pl.when(jnp.logical_not(self.end))
+        def _():
+            for i in range(1, 5):
+                self.copy(self.src, 0, i, z).wait_send()
+
+
+CHUNKS = 4
+EARLY = 3
+OTHERS = ("dg", "ds", "xp", "yp", "xs", "ys", "sib")
+
+
+def meet_all(p, devices):
+    mine = p["dp"] * 8 + p["me"]
+    barrier = pltpu.get_barrier_semaphore()
+
+    def other(k):
+        to = lax.rem(mine + k, devices)
+        return dict(device_id=(lax.div(to, 8), lax.rem(to, 8)), device_id_type=MESH), to
+
+    @pl.loop(1, devices)
+    def _(k):
+        pl.semaphore_signal(barrier, inc=1, **other(k)[0])
+
+    return other, lambda: pl.semaphore_wait(barrier, devices - 1)
+
+
+class Local:
+    def __init__(self, sems):
+        self.sems, self.used = sems, 0
+
+    def take(self, count=1):
+        self.used += count
+        return self.used - count
+
+
+class Produced:
+    def __init__(self, p, produce, stage, kept, paired, send, recv):
+        self.p, self.produce, self.stage = p, produce, stage
+        self.kept, self.paired, self.send, self.recv = kept, paired, send, recv
+        self.pairs = {}
+
+    def ready(self, i):
+        k = len(self.pairs)
+        _, own, other = ORDER[k]
+        rows = self.kept.shape[1]
+        stage = self.stage.at[pl.ds(k % 2 * rows, rows)]
+        if k >= 2:
+            self.pairs[ORDER[k - 2][0]].wait_send()
+        self.produce(other, stage)
+        self.pairs[i] = remote(self.p, stage, self.paired.at[i], self.send, self.recv, i, "sib")
+        self.pairs[i].start()
+        self.produce(own, self.kept.at[i])
+        self.pairs[i].wait_recv()
+
+    def finish(self):
+        for i, _, _ in ORDER[2:]:
+            self.pairs[i].wait_send()
+
+
+def front_kernel(
+    groups,
+    own_cot,
+    w_out,
+    w_down,
+    tokens,
+    gains,
+    w_query,
+    w_key,
+    w_value,
+    w_gate,
+    w_up,
+    cos,
+    sin,
+    starts,
+    hidden,
+    gain_one,
+    gain_two,
+    rotated,
+    attended,
+    stats,
+    normed_one,
+    cot,
+    normed_two,
+    qkv,
+    out_weight,
+    units,
+    down,
+    gains_land,
+    head_blocks,
+    unit_blocks,
+    x,
+    w,
+    wo,
+    pre,
+    mine,
+    stage,
+    kept,
+    paired,
+    far,
+    final,
+    send,
+    recv,
+    asend,
+    arecv,
+    csend,
+    crecv,
+    nsend,
+    nrecv,
+    gsend,
+    grecv,
+    esend,
+    erecv,
+    zsend,
+    zrecv,
+    local,
+):
+    p = plane()
+    devices = groups * 8
+    other, met = meet_all(p, devices)
+    shards, rows, width = x.shape
+    held = w_query.shape[0]
+    pairs = width // 8 // PAIR
+    piece = down.shape[2]
+    me, z = p["me"], p["dp"]
+    mine_index = z * 8 + me
+    sems = Local(local)
+
+    def move(src, dst, i):
+        return pltpu.make_async_copy(src, dst, local.at[i])
+
+    for s in range(shards):
+        for pair in range(pairs):
+            for i, weight in enumerate((w_query, w_key, w_value)):
+                head = lambda k: ((2 * pair + k) * 8 + s) * HD
+                base = (pair * 3 + i) * PAIR
+                head_blocks[s, :, base : base + PAIR] = jnp.concatenate(
+                    [weight[:, head(k) : head(k) + HD] for k in range(2)], axis=1
+                )
+    met()
+
+    def gain_copy(k, sender):
+        return pltpu.make_async_remote_copy(
+            src_ref=gains,
+            dst_ref=gains_land.at[sender],
+            send_sem=gsend.at[k],
+            recv_sem=grecv.at[sender],
+            **other(k)[0],
+        )
+
+    @pl.loop(1, devices)
+    def _(k):
+        gain_copy(k, mine_index).start()
+
+    gains_land[mine_index] = gains[...]
+    held_at = pl.ds(pl.multiple_of(me * held, held), held)
+
+    def exchange(block, out, i):
+        copies = [
+            remote(p, block(p[name]), out, esend, erecv, i * 7 + j, name)
+            for j, name in enumerate(OTHERS)
+        ]
+        copies.append(move(block(me), out, sems.take()))
+        for copy in copies:
+            copy.start()
+        return copies
+
+    head_copies = exchange(lambda s: head_blocks.at[s], qkv.at[z, held_at], 0)
+    wo_line = LineGather(p, w_out, out_weight, zsend, zrecv, 0, local.at[sems.take()])
+    wo_line.start()
+
+    for s in range(shards):
+        for i, weight in enumerate((w_gate, w_up)):
+            for j in range(CHUNKS):
+                for pair in range(groups // 2):
+                    unit = lambda k: ((2 * pair + k) * 8 + s) * CHUNKS * piece + j * piece
+                    base = i * groups * piece + pair * 2 * piece
+                    unit_blocks[s, j, :, base : base + 2 * piece] = jnp.concatenate(
+                        [weight[:, unit(k) : unit(k) + piece] for k in range(2)], axis=1
+                    )
+
+    unit_copies = exchange(lambda s: unit_blocks.at[s], units.at[:, z, held_at], 1)
+
+    @pl.loop(1, devices)
+    def _(k):
+        gain_copy(k, lax.rem(mine_index + devices - k, devices)).wait()
+
+    for out, base in ((gain_one, 0), (gain_two, held)):
+        for k in range(0, devices, 2):
+            out[:, k * held : (k + 2) * held] = jnp.concatenate(
+                [gains_land[k + i, 0:1, base : base + held] for i in range(2)], axis=1
+            )
+
+    def norm_tokens(at):
+        t = tokens[at, :].astype(f32)
+        scale = lax.rsqrt(jnp.mean(t * t, axis=-1, keepdims=True) + norm_eps)
+        mine[at, :] = (t * scale * gain_one[...]).astype(bf16)
+
+    over_rows(rows, norm_tokens)
+    n1_sent = gather_start(p, mine, x, asend, arecv, 0)
+    n1_own = move(mine, x.at[me], sems.take())
+    n1_own.start()
+    for copy in head_copies:
+        copy.wait()
+    qkv_line = LineGather(p, qkv.at[z], qkv, zsend, zrecv, 1)
+    qkv_line.start()
+    n1_late = gather_forward(p, n1_sent, x, asend, arecv, 0)
+    wo_line.second()
+    qkv_line.second()
+    for copy in unit_copies:
+        copy.wait()
+    chunk_lines = [
+        (
+            LineGather(p, units.at[j, z], units.at[j], zsend, zrecv, 2 + 2 * j),
+            LineGather(
+                p,
+                w_down.at[pl.ds(j * piece, piece)],
+                down.at[j],
+                zsend,
+                zrecv,
+                3 + 2 * j,
+                local.at[sems.take()],
+            ),
+        )
+        for j in range(EARLY)
+    ]
+
+    def serve(j, what):
+        for line in chunk_lines[j]:
+            getattr(line, what)()
+
+    gather_wait(n1_sent, n1_late)
+    n1_own.wait()
+    cot_sent = gather_start(p, own_cot, cot, csend, crecv, 0)
+    cot_own = move(own_cot, cot.at[me], sems.take())
+    cot_own.start()
+    wo_line.third()
+    qkv_line.third()
+    serve(0, "start")
+    keep_normed = move(x, normed_one, sems.take())
+    keep_normed.start()
+    qkv_line.finish()
+    load_w = move(qkv, w, sems.take())
+    load_w.start()
+    load_w.wait()
+
+    @pl.loop(0, shards)
+    def _(s):
+        pre[s] = dot(x[s], w[...].reshape(width, w.shape[2])).reshape(pre.shape[1:])
+
+    def attention(r):
+        @pl.loop(0, pairs)
+        def _(pair):
+            attend_pair(
+                pre,
+                cos,
+                sin,
+                starts[r],
+                rotated,
+                attended,
+                stats,
+                r,
+                pair,
+            )
+
+    attention(0)
+    serve(0, "second")
+    serve(1, "start")
+    cot_late = gather_forward(p, cot_sent, cot, csend, crecv, 0)
+    attention(1)
+    serve(0, "third")
+    wo_line.finish()
+    load_wo = move(out_weight, wo, sems.take())
+    load_wo.start()
+    load_wo.wait()
+    gather_wait(cot_sent, cot_late)
+    cot_own.wait()
+
+    def produce(name, out):
+        s = p[name]
+        terms = attended[s].reshape(rows, attended.shape[3])
+
+        @pl.loop(0, width // 512)
+        def _(n):
+            at = pl.ds(pl.multiple_of(n * 512, 512), 512)
+            out[:, at] = dot(terms, wo[:, :, at].reshape(terms.shape[1], 512)).astype(bf16)
+
+    def meanwhile():
+        serve(1, "second")
+        serve(2, "start")
+
+    source = Produced(p, produce, stage, kept, paired, send, recv)
+    sends = scatter_plane(p, source, rows, kept, paired, far, final, send, recv, meanwhile)
+    keep_normed.wait()
+
+    def step(at):
+        h = tokens[at, :].astype(f32) + total(kept, paired, final, at)
+        hidden[at, :] = h
+        scale = lax.rsqrt(jnp.mean(h * h, axis=-1, keepdims=True) + norm_eps)
+        mine[at, :] = (h * scale * gain_two[...]).astype(bf16)
+
+    over_rows(rows, step)
+    n2_sent = gather_start(p, mine, normed_two, nsend, nrecv, 0)
+    n2_own = move(mine, normed_two.at[me], sems.take())
+    n2_own.start()
+    serve(1, "third")
+    serve(2, "second")
+    n2_late = gather_forward(p, n2_sent, normed_two, nsend, nrecv, 0)
+    serve(2, "third")
+    gather_wait(n2_sent, n2_late)
+    n2_own.wait()
+    for j in range(EARLY):
+        serve(j, "finish")
+    source.finish()
+    for copy in sends:
+        copy.wait_send()
+
+
+def front_plane(
+    groups, tokens, cotangent, gains, w_query, w_key, w_value, w_out, w_gate, w_up, w_down, tables, collective_id
+):
+    cos, sin, starts = tables
+    shards, batch, shard_len, _ = cos.shape
+    rows, width = tokens.shape
+    held, devices = w_query.shape[0], groups * shards
+    mine = width // shards
+    wide = 3 * mine
+    pairs = mine // PAIR
+    chunk = 2 * groups * w_down.shape[0] // CHUNKS
+    piece = w_down.shape[0] // CHUNKS
+    length = shards * shard_len
+    sds = jax.ShapeDtypeStruct
+    full = (shards, rows, width)
+    scratch = [
+        pltpu.VMEM((devices, 8, 2 * held), f32),
+        pltpu.VMEM((shards, held, wide), bf16),
+        pltpu.VMEM((shards, CHUNKS, held, chunk), bf16),
+        pltpu.VMEM(full, bf16),
+        pltpu.VMEM((groups, shards * held, wide), bf16),
+        pltpu.VMEM((groups, held, width), bf16),
+        pltpu.VMEM((shards, batch, shard_len, wide), f32),
+        pltpu.VMEM((rows, width), bf16),
+        pltpu.VMEM((2 * rows, width), bf16),
+        *scatter_scratch(rows, width)[:6],
+        *[DMA((GATHER_SEMS,))] * 6,
+        *[DMA((devices,))] * 2,
+        *[DMA((14,))] * 2,
+        *[DMA((LINE_SEMS * (2 + 2 * EARLY),))] * 2,
+        DMA((24,)),
+    ]
+    return pl.pallas_call(
+        functools.partial(front_kernel, groups),
+        out_shape=[
+            sds((rows, width), f32),
+            sds((1, width), f32),
+            sds((1, width), f32),
+            sds((shards, batch, shard_len, wide), bf16),
+            sds((shards, batch, shard_len, mine), bf16),
+            sds((batch, pairs, 2, length), f32),
+            sds(full, bf16),
+            sds(full, bf16),
+            sds(full, bf16),
+            sds((groups, shards * held, wide), bf16),
+            sds((groups, held, width), bf16),
+            sds((CHUNKS, groups, shards * held, chunk), bf16),
+            sds((EARLY, groups, piece, width), bf16),
+        ],
+        in_specs=[ANY] * 3 + [VMEM] * 10,
+        out_specs=[VMEM] * 6 + [ANY] * 7,
+        scratch_shapes=scratch,
+        compiler_params=pltpu.CompilerParams(
+            collective_id=collective_id, has_side_effects=True, vmem_limit_bytes=62 * MIB
+        ),
+        cost_estimate=lasting(200),
+    )(
+        cotangent,
+        w_out,
+        w_down,
+        tokens,
+        jnp.broadcast_to(gains.reshape(1, -1).astype(f32), (8, 2 * held)),
+        w_query,
+        w_key,
+        w_value,
+        w_gate,
+        w_up,
+        cos,
+        sin,
+        starts,
+    )
+
+
 def layer(
     groups,
     shards,
@@ -1351,74 +1782,104 @@
     whole_heads = held % HD == 0
     outer, inner = (groups, held) if whole_heads else (1, width // shards)
     pairs = width // shards // PAIR
+    both = ("dp", "seq")
+    fast = groups == 4 and shards == 8
     flat = lambda v: v.reshape(shards * count, v.shape[-1])
     split = lambda v: v.reshape(shards, count, v.shape[-1])
 
-    gains = lax.all_gather(
-        jnp.stack([norm1_gain, norm2_gain]), ("dp", "seq"), axis=1, tiled=True
-    ).astype(f32)
-    gain_one, gain_two = gains[:1], gains[1:]
-
-    def by_head(w):
-        blocks = w.reshape(held, outer, shards, inner)
-        return jnp.moveaxis(blocks, 2, 0).reshape(shards, held, pairs, PAIR)
-
-    chunks = CHUNKS if shards == 8 else 1
+    chunks = CHUNKS if fast else 1
     piece = hidden_held // chunks
-
-    def by_unit(gate, up):
-        blocks = jnp.stack([gate, up]).reshape(2, held, groups, shards, chunks, piece)
-        return jnp.transpose(blocks, (3, 1, 4, 0, 2, 5)).reshape(shards, held, 2 * hidden_here)
-
-    heads = jnp.stack([by_head(w) for w in (w_query, w_key, w_value)], axis=3)
-    heads = heads.reshape(shards, held, 3 * pairs * PAIR)
-    heads, units = exchange_plane([heads, by_unit(w_gate, w_up)], shards, 1)
-    heads = heads.reshape(shards * held, heads.shape[-1])
-    units = units.reshape(shards * held, units.shape[-1])
-    qkv_weight = lax.all_gather(heads, "dp", axis=0, tiled=True)
-    if whole_heads:
-        out_weight = lax.all_gather(w_out, "dp", axis=0, tiled=True)
-    else:
-        whole = lax.all_gather(w_out, ("dp", "seq"), axis=0, tiled=True)
-        out_weight = lax.dynamic_slice_in_dim(whole, lax.axis_index("seq") * inner, inner, 0)
-    unit_weight = lax.all_gather(units, "dp", axis=0, tiled=True)
-    down_weight = lax.all_gather(w_down, "dp", axis=0, tiled=True)
-
+    gains = jnp.stack([norm1_gain, norm2_gain])
     own_tokens = tokens.reshape(count, width)
     own_cotangent = cotangent.reshape(count, width)
     inputs = own_tokens.astype(f32)
-    own_normed = (inputs * rms_scale(inputs) * gain_one).astype(bf16)
-    normed_split, cot_split = gather_plane([own_normed, own_cotangent], shards, 2)
-    normed_one = flat(normed_split)
-
     cos, sin, starts = rope_tables(doc_ids, shards)
     starts = starts[:, None, :]
     by_row = lambda v: v.reshape(shards, rows, shard_len, v.shape[-1])
-    pre = by_row(dot(normed_one, qkv_weight))
-    rotated, attended, stats = attend(pre, cos, sin, starts)
-    attended = flat(attended)
-    hidden, normed_two = forward_plane(
-        split(dot(attended, out_weight).astype(bf16)), own_tokens, gain_two, 3
-    )
-
-    if shards == 8:
+
+    if fast:
+        (
+            hidden,
+            gain_one,
+            gain_two,
+            rotated,
+            attended,
+            stats,
+            normed_one,
+            cot,
+            normed_two,
+            qkv_weight,
+            out_weight,
+            unit_weight,
+            down_weight,
+        ) = front_plane(
+            groups,
+            own_tokens,
+            own_cotangent,
+            gains,
+            w_query,
+            w_key,
+            w_value,
+            w_out,
+            w_gate,
+            w_up,
+            w_down,
+            (cos, sin, starts),
+            1,
+        )
+        qkv_weight = qkv_weight.reshape(width, -1)
+        out_weight = out_weight.reshape(-1, width)
+        attended, normed_one = flat(attended), flat(normed_one)
         (
             grad_hidden,
             gain_two_term,
             branch,
             out_terms,
             unit_sums,
-            _,
+            down_sums,
             unit_terms,
             down_terms,
             *_,
-        ) = fed = feed_plane(
-            normed_two, cot_split, unit_weight, down_weight, own_cotangent, hidden, gain_two, 4
-        )
-        down_sums = fed[5]
+        ) = feed_plane(
+            normed_two,
+            cot,
+            unit_weight,
+            down_weight,
+            w_down,
+            own_cotangent,
+            hidden,
+            gain_two,
+            2,
+        )
     else:
-        cot = flat(cot_split)
-        normed_two = flat(normed_two)
+        gains = lax.all_gather(gains, both, axis=1, tiled=True).astype(f32)
+        gain_one, gain_two = gains[:1], gains[1:]
+
+        def by_head(w):
+            blocks = w.reshape(held, outer, shards, inner)
+            return jnp.moveaxis(blocks, 2, 0).reshape(shards, held, pairs, PAIR)
+
+        blocks = jnp.stack([w_gate, w_up]).reshape(2, held, groups, shards, hidden_held)
+        units = jnp.transpose(blocks, (3, 1, 0, 2, 4)).reshape(shards, held, 2 * hidden_here)
+        heads = jnp.stack([by_head(w) for w in (w_query, w_key, w_value)], axis=3)
+        heads, units = exchange_plane([heads.reshape(shards, held, -1), units], shards, 1)
+        spread = lambda w: lax.all_gather(w, "dp", axis=0, tiled=True)
+        qkv_weight = spread(heads.reshape(shards * held, -1))
+        unit_weight = spread(units.reshape(shards * held, -1))
+        down_weight = spread(w_down)
+        if whole_heads:
+            out_weight = spread(w_out)
+        else:
+            whole = lax.all_gather(w_out, both, axis=0, tiled=True)
+            out_weight = lax.dynamic_slice_in_dim(whole, lax.axis_index("seq") * inner, inner, 0)
+        own_normed = (inputs * rms_scale(inputs) * gain_one).astype(bf16)
+        normed_one, cot = [flat(v) for v in gather_plane([own_normed, own_cotangent], shards, 2)]
+        pre = by_row(dot(normed_one, qkv_weight))
+        rotated, attended, stats = attend(pre, cos, sin, starts)
+        attended = flat(attended)
+        hidden = inputs + reduce_plane(split(dot(attended, out_weight).astype(bf16)))
+        normed_two = (hidden * rms_scale(hidden) * gain_two).astype(bf16)
+        normed_two = flat(lax.all_gather(normed_two, "seq"))
         gate_weight, up_weight = unit_weight[:, :hidden_here], unit_weight[:, hidden_here:]
         gate_pre, up_pre = dot(normed_two, gate_weight), dot(normed_two, up_weight)
         sigmoid = jax.nn.sigmoid(gate_pre)
@@ -1449,7 +1910,7 @@
     last_terms = split(dot_t(grad_pre, qkv_weight).astype(bf16))
     head_terms = dot(normed_one.T, grad_pre).astype(bf16)
 
-    if shards == 8:
+    if fast:
         (
             grad_tokens,
             out_tokens,
@@ -1474,7 +1935,7 @@
             grad_hidden,
             gain_one,
             gain_two_term,
-            5,
+            3,
         )
         grad_norms = gain_sums[:2, :held]
         down_sums = jnp.concatenate([down_sums, down_last[None]]).reshape(hidden_held, width)

time: 909 us -> 791 us (0.87)
  waiting for transfers between devices: 68.2 us -> 0 us
  Pallas kernels: 628 us -> 683 us
  blocking collectives: 41.1 us -> 0 us
  local copies, waits for them, and re-layouts: 71.1 us -> 43.3 us
  matrix products: 49.6 us -> 29 us
  between operations: 14.4 us -> 1.06 us
    all_gather x4 -> x0, waiting for transfers between devices: 66.3 us -> none  [the longest x1 66.3 us: layer(): unit_weight = lax.all_gather(units, 'dp', axis=0, tiled=True)]
    pallas_call x4 -> x1, Pallas kernels: 217 us -> 273 us  [front_plane(): pl.pallas_call(functools.partial(front_kernel, groups), out_shape=[sds((r...]
    all_gather x1 -> x0, blocking collectives: 41.1 us -> none  [layer(): lax.all_gather(jnp.stack([norm1_gain, norm2_gain]), ('dp', 'seq'), axis=1...]
    dot_general x4 -> x2, matrix products: 38 us -> 17.5 us  [dot(): return jnp.dot(a, b, preferred_element_type=f32)]
    reshape x8 -> x0, local copies, waits for them, and re-layouts: 13.4 us -> none  [the longest x1 7.69 us: by_unit(): jnp.transpose(blocks, (3, 1, 4, 0, 2, 5))]
    another operation x8 -> x0, local copies, waits for them, and re-layouts: 10.9 us -> none  [the longest x4 9.1 us: by_unit(): jnp.stack([gate, up]).reshape(2, held, groups, shards, chunks, piece)]
  transfers between devices with their start and end apart: 4 -> 0, of which waited for: 1 -> 0; matrix products, arithmetic and copies ran while one was open for 3% -> 0% of each run, Pallas kernels for 20% -> 0%
where the time goes in v3:
time: 791 us; the launch traced here: 781 us
  Pallas kernels  683 us (86%)
  local copies, waits for them, and re-layouts  43.3 us (5%)
  matrix products  29 us (4%)
  other arithmetic  24.1 us (3%)
    pallas_call x1, Pallas kernels, front_plane(): pl.pallas_call(functools.partial(front_kernel, groups), out_shape=[sds((r...  273 us
    pallas_call x1, Pallas kernels, feed_plane(): pl.pallas_call(feed_kernel, out_shape=[sds((rows, width), f32), sds((1, w...  208 us
    pallas_call x1, Pallas kernels, tail_plane(): pl.pallas_call(functools.partial(tail_kernel, devices), out_shape=[sds((r...  179 us
    pallas_call x1, Pallas kernels, attend_back(): pl.pallas_call(attend_back_kernel, grid=(rows, pairs), out_shape=jax.Shap...  23.7 us
    convert_element_type x4, local copies, waits for them, and re-layouts, unit_grad(): jnp.transpose(units_back[:, :, :, i], (2, 3, 1, 0, 4)).reshape(held, -1)  22.6 us
    dot_general x2, matrix products, dot(): return jnp.dot(a, b, preferred_element_type=f32)  17.5 us

profile of v3, /device:TPU:0, one launch (start us, length us, event | category | flops | bytes accessed | tf_op | source)
XLA Modules:
  0.0 780.6 jit_solution(17826388331032798978)
XLA Ops:
  5.2 3.7 fusion.3
  9.0 3.0 maximum_bitcast_fusion
  12.0 273.0 %shard_map.203 = (f32[256,2048]{1,0:T(8,128)}, f32[1,2048]{1,0:T(1,128)}, f32[1,2048]{1,0:T(1,128)}, bf16[8,2,128,768]{3,2,1,0:T(8,128)(2,1)}, bf16[8,2,128,256]...) custom-call(bf16[256,2048]{1,0:T(8,128)(2,1)} %bitcast.75, ...), custom_call_target="tpu_custom_call" | custom-call | bytes 700000000 | tf_op jit(solution)/shard_map/pallas_call | solution.py:1720
  284.9 207.7 %shard_map.204 = (f32[256,2048]{1,0:T(8,128)}, f32[1,2048]{1,0:T(1,128)}, bf16[8,256,2048]{2,1,0:T(8,128)(2,1)}, bf16[8,256,2048]{2,1,0:T(8,128)(2,1)}, bf16[3,5...) custom-call(bf16[8,256,2048]{2,1,0:T(8,128)(2,1)} %get-tuple-element, ...), custom_call_target="tpu_custom_call" | custom-call | bytes 560000000 | tf_op jit(solution)/shard_map/pallas_call | solution.py:958
  492.7 6.8 convolution_convert_fusion.2
  499.6 2.4 convolution_convert_fusion.3
  502.1 23.7 %shard_map.205 = bf16[8,2,128,768]{3,2,1,0:T(8,128)(2,1)} custom-call(bf16[8,2,128,768]{3,2,1,0:T(8,128)(2,1)} %get-tuple-element.39.rotated, bf16[8,2,128,256]{3,2,1,0:T(8,128)(2,1)S(1)} %bitcast.71, f32[8,2,128,128]{3,2,1,0:T(8,128)S(1)} %copy-done, f32[8,2,128,128]{3,2,1,0:T(8,128)S(1)} %copy-done.1, s32[2,1,1024]{2,1,0:T(1,128)S(1)} %bitcast.70, ...), custom_call_target="tpu_custom_call" | custom-call | flops 10737418240 | bytes 9437184 | tf_op jit(solution)/shard_map/pallas_call | solution.py:461
  525.8 10.7 %convolution_convert_fusion.1 = bf16[2048,768]{1,0:T(8,128)(2,1)} fusion(bf16[2048,2048]{1,0:T(8,128)(2,1)S(1)} %bitcast.95, bf16[2048,768]{1,0:T(8,128)(2,1)} %bitcast.98), kind=kOutput, calls=%fused_computation.3 | convolution fusion | flops 6444023808 | bytes 14680064 | tf_op jit(solution)/shard_map/dot_general | solution.py:325
  536.5 9.0 %convolution_convert_fusion = bf16[2048,2048]{1,0:T(8,128)(2,1)} fusion(bf16[2048,768]{1,0:T(8,128)(2,1)S(1)} %bitcast.99, bf16[2048,768]{1,0:T(8,128)(2,1)S(1)} %bitcast.96), kind=kOutput, calls=%fused_computation | convolution fusion | flops 6446645248 | bytes 14680064 | tf_op jit(solution)/shard_map/dot_general | solution.py:321
  545.5 178.8 %shard_map.206 = (bf16[256,2048]{1,0:T(8,128)(2,1)}, bf16[256,2048]{1,0:T(8,128)(2,1)}, f32[8,128]{1,0:T(8,128)}, bf16[64,2048]{1,0:T(8,128)(2,1)}, bf16[64,2048...) custom-call(bf16[8,256,2048]{2,1,0:T(8,128)(2,1)} %bitcast.74, ...), custom_call_target="tpu_custom_call" | custom-call | bytes 420000000 | tf_op jit(solution)/shard_map/pallas_call | solution.py:1244
  724.3 1.3 slice_bitcast_fusion.2
  725.6 1.0 pad_maximum_fusion
  726.6 1.8 convert_element_type.118
  728.4 1.6 bitcast_convert_fusion
  730.4 5.1 fusion
  736.9 1.2 reshape.203
  739.5 1.2 reshape.202
  742.1 1.2 reshape.201
  743.3 7.7 reshape.199
  751.0 4.8 convert_bitcast_fusion
  755.8 4.7 copy.34
  760.5 5.5 reshape.205
  766.0 6.9 copy.33
  772.8 5.6 reshape.204
  (53 shorter events, 11.2 us)
Async XLA Ops:
  284.9 207.8 %copy-start.5 = (bf16[8,2,128,256]{3,2,1,0:T(8,128)(2,1)S(1)}, bf16[8,2,128,256]{3,2,1,0:T(8,128)(2,1)}, u32[]{:S(2)}) copy-start(bf16[8,2,128,256]{3,2,1,0:T(8,128)(2,1)} %get-tuple-element.54) | copy-start | bytes 3145732
  492.7 6.9 copy-start.4
  492.7 6.9 copy-start.11
  499.6 2.4 copy-start
  499.6 2.5 copy-start.1
  499.6 2.5 copy-start.2
  499.6 2.5 copy-start.3
  499.6 26.2 %slice-start = ((s8[8388608]{0:T(1024)(128)(4,1)}), s8[4194304]{0:T(1024)(128)(4,1)S(1)}, s32[]{:S(2)}) async-start(s8[8388608]{0:T(1024)(128)(4,1)} %bitcast.93), calls=%async_computation | async-start | bytes 8388608
  502.1 23.7 %slice-start.1 = ((s8[8388608]{0:T(1024)(128)(4,1)}), s8[4194304]{0:T(1024)(128)(4,1)S(1)}, s32[]{:S(2)}) async-start(s8[8388608]{0:T(1024)(128)(4,1)} %bitcast.93), calls=%async_computation.1 | async-start | bytes 8388608
  525.8 10.7 %copy-start.10 = (bf16[4,512,768]{2,1,0:T(8,128)(2,1)S(1)}, bf16[4,512,768]{2,1,0:T(8,128)(2,1)}, u32[]{:S(2)}) copy-start(bf16[4,512,768]{2,1,0:T(8,128)(2,1)} %get-tuple-element.49) | copy-start | bytes 9437188
  525.8 10.7 %copy-start.12 = (bf16[8,2,128,768]{3,2,1,0:T(8,128)(2,1)S(1)}, bf16[8,2,128,768]{3,2,1,0:T(8,128)(2,1)}, u32[]{:S(2)}) copy-start(bf16[8,2,128,768]{3,2,1,0:T(8,128)(2,1)} %shard_map.205) | copy-start | bytes 9437188
  545.5 180.1 %copy-start.9 = (bf16[3,64,2048]{2,1,0:T(8,128)(2,1)S(1)}, bf16[3,64,2048]{2,1,0:T(8,128)(2,1)}, u32[]{:S(2)}) copy-start(bf16[3,64,2048]{2,1,0:T(8,128)(2,1)} %get-tuple-element.65) | copy-start | bytes 2359300
  724.3 5.7 copy-start.8
  772.8 5.6 copy-start.7
  772.8 6.6 copy-start.6

commit v4 on v3

--- a/solution.py
+++ b/solution.py
@@ -87,7 +87,7 @@
     return copy
 
 
-def gather_forward(p, sent, out, send, recv, base):
+def gather_forward(p, sent, out, send, recv, base, halfway=None):
     quarter = out.shape[1] // 4
     part = lambda owner, k: out.at[p[owner], pl.ds(k * quarter, quarter)]
     passed = []
@@ -101,6 +101,8 @@
         if j < 2:
             sent["far", ky] = gather_pass(p, part("yp", ky), send, recv, base + 9 + ky, "xp")
         passed.append(gather_pass(p, part("yp", ky), send, recv, base + 17 + ky, "sib"))
+        if j == 1 and halfway is not None:
+            halfway()
 
     def last():
         for k in (0, 2, 1, 3):
@@ -235,55 +237,80 @@
 ORDER = ((3, "dg", "ds"), (1, "xp", "xs"), (2, "yp", "ys"), (0, "me", "sib"))
 
 
-def scatter_plane(p, source, rows, kept, paired, far, final, send, recv, meanwhile=None):
-    half = rows // 2
-    low, high = pl.ds(0, half), pl.ds(half, half)
-    sends = []
-
-    def add_pair(i):
-        source.ready(i)
+class PlaneSum:
+    def __init__(self, p, source, rows, kept, paired, far, final, send, recv):
+        self.p, self.source, self.rows = p, source, rows
+        self.kept, self.paired, self.far, self.final = kept, paired, far, final
+        self.send, self.recv = send, recv
+        self.half = rows // 2
+        self.low, self.high = pl.ds(0, self.half), pl.ds(self.half, self.half)
+        self.sends, self.near = [], []
+
+    def add_pair(self, i):
+        kept, paired = self.kept, self.paired
+        self.source.ready(i)
 
         def step(at):
             kept[i, at, :] = (kept[i, at, :].astype(f32) + paired[i, at, :].astype(f32)).astype(
                 bf16
             )
 
-        over_rows(rows, step)
-
-    def put(src, dst, i, to):
-        copy = remote(p, src, dst, send, recv, i, to)
+        over_rows(self.rows, step)
+
+    def put(self, src, dst, i, to):
+        copy = remote(self.p, src, dst, self.send, self.recv, i, to)
         copy.start()
-        sends.append(copy)
+        self.sends.append(copy)
         return copy
 
-    add_pair(3)
-    far_x = put(kept.at[3, low], far.at[0], 4, "xp")
-    far_y = put(kept.at[3, high], far.at[1], 5, "yp")
-    add_pair(1)
-    near = [put(kept.at[1, low], final.at[0, low], 6, "xp")]
-    add_pair(2)
-    near.append(put(kept.at[2, high], final.at[1, high], 7, "yp"))
-    far_x.wait_recv()
-
-    def step_x(at):
-        kept[2, at, :] = (kept[2, at, :].astype(f32) + far[0, at, :].astype(f32)).astype(bf16)
-
-    over_rows(half, step_x)
-    near.append(put(kept.at[2, low], final.at[1, low], 8, "yp"))
-    far_y.wait_recv()
-
-    def step_y(at):
-        up = pl.ds(pl.multiple_of(at.start + half, BLOCK), BLOCK)
-        kept[1, up, :] = (kept[1, up, :].astype(f32) + far[1, at, :].astype(f32)).astype(bf16)
-
-    over_rows(half, step_y)
-    near.append(put(kept.at[1, high], final.at[0, high], 9, "xp"))
-    source.ready(0)
+    def first(self):
+        kept, far, final, low, high = self.kept, self.far, self.final, self.low, self.high
+        self.add_pair(3)
+        self.far_x = self.put(kept.at[3, low], far.at[0], 4, "xp")
+        self.far_y = self.put(kept.at[3, high], far.at[1], 5, "yp")
+        self.add_pair(1)
+        self.near.append(self.put(kept.at[1, low], final.at[0, low], 6, "xp"))
+        self.add_pair(2)
+        self.near.append(self.put(kept.at[2, high], final.at[1, high], 7, "yp"))
+
+    def second(self):
+        kept, far, final, low, high = self.kept, self.far, self.final, self.low, self.high
+        half = self.half
+        self.far_x.wait_recv()
+
+        def step_x(at):
+            kept[2, at, :] = (kept[2, at, :].astype(f32) + far[0, at, :].astype(f32)).astype(bf16)
+
+        over_rows(half, step_x)
+        self.near.append(self.put(kept.at[2, low], final.at[1, low], 8, "yp"))
+        self.far_y.wait_recv()
+
+        def step_y(at):
+            up = pl.ds(pl.multiple_of(at.start + half, BLOCK), BLOCK)
+            kept[1, up, :] = (kept[1, up, :].astype(f32) + far[1, at, :].astype(f32)).astype(bf16)
+
+        over_rows(half, step_y)
+        self.near.append(self.put(kept.at[1, high], final.at[0, high], 9, "xp"))
+        self.source.ready(0)
+
+    def third(self):
+        for copy in self.near:
+            copy.wait_recv()
+
+    def finish(self):
+        self.source.finish()
+        for copy in self.sends:
+            copy.wait_send()
+
+
+def scatter_plane(p, source, rows, kept, paired, far, final, send, recv, meanwhile=None):
+    sums = PlaneSum(p, source, rows, kept, paired, far, final, send, recv)
+    sums.first()
+    sums.second()
     if meanwhile is not None:
         meanwhile()
-    for copy in near:
-        copy.wait_recv()
-    return sends
+    sums.third()
+    return sums
 
 
 def total(kept, paired, final, at):
@@ -323,6 +350,10 @@
 
 def dot(a, b):
     return jnp.dot(a, b, preferred_element_type=f32)
+
+
+def dot_l(a, b):
+    return lax.dot_general(a, b, (((0,), (0,)), ((), ())), preferred_element_type=f32)
 
 
 def allowed_pairs(start, keys, queries, offset):
@@ -404,14 +435,14 @@
     )(pre, cos, sin, starts)
 
 
-def attend_back_kernel(rotated, grad, cos, sin, starts, stats, result, key_acc, value_acc):
+def attend_back_pair(rotated, grad, cos, sin, starts, stats, result, key_acc, value_acc, r, pair):
     shards, _, shard_len, _ = rotated.shape
     length = shards * shard_len
     block = min(256, length)
     per = block // shard_len
-    all_in = rotated[...].reshape(length, 3 * PAIR)
-    query, key, value = all_in[:, :PAIR], all_in[:, PAIR : 2 * PAIR], all_in[:, 2 * PAIR :]
-    grad_all = grad[...].reshape(length, PAIR)
+    lanes = lambda i: pl.ds(pl.multiple_of((pair * 3 + i) * PAIR, PAIR), PAIR)
+    query, key, value = (rotated[:, r, :, lanes(i)].reshape(length, PAIR) for i in range(3))
+    grad_all = grad[:, r, :, pl.ds(pl.multiple_of(pair * PAIR, PAIR), PAIR)].reshape(length, PAIR)
     key_t = key.astype(f32).T.astype(bf16)
     left = lax.broadcasted_iota(jnp.int32, (block, PAIR), 1) < HD
     top = lax.broadcasted_iota(jnp.int32, (PAIR, block), 0) < HD
@@ -422,15 +453,15 @@
     for i in range(length // block):
         keys = (i + 1) * block
         at = slice(i * block, (i + 1) * block)
-        start = starts[0, :, at]
-        mask = allowed_pairs(start, keys, block, i * block)
+        here = slice(i * per, (i + 1) * per)
+        mask = allowed_pairs(starts[:, at], keys, block, i * block)
         results = []
         for h in range(2):
             side = left if h == 0 else ~left
             own = jnp.where(side, query[at], jnp.zeros_like(query[at]))
             own_grad = jnp.where(side, grad_all[at], jnp.zeros_like(grad_all[at]))
             scores = dot_t(key[:keys], own * jnp.asarray(0.125, bf16))
-            probs = jnp.exp(jnp.where(mask, scores - stats[0, 0, h : h + 1, at], -1e30))
+            probs = jnp.exp(jnp.where(mask, scores - stats[r, pair, h : h + 1, at], -1e30))
             grad_probs = dot_t(value[:keys], own_grad)
             inner = jnp.sum(probs * grad_probs, axis=0, keepdims=True)
             grad_scores = (probs * (grad_probs - inner) * 0.125).astype(bf16)
@@ -438,17 +469,20 @@
             value_acc[:keys, :] += dot(probs.astype(bf16), own_grad)
             results.append(dot(key_t[:, :keys], grad_scores))
         merged = jnp.where(top, results[0], results[1]).T
-        cos_here = cos[i * per : (i + 1) * per].reshape(block, PAIR)
-        sin_here = sin[i * per : (i + 1) * per].reshape(block, PAIR)
+        cos_here, sin_here = cos[here, r].reshape(block, PAIR), sin[here, r].reshape(block, PAIR)
         turned = merged * cos_here - swap_halves(merged, first[:block]) * sin_here
-        result[i * per : (i + 1) * per, 0, :, :PAIR] = turned.astype(bf16).reshape(
-            per, shard_len, PAIR
-        )
-    cos_all, sin_all = cos[...].reshape(length, PAIR), sin[...].reshape(length, PAIR)
+        result[here, r, :, lanes(0)] = turned.astype(bf16).reshape(per, shard_len, PAIR)
+    cos_all, sin_all = cos[:, r].reshape(length, PAIR), sin[:, r].reshape(length, PAIR)
     key_grad = key_acc[...]
     turned = key_grad * cos_all - swap_halves(key_grad, first) * sin_all
-    result[:, 0, :, PAIR : 2 * PAIR] = turned.astype(bf16).reshape(shards, shard_len, PAIR)
-    result[:, 0, :, 2 * PAIR :] = value_acc[...].astype(bf16).reshape(shards, shard_len, PAIR)
+    result[:, r, :, lanes(1)] = turned.astype(bf16).reshape(shards, shard_len, PAIR)
+    result[:, r, :, lanes(2)] = value_acc[...].astype(bf16).reshape(shards, shard_len, PAIR)
+
+
+def attend_back_kernel(rotated, grad, cos, sin, starts, stats, result, key_acc, value_acc):
+    attend_back_pair(
+        rotated, grad, cos, sin, starts[0], stats, result, key_acc, value_acc, 0, 0
+    )
 
 
 def attend_back(rotated, grad, cos, sin, starts, stats):
@@ -634,15 +668,15 @@
     d,
     unit_stage,
     act_stage,
-    unit_t,
-    act_t,
+    unit_kept,
+    act_kept,
     unit_grad,
     down_grad,
     unit_acc,
     down_acc,
     unit_parts,
     down_parts,
-    turned,
+    stage,
     kept,
     paired,
     far,
@@ -699,6 +733,9 @@
     def move(src, dst, i):
         return pltpu.make_async_copy(src, dst, local.at[i])
 
+    def shard_rows(s, count=1):
+        return pl.ds(pl.multiple_of(s * rows, rows), count * rows)
+
     def chunk_loads(j):
         return (
             move(all_units(j), w.at[j % 2], w_sem + j % 2),
@@ -711,8 +748,8 @@
 
     start_chunk(0)
     for s in range(shards):
-        move(normed.at[s], x.at[s], x_sem + s).start()
-        move(cot.at[s], c.at[s], c_sem + s).start()
+        move(normed.at[s], x.at[shard_rows(s)], x_sem + s).start()
+        move(cot.at[s], c.at[shard_rows(s)], c_sem + s).start()
     pl.semaphore_wait(barrier, len(others))
     for gather in late:
         gather.start()
@@ -723,7 +760,7 @@
             LineSum(
                 p,
                 lambda owner, j=j: unit_terms.at[
-                    j, :, pl.ds(pl.multiple_of(owner * chunk, chunk), chunk)
+                    j, pl.ds(pl.multiple_of(owner * chunk, chunk), chunk)
                 ],
                 unit_land.at[j],
                 zsend,
@@ -746,7 +783,7 @@
         line[j][0].second(unit_acc.at[j], unit_parts.at[0], local, z_sem)
         line[j][1].second(down_acc.at[j], down_parts.at[0], local, z_sem + 2)
 
-    for j in range(CHUNKS):
+    def work(j):
         slot = j % 2
         if j == EARLY:
             for gather in late:
@@ -757,73 +794,74 @@
         if j + 1 < EARLY:
             start_chunk(j + 1)
         if j > 0:
-            move(unit_stage, kept_units.at[:, :, pl.ds(0, chunk)], us_sem).wait()
-            move(act_stage, kept_acts.at[:, :, pl.ds(0, part)], as_sem).wait()
-
-        @pl.loop(0, shards)
+            keep(j - 1, "wait")
+
+        @pl.loop(0, shards, step=2)
         def _(s):
+            both = shard_rows(s, 2)
             if j == 0:
-                move(normed.at[s], x.at[s], x_sem + s).wait()
-                move(cot.at[s], c.at[s], c_sem + s).wait()
-            pre = dot(x[s], w[slot].reshape(shards * rows, chunk))
-            grad_act = dot_t(c[s], d[slot].reshape(part, width))
+                for k in range(2):
+                    move(normed.at[s + k], x.at[shard_rows(s + k)], x_sem + s + k).wait()
+                    move(cot.at[s + k], c.at[shard_rows(s + k)], c_sem + s + k).wait()
+            pre = dot(x[both], w[slot].reshape(width, chunk))
+            grad_act = dot_t(c[both], d[slot].reshape(part, width))
             gate, up = pre[:, :part], pre[:, part:]
             sigmoid = 1.0 / (1.0 + jnp.exp(-gate))
             silu = gate * sigmoid
-            act = (silu * up).astype(bf16).astype(f32)
-            grad_gate = (grad_act * up * sigmoid * (1.0 + gate * (1.0 - sigmoid))).astype(bf16)
-            grad_up = (grad_act * silu).astype(bf16)
-            at = pl.ds(pl.multiple_of(s * rows, rows), rows)
-            act_stage[s] = act.astype(bf16)
-            unit_stage[s, :, :part] = grad_gate
-            unit_stage[s, :, part:] = grad_up
-            act_t[:, at] = act.T.astype(bf16)
-            unit_t[:part, at] = grad_gate.astype(f32).T.astype(bf16)
-            unit_t[part:, at] = grad_up.astype(f32).T.astype(bf16)
-
-        move(unit_stage, kept_units.at[:, :, pl.ds(j * chunk, chunk)], us_sem).start()
-        move(act_stage, kept_acts.at[:, :, pl.ds(j * part, part)], as_sem).start()
-
-        @pl.loop(0, width // 256)
+            act_stage[both] = (silu * up).astype(bf16)
+            unit_stage[both, :part] = (
+                grad_act * up * sigmoid * (1.0 + gate * (1.0 - sigmoid))
+            ).astype(bf16)
+            unit_stage[both, part:] = (grad_act * silu).astype(bf16)
+
+        keep(j, "start")
+
+    def keep(j, what):
+        getattr(move(unit_stage, kept_units.at[:, pl.ds(j * chunk, chunk)], us_sem), what)()
+        getattr(move(act_stage, kept_acts.at[:, pl.ds(j * part, part)], as_sem), what)()
+
+    def weigh(j, units_now, acts_now):
+        @pl.loop(0, width // 512)
         def _(n):
-            at = pl.ds(pl.multiple_of(n * 256, 256), 256)
-            unit_grad[:, at] = dot(unit_t[...], x[:, :, at].reshape(shards * rows, 256)).astype(
-                bf16
-            )
-            down_grad[:, at] = dot(act_t[...], c[:, :, at].reshape(shards * rows, 256)).astype(
-                bf16
-            )
-
-        keep_unit = move(unit_grad, unit_terms.at[j], ug_sem)
-        keep_down = move(down_grad, down_terms.at[j], dg_sem)
-        keep_unit.start()
-        keep_down.start()
-        keep_unit.wait()
-        keep_down.wait()
+            at = pl.ds(pl.multiple_of(n * 512, 512), 512)
+            unit_grad[at] = dot_l(x[:, at], units_now[...]).astype(bf16)
+            down_grad[:, at] = dot_l(acts_now[...], c[:, at]).astype(bf16)
+
+        store = [
+            move(unit_grad, unit_terms.at[j], ug_sem),
+            move(down_grad, down_terms.at[j], dg_sem),
+        ]
+        for copy in store:
+            copy.start()
+        for copy in store:
+            copy.wait()
+        if j < EARLY:
+            for sums in line[j]:
+                sums.first()
+
+    for j in range(CHUNKS):
+        work(j)
+        weigh(j, unit_stage, act_stage)
         for gather in late:
             if j == 0:
                 gather.second()
             if j == 1:
                 gather.third()
-        if j < EARLY:
-            for sums in line[j]:
-                sums.first()
         if j >= 2:
             pass_on(j - 2)
-    move(unit_stage, kept_units.at[:, :, pl.ds(0, chunk)], us_sem).wait()
-    move(act_stage, kept_acts.at[:, :, pl.ds(0, part)], as_sem).wait()
+    keep(CHUNKS - 1, "wait")
 
     load_w = [
         move(
             all_units(j).at[k // 2, pl.ds(k % 2 * rows, rows)],
-            x.at[k, :, pl.ds(j * chunk, chunk)],
+            x.at[shard_rows(k), pl.ds(j * chunk, chunk)],
             last_w + 8 * j + k,
         )
         for j in range(CHUNKS)
         for k in range(shards)
     ]
     load_d = [
-        move(all_down(j).at[k], c.at[j, pl.ds(k * piece, piece)], last_d + 4 * j + k)
+        move(all_down(j).at[k], c.at[pl.ds(j * part + k * piece, piece)], last_d + 4 * j + k)
         for j in range(CHUNKS)
         for k in range(4)
     ]
@@ -834,7 +872,9 @@
 
     def load_kept(k):
         return move(
-            kept_units.at[p[order[k]]], unit_t.at[pl.ds(k % 2 * rows, rows)], ub_sem + k % 2
+            kept_units.at[shard_rows(p[order[k]])],
+            unit_kept.at[pl.ds(k % 2 * rows, rows)],
+            ub_sem + k % 2,
         )
 
     load_kept(0).start()
@@ -848,23 +888,25 @@
             for load in load_w:
                 load.wait()
 
-        @pl.loop(0, shards)
+        @pl.loop(0, width // 1024)
         def _(n):
-            at = pl.ds(pl.multiple_of(n * rows, rows), rows)
-            out[:, at] = dot_t(unit_t[k % 2 * rows : (k % 2 + 1) * rows], x[n]).astype(bf16)
+            at = pl.ds(pl.multiple_of(n * 1024, 1024), 1024)
+            out[:, at] = dot_t(unit_kept[k % 2 * rows : (k % 2 + 1) * rows], x[at]).astype(bf16)
 
     def act_load(s):
         slot = lax.rem(s, 2)
-        half = pl.multiple_of(slot * (width // 2), width // 2)
-        return move(kept_acts.at[s], act_t.at[:, pl.ds(half, width // 2)], ab_sem + slot)
+        return move(kept_acts.at[shard_rows(s)], act_kept.at[slot], ab_sem + slot)
 
     def out_store(s):
         slot = lax.rem(s, 2)
-        at = pl.ds(pl.multiple_of(slot * rows, rows), rows)
-        return move(unit_grad.at[at], out_terms.at[s], out_sem + slot)
+        return move(unit_grad_rows(slot), out_terms.at[s], out_sem + slot)
+
+    def unit_grad_rows(slot):
+        return stage.at[shard_rows(slot)]
 
     def forward_terms():
         source.finish()
+        source.pairs.clear()
         for load in load_d:
             load.wait()
         act_load(0).start()
@@ -882,16 +924,12 @@
                 out_store(s - 2).wait()
 
             slot = lax.rem(s, 2)
-            to = pl.ds(pl.multiple_of(slot * rows, rows), rows)
-
-            @pl.loop(0, width // 256)
+            acts = act_kept[slot]
+
+            @pl.loop(0, width // 1024)
             def _(n):
-                at = pl.ds(pl.multiple_of(n * 256, 256), 256)
-                summed = jnp.zeros((rows, 256), f32)
-                for j in range(CHUNKS):
-                    base = pl.multiple_of(slot * (width // 2) + j * part, part)
-                    summed = summed + dot(act_t[:, pl.ds(base, part)], c[j, :, at])
-                unit_grad[to, at] = summed.astype(bf16)
+                at = pl.ds(pl.multiple_of(n * 1024, 1024), 1024)
+                stage[shard_rows(slot), at] = dot(acts, c[: acts.shape[1], at]).astype(bf16)
 
             out_store(s).start()
 
@@ -899,7 +937,7 @@
         out_store(shards - 1).wait()
         pass_on(2)
 
-    source = Produced(p, produce, unit_grad, kept, paired, send, recv)
+    source = Produced(p, produce, stage, kept, paired, send, recv)
     sends = scatter_plane(
         p, source, rows, kept, paired, far, final, send, recv, meanwhile=forward_terms
     )
@@ -923,14 +961,8 @@
 
     def sum_up(j):
         line[j][0].total(unit_parts, local, z_sem)
-
-        @pl.loop(0, chunk // 128)
-        def _(n):
-            at = pl.ds(pl.multiple_of(n * 128, 128), 128)
-            turned[:, at] = unit_parts[0, at, :].astype(f32).T.astype(bf16)
-
         line[j][1].total(down_parts, local, z_sem + 4)
-        out = [move(turned, unit_sums.at[j], turn_sem), move(down_parts.at[0], down_sums.at[j], turn_sem + 1)]
+        out = [move(unit_parts.at[0], unit_sums.at[j], turn_sem), move(down_parts.at[0], down_sums.at[j], turn_sem + 1)]
         for copy in out:
             copy.start()
         for copy in out:
@@ -944,8 +976,7 @@
     for j in range(EARLY):
         for sums in line[j]:
             sums.finish()
-    for copy in sends:
-        copy.wait_send()
+    sends.finish()
 
 
 def feed_plane(normed, cot, units, down, w_down, own_cot, hidden, gain, collective_id):
@@ -964,10 +995,10 @@
             sds((shards, rows, width), bf16),
             sds((EARLY, chunk, chunk), bf16),
             sds((EARLY, piece, width), bf16),
-            sds((CHUNKS, chunk, width), bf16),
+            sds((CHUNKS, width, chunk), bf16),
             sds((CHUNKS, part, width), bf16),
-            sds((shards, rows, wide), bf16),
-            sds((shards, rows, wide // 2), bf16),
+            sds((shards * rows, wide), bf16),
+            sds((shards * rows, wide // 2), bf16),
             sds((EARLY, 4, chunk, chunk), bf16),
             sds((EARLY, 4, piece, width), bf16),
             sds((4, width // 4, chunk), bf16),
@@ -976,21 +1007,21 @@
         in_specs=[ANY] * 5 + [VMEM] * 3,
         out_specs=[VMEM, VMEM] + [ANY] * 12,
         scratch_shapes=[
-            pltpu.VMEM((shards, rows, width), bf16),
-            pltpu.VMEM((shards, rows, width), bf16),
+            pltpu.VMEM((shards * rows, width), bf16),
+            pltpu.VMEM((shards * rows, width), bf16),
             pltpu.VMEM((2, 4, width // 4, chunk), bf16),
             pltpu.VMEM((2, 4, piece, width), bf16),
-            pltpu.VMEM((shards, rows, chunk), bf16),
-            pltpu.VMEM((shards, rows, part), bf16),
-            pltpu.VMEM((chunk, shards * rows), bf16),
-            pltpu.VMEM((part, shards * rows), bf16),
-            pltpu.VMEM((chunk, width), bf16),
+            pltpu.VMEM((shards * rows, chunk), bf16),
+            pltpu.VMEM((shards * rows, part), bf16),
+            pltpu.VMEM((2 * rows, wide), bf16),
+            pltpu.VMEM((2, rows, wide // 2), bf16),
+            pltpu.VMEM((width, chunk), bf16),
             pltpu.VMEM((part, width), bf16),
             pltpu.VMEM((EARLY, chunk, chunk), bf16),
             pltpu.VMEM((EARLY, piece, width), bf16),
             pltpu.VMEM((4, chunk, chunk), bf16),
             pltpu.VMEM((4, piece, width), bf16),
-            pltpu.VMEM((chunk, chunk), bf16),
+            pltpu.VMEM((2 * rows, width), bf16),
         ]
         + scatter_scratch(rows, width)[:6]
         + [
@@ -1020,31 +1051,56 @@
 
 def tail_kernel(
     devices,
-    terms,
+    branch,
+    normed_one,
+    rotated_in,
     out_terms,
     unit_terms,
     down_terms,
-    head_terms,
-    wo_terms,
     unit_sums,
-    tokens,
+    down_sums,
     hidden,
     grad_hidden,
+    qkv,
+    out_weight,
+    attended,
+    stats,
+    cos,
+    sin,
+    starts,
+    tokens,
     gain,
     gain_two_term,
     grad_tokens,
     out_tokens,
     gain_sums,
-    down_sum,
-    wo_sum,
-    units_out,
-    heads_out,
+    grad_query,
+    grad_key,
+    grad_value,
+    grad_out,
+    grad_gate,
+    grad_up,
+    grad_down,
+    head_terms,
+    wo_terms,
     unit_sum,
     head_sum,
     unit_land,
     down_land,
     head_land,
     wo_land,
+    x,
+    rotated,
+    grads,
+    key_acc,
+    value_acc,
+    head_grad,
+    wo_grad,
+    residual,
+    units,
+    heads,
+    wide_out,
+    row_out,
     gain_one_term,
     gain_mine,
     gain_land,
@@ -1052,75 +1108,192 @@
     down_acc,
     head_acc,
     wo_acc,
-    unit_parts,
-    down_parts,
-    head_parts,
-    turned,
+    parts,
+    row_parts,
+    stage,
     zsend,
     zrecv,
     esend,
     erecv,
     gsend,
     grecv,
+    ready,
     local,
-    *scratch,
+    kept,
+    paired,
+    far,
+    final,
+    send,
+    recv,
+    loads,
 ):
     p = plane()
-    names = ("dg", "ds", "xp", "yp", "xs", "ys", "sib")
+    other, met = meet_all(p, devices)
     mine = p["dp"] * 8 + p["me"]
-    barrier = pltpu.get_barrier_semaphore()
-
-    def other(k):
-        to = lax.rem(mine + k, devices)
-        return dict(device_id=(lax.div(to, 8), lax.rem(to, 8)), device_id_type=MESH), to
-
-    @pl.loop(1, devices)
-    def _(k):
-        pl.semaphore_signal(barrier, inc=1, **other(k)[0])
-
-    pl.semaphore_wait(barrier, devices - 1)
-    chunk = unit_terms.shape[1]
+    sems = Local(local)
+    rows, width = tokens.shape
+    shards, batch, shard_len, wide = rotated.shape
+    pairs = wide // (3 * PAIR)
+    chunk = unit_terms.shape[2]
     piece = down_terms.shape[1] // 4
-    rows = tokens.shape[0]
-    held = units_out.shape[2]
-    line = [
-        LineSum(p, lambda owner: head_terms.at[owner], head_land, zsend, zrecv, 0),
-        LineSum(
-            p,
-            lambda owner: unit_terms.at[
-                EARLY, :, pl.ds(pl.multiple_of(owner * chunk, chunk), chunk)
-            ],
-            unit_land,
-            zsend,
-            zrecv,
-            4,
-        ),
-        LineSum(
-            p,
-            lambda owner: down_terms.at[EARLY, pl.ds(pl.multiple_of(owner * piece, piece), piece)],
-            down_land,
-            zsend,
-            zrecv,
-            8,
-        ),
-        LineSum(p, lambda owner: wo_terms.at[owner], wo_land, zsend, zrecv, 12),
-    ]
-    for sums in line:
-        sums.first_far()
-    for sums in line:
-        sums.first_rest()
-    kept, paired, far, final, send, recv, loads = scratch[:7]
-    source = FromMemory(p, terms, kept, paired, send, recv, loads)
-    copies = []
+    span = unit_land.shape[1]
+    held = units.shape[2]
+    late = unit_terms.shape[0] - 1
+    z_sem = sems.take(4)
+
+    def move(src, dst, i=None):
+        return pltpu.make_async_copy(src, dst, local.at[sems.take() if i is None else i])
+
+    def shard_rows(s):
+        return pl.ds(pl.multiple_of(s * rows, rows), rows)
+
+    x_loads = [move(branch.at[s], x.at[pl.ds(s * rows, rows)]) for s in range(shards)]
+    load_rotated = move(rotated_in, rotated)
+    load_hidden = move(hidden, residual)
+    for load in x_loads + [load_rotated, load_hidden]:
+        load.start()
+
+    def of_owner(ref, count):
+        return lambda owner: ref.at[pl.ds(pl.multiple_of(owner * count, count), count)]
+
+    unit_line = LineSum(p, of_owner(unit_terms.at[late], span), unit_land, zsend, zrecv, 0)
+    down_line = LineSum(p, of_owner(down_terms.at[late], piece), down_land, zsend, zrecv, 4)
+    head_line = LineSum(p, of_owner(head_terms, span), head_land, zsend, zrecv, 8)
+    wo_line = LineSum(p, of_owner(wo_terms, held), wo_land, zsend, zrecv, 12)
+    met()
+    unit_line.first()
+    down_line.first()
+    out_source = FromMemory(p, out_terms, kept, paired, send, recv, loads)
+    out_sum = PlaneSum(p, out_source, rows, kept, paired, far, final, send, recv)
+    exchanged = {}
 
     def exchange(i, block, out):
-        for j, name in enumerate(names):
-            copies.append(remote(p, block(p[name]), out, esend, erecv, i * 7 + j, name))
-            copies[-1].start()
-        copies.append(pltpu.make_async_copy(block(p["me"]), out, local.at[i]))
-        copies[-1].start()
-
-    sends = scatter_plane(p, source, rows, kept, paired, far, final, send, recv)
+        copies = [
+            remote(p, block(p[name]), out, esend, erecv, i * 7 + j, name)
+            for j, name in enumerate(OTHERS)
+        ]
+        copies.append(move(block(p["me"]), out))
+        for copy in copies:
+            copy.start()
+        exchanged[i] = copies
+
+    def exchange_units(j, source):
+        exchange(j, of_owner(source, held), units.at[j, p["me"]])
+
+    for load in x_loads:
+        load.wait()
+
+    @pl.loop(0, shards, step=2)
+    def _(s):
+        at = pl.ds(pl.multiple_of(s * rows, rows), 2 * rows)
+        grad = dot_t(x[at], out_weight[...].reshape(-1, width)).astype(bf16)
+        grads[pl.ds(s, 2)] = grad.reshape((2,) + grads.shape[1:])
+
+    out_sum.first()
+
+    @pl.loop(0, width // 512)
+    def _(n):
+        at = pl.ds(pl.multiple_of(n * 512, 512), 512)
+        acts = attended[...].reshape(shards * rows, -1)
+        wo_grad[:, at] = dot_l(acts, x[:, at]).astype(bf16)
+
+    store_wo = move(wo_grad, wo_terms)
+    store_wo.start()
+    n1_loads = [move(normed_one.at[s], x.at[pl.ds(s * rows, rows)]) for s in range(shards)]
+    for load in n1_loads:
+        load.start()
+    store_wo.wait()
+    wo_line.first()
+    load_rotated.wait()
+
+    def attention(r):
+        @pl.loop(0, pairs)
+        def _(pair):
+            attend_back_pair(
+                rotated,
+                grads,
+                cos,
+                sin,
+                starts[r],
+                stats,
+                rotated,
+                key_acc,
+                value_acc,
+                r,
+                pair,
+            )
+
+    attention(0)
+    out_sum.second()
+    unit_line.second(unit_acc, parts.at[0, :, pl.ds(0, chunk)], local, z_sem)
+    down_line.second(down_acc, row_parts.at[0], local, z_sem)
+    for j in range(late):
+        exchange_units(j, unit_sums.at[j])
+    attention(1)
+    for load in n1_loads:
+        load.wait()
+    out_sum.third()
+    load_hidden.wait()
+
+    def step_out(at):
+        out_tokens[at, :] = (residual[at, :] + total(kept, paired, final, at)).astype(bf16)
+
+    over_rows(rows, step_out)
+    out_sum.finish()
+    for name in ("sib", "xp", "yp"):
+        pl.semaphore_signal(ready, inc=1, device_id=(p["dp"], p[name]), device_id_type=MESH)
+    load_grad = move(grad_hidden, residual)
+    load_grad.start()
+
+    @pl.loop(0, width // 512)
+    def _(n):
+        at = pl.ds(pl.multiple_of(n * 512, 512), 512)
+        head_grad[at] = dot_l(x[:, at], rotated[...].reshape(shards * rows, wide)).astype(bf16)
+
+    store_head = move(head_grad, head_terms)
+    store_head.start()
+    store_head.wait()
+    head_line.first()
+    pl.semaphore_wait(ready, 3)
+
+    def produce(name, out):
+        s = p[name]
+        grad = rotated[s].reshape(rows, wide)
+
+        @pl.loop(0, 4)
+        def _(n):
+            at = pl.ds(pl.multiple_of(n * span, span), span)
+            out[:, at] = dot_t(grad, qkv[n]).astype(bf16)
+
+    source = Produced(p, produce, stage, kept, paired, send, recv)
+    sums = PlaneSum(p, source, rows, kept, paired, far, final, send, recv)
+    sums.first()
+    wo_line.second(wo_acc, row_parts.at[1], local, z_sem)
+    sums.second()
+    head_line.second(head_acc, parts.at[1], local, z_sem)
+
+    def emit_rows(source, at, out):
+        row_out[...] = source.astype(f32)
+        copy = move(row_out, out.at[at], z_sem)
+        copy.start()
+        copy.wait()
+
+    for j in range(late):
+        copy = move(down_sums.at[j], row_parts.at[0], z_sem)
+        copy.start()
+        copy.wait()
+        emit_rows(row_parts[0], pl.ds(j * piece, piece), grad_down)
+    unit_line.total(parts.at[:, :, pl.ds(0, chunk)], local, z_sem)
+    copy = move(parts.at[0, :, pl.ds(0, chunk)], unit_sum, z_sem)
+    copy.start()
+    copy.wait()
+    exchange_units(late, unit_sum)
+    down_line.total(row_parts, local, z_sem)
+    emit_rows(row_parts[0], pl.ds(late * piece, piece), grad_down)
+    wo_line.total(row_parts, local, z_sem)
+    grad_out[...] = row_parts[0].astype(f32)
+    load_grad.wait()
+    sums.third()
     gain_one_term[...] = jnp.zeros_like(gain_one_term)
 
     def step(at):
@@ -1130,15 +1303,11 @@
         weighted = g * gain[...]
         inner = jnp.mean(weighted * t, axis=-1, keepdims=True)
         grad_tokens[at, :] = (
-            grad_hidden[at, :] + scale * weighted - t * (scale * scale * scale * inner)
+            residual[at, :] + scale * weighted - t * (scale * scale * scale * inner)
         ).astype(bf16)
         gain_one_term[...] += jnp.sum(g * t * scale, axis=0, keepdims=True)
 
     over_rows(rows, step)
-    line[0].second(head_acc, head_parts.at[0], local, 8)
-    line[1].second(unit_acc, unit_parts.at[0], local, 8)
-    line[2].second(down_acc, down_parts.at[0], local, 8)
-    line[3].second(wo_acc, down_parts.at[1], local, 8)
     gain_mine[...] = jnp.zeros_like(gain_mine)
     for k in range(devices):
         at = slice(k * held, (k + 1) * held)
@@ -1159,19 +1328,30 @@
     def _(k):
         gain_copy(k).start()
 
-    def rows_of(ref):
-        return lambda s: ref.at[pl.ds(pl.multiple_of(s * held, held), held)]
-
-    for j in range(EARLY):
-        exchange(j, rows_of(unit_sums.at[j]), units_out.at[j, p["me"]])
-    kept, paired, far, final, send, recv, loads = scratch[7:]
-    source_out = FromMemory(p, out_terms, kept, paired, send, recv, loads)
-    sends += scatter_plane(p, source_out, rows, kept, paired, far, final, send, recv)
-
-    def step_out(at):
-        out_tokens[at, :] = (hidden[at, :] + total(kept, paired, final, at)).astype(bf16)
-
-    over_rows(rows, step_out)
+    head_line.total(parts, local, z_sem)
+    copy = move(parts.at[0], head_sum, z_sem)
+    copy.start()
+    copy.wait()
+    exchange(late + 1, of_owner(head_sum, held), heads.at[p["me"]])
+    for j in range(late + 1):
+        for copy in exchanged[j]:
+            copy.wait()
+    stores = []
+    for i, out in enumerate((grad_gate, grad_up)):
+        for k in range(4):
+            if len(stores) >= 2:
+                stores[-2].wait()
+            for s in range(shards):
+                for a in range(2):
+                    base = (i * 4 + k) * piece
+                    tile = jnp.concatenate(
+                        [units[2 * a + b, s, :, base : base + piece] for b in range(2)], axis=1
+                    )
+                    at = (s * 2 + a) * 2 * piece
+                    wide_out[k % 2, :, at : at + 2 * piece] = tile.astype(f32)
+            wide = wide_out.shape[2]
+            stores.append(move(wide_out.at[k % 2], out.at[:, pl.ds(k * wide, wide)]))
+            stores[-1].start()
     gain_land[0] = gain_mine[mine]
 
     @pl.loop(1, devices)
@@ -1179,123 +1359,135 @@
         gain_copy(k).wait()
 
     gain_sums[...] = jnp.sum(gain_land[...], axis=0)
-
-    def store(src, dst, i):
-        copy = pltpu.make_async_copy(src, dst, local.at[i])
-        copy.start()
+    for copy in exchanged[late + 1]:
         copy.wait()
-
-    line[0].total(head_parts, local, 8)
-    store(head_parts.at[0], head_sum, 8)
-    exchange(EARLY + 1, rows_of(head_sum), heads_out.at[p["me"]])
-    line[1].total(unit_parts, local, 8)
-
-    @pl.loop(0, chunk // 128)
-    def _(n):
-        at = pl.ds(pl.multiple_of(n * 128, 128), 128)
-        turned[:, at] = unit_parts[0, at, :].astype(f32).T.astype(bf16)
-
-    store(turned, unit_sum, 8)
-    exchange(EARLY, rows_of(unit_sum), units_out.at[EARLY, p["me"]])
-    line[2].total(down_parts, local, 8)
-    store(down_parts.at[0], down_sum, 8)
-    line[3].total(down_parts, local, 8)
-    store(down_parts.at[0], wo_sum, 8)
-    for copy in copies:
+    for i, out in enumerate((grad_query, grad_key, grad_value)):
+        for k in range(4):
+            for s in range(0, shards, 2):
+                base = (k // 2 * 3 + i) * PAIR + k % 2 * HD
+                tile = jnp.concatenate(
+                    [heads[s + b, :, base : base + HD] for b in range(2)], axis=1
+                )
+                at = (k * shards + s) * HD
+                out[:, at : at + 2 * HD] = tile.astype(f32)
+    for copy in stores[-2:]:
         copy.wait()
-    for sums in line:
-        sums.finish()
-    source.finish()
-    source_out.finish()
-    for copy in sends:
-        copy.wait_send()
+    for line in (unit_line, down_line, head_line, wo_line):
+        line.finish()
+    sums.finish()
 
 
 def tail_plane(
     groups,
-    shards,
-    terms,
+    branch,
+    normed_one,
+    rotated,
     out_terms,
     unit_terms,
     down_terms,
-    head_terms,
-    wo_terms,
     unit_sums,
-    tokens,
+    down_sums,
     hidden,
     grad_hidden,
+    qkv,
+    out_weight,
+    attended,
+    stats,
+    cos,
+    sin,
+    starts,
+    tokens,
     gain,
     gain_two_term,
     collective_id,
 ):
     rows, width = tokens.shape
+    shards, batch, shard_len, wide = rotated.shape
     devices = groups * shards
-    chunk, piece = unit_terms.shape[1], down_terms.shape[1] // 4
     held = width // devices
-    span, heads_wide = head_terms.shape[1:]
-    wo_rows = wo_terms.shape[1]
+    span = width // groups
+    chunk = unit_terms.shape[2]
+    piece = down_terms.shape[1] // groups
+    units_wide = CHUNKS * chunk // 2 // groups * devices
+    length = shards * shard_len
     sds = jax.ShapeDtypeStruct
-    unit, down_, head, wo_ = (
-        (chunk, chunk),
-        (piece, width),
-        (span, heads_wide),
-        (wo_rows, width),
-    )
+    unit, down, head, wo = (span, chunk), (piece, width), (span, wide), (held, width)
     return pl.pallas_call(
         functools.partial(tail_kernel, devices),
         out_shape=[
             sds((rows, width), bf16),
             sds((rows, width), bf16),
             sds((8, 128), f32),
-            sds(down_, bf16),
-            sds(wo_, bf16),
-            sds((CHUNKS, shards, held, chunk), bf16),
-            sds((shards, held, heads_wide), bf16),
+            *[sds((held, width), f32)] * 4,
+            *[sds((held, units_wide), f32)] * 2,
+            sds((CHUNKS * piece, width), f32),
+            sds((width, wide), bf16),
+            sds((groups * held, width), bf16),
             sds(unit, bf16),
             sds(head, bf16),
             sds((4,) + unit, bf16),
-            sds((4,) + down_, bf16),
+            sds((4,) + down, bf16),
             sds((4,) + head, bf16),
-            sds((4,) + wo_, bf16),
+            sds((4,) + wo, bf16),
         ],
-        in_specs=[ANY] * 7 + [VMEM] * 5,
-        out_specs=[VMEM] * 3 + [ANY] * 10,
+        in_specs=[ANY] * 10 + [VMEM] * 9 + [VMEM],
+        out_specs=[VMEM] * 7 + [ANY] * 11,
         scratch_shapes=[
+            pltpu.VMEM((shards * rows, width), bf16),
+            pltpu.VMEM(rotated.shape, bf16),
+            pltpu.VMEM(attended.shape, bf16),
+            pltpu.VMEM((length, PAIR), f32),
+            pltpu.VMEM((length, PAIR), f32),
+            pltpu.VMEM((width, wide), bf16),
+            pltpu.VMEM((groups * held, width), bf16),
+            pltpu.VMEM((rows, width), f32),
+            pltpu.VMEM((CHUNKS, shards, held, chunk), bf16),
+            pltpu.VMEM((shards, held, wide), bf16),
+            pltpu.VMEM((2, held, units_wide // groups), f32),
+            pltpu.VMEM(down, f32),
             pltpu.VMEM((1, width), f32),
             pltpu.VMEM((devices, 8, 128), f32),
             pltpu.VMEM((devices, 8, 128), f32),
             pltpu.VMEM(unit, bf16),
-            pltpu.VMEM(down_, bf16),
+            pltpu.VMEM(down, bf16),
             pltpu.VMEM(head, bf16),
-            pltpu.VMEM(wo_, bf16),
-            pltpu.VMEM((4,) + unit, bf16),
-            pltpu.VMEM((4,) + down_, bf16),
+            pltpu.VMEM(wo, bf16),
             pltpu.VMEM((4,) + head, bf16),
-            pltpu.VMEM(unit, bf16),
+            pltpu.VMEM((4,) + down, bf16),
+            pltpu.VMEM((2 * rows, width), bf16),
             DMA((16,)),
             DMA((16,)),
             DMA((35,)),
             DMA((35,)),
             DMA((devices,)),
             DMA((devices,)),
-            DMA((12,)),
+            pltpu.SemaphoreType.REGULAR,
+            DMA((48,)),
         ]
-        + scatter_scratch(rows, width) * 2,
+        + scatter_scratch(rows, width),
         compiler_params=pltpu.CompilerParams(
-            collective_id=collective_id, has_side_effects=True, vmem_limit_bytes=60 * MIB
+            collective_id=collective_id, has_side_effects=True, vmem_limit_bytes=62 * MIB
         ),
-        cost_estimate=lasting(120),
+        cost_estimate=lasting(130),
     )(
-        terms,
+        branch,
+        normed_one,
+        rotated,
         out_terms,
         unit_terms,
         down_terms,
-        head_terms,
-        wo_terms,
         unit_sums,
-        tokens,
+        down_sums,
         hidden,
         grad_hidden,
+        qkv,
+        out_weight,
+        attended,
+        stats,
+        cos,
+        sin,
+        starts,
+        tokens,
         gain,
         gain_two_term,
     )
@@ -1424,7 +1616,8 @@
 
     def finish(self):
         for i, _, _ in ORDER[2:]:
-            self.pairs[i].wait_send()
+            if i in self.pairs:
+                self.pairs[i].wait_send()
 
 
 def front_kernel(
@@ -1548,8 +1741,6 @@
                         [weight[:, unit(k) : unit(k) + piece] for k in range(2)], axis=1
                     )
 
-    unit_copies = exchange(lambda s: unit_blocks.at[s], units.at[:, z, held_at], 1)
-
     @pl.loop(1, devices)
     def _(k):
         gain_copy(k, lax.rem(mine_index + devices - k, devices)).wait()
@@ -1566,18 +1757,16 @@
         mine[at, :] = (t * scale * gain_one[...]).astype(bf16)
 
     over_rows(rows, norm_tokens)
-    n1_sent = gather_start(p, mine, x, asend, arecv, 0)
-    n1_own = move(mine, x.at[me], sems.take())
-    n1_own.start()
     for copy in head_copies:
         copy.wait()
     qkv_line = LineGather(p, qkv.at[z], qkv, zsend, zrecv, 1)
     qkv_line.start()
-    n1_late = gather_forward(p, n1_sent, x, asend, arecv, 0)
-    wo_line.second()
+    n1_sent = gather_start(p, mine, x, asend, arecv, 0)
+    n1_own = move(mine, x.at[me], sems.take())
+    n1_own.start()
+    n1_late = gather_forward(p, n1_sent, x, asend, arecv, 0, wo_line.second)
     qkv_line.second()
-    for copy in unit_copies:
-        copy.wait()
+    unit_copies = exchange(lambda s: unit_blocks.at[s], units.at[:, z, held_at], 1)
     chunk_lines = [
         (
             LineGather(p, units.at[j, z], units.at[j], zsend, zrecv, 2 + 2 * j),
@@ -1600,11 +1789,13 @@
 
     gather_wait(n1_sent, n1_late)
     n1_own.wait()
+    qkv_line.third()
+    wo_line.third()
+    for copy in unit_copies:
+        copy.wait()
     cot_sent = gather_start(p, own_cot, cot, csend, crecv, 0)
     cot_own = move(own_cot, cot.at[me], sems.take())
     cot_own.start()
-    wo_line.third()
-    qkv_line.third()
     serve(0, "start")
     keep_normed = move(x, normed_one, sems.take())
     keep_normed.start()
@@ -1680,9 +1871,7 @@
     n2_own.wait()
     for j in range(EARLY):
         serve(j, "finish")
-    source.finish()
-    for copy in sends:
-        copy.wait_send()
+    sends.finish()
 
 
 def front_plane(
@@ -1787,8 +1976,6 @@
     flat = lambda v: v.reshape(shards * count, v.shape[-1])
     split = lambda v: v.reshape(shards, count, v.shape[-1])
 
-    chunks = CHUNKS if fast else 1
-    piece = hidden_held // chunks
     gains = jnp.stack([norm1_gain, norm2_gain])
     own_tokens = tokens.reshape(count, width)
     own_cotangent = cotangent.reshape(count, width)
@@ -1827,9 +2014,6 @@
             (cos, sin, starts),
             1,
         )
-        qkv_weight = qkv_weight.reshape(width, -1)
-        out_weight = out_weight.reshape(-1, width)
-        attended, normed_one = flat(attended), flat(normed_one)
         (
             grad_hidden,
             gain_two_term,
@@ -1903,6 +2087,57 @@
         grad_hidden = own_cotangent.astype(f32) + back
         branch = lax.all_gather(grad_hidden.astype(bf16), "seq")
 
+    if fast:
+        (
+            grad_tokens,
+            out_tokens,
+            grad_norms,
+            grad_query,
+            grad_key,
+            grad_value,
+            grad_out,
+            grad_gate,
+            grad_up,
+            grad_down,
+            *_,
+        ) = tail_plane(
+            groups,
+            branch,
+            normed_one,
+            rotated,
+            out_terms,
+            unit_terms,
+            down_terms,
+            unit_sums,
+            down_sums,
+            hidden,
+            grad_hidden,
+            qkv_weight,
+            out_weight,
+            attended,
+            stats,
+            cos,
+            sin,
+            starts,
+            own_tokens,
+            gain_one,
+            gain_two_term,
+            3,
+        )
+        return (
+            out_tokens.reshape(tokens.shape),
+            grad_tokens.reshape(tokens.shape),
+            grad_norms[0, :held],
+            grad_query,
+            grad_key,
+            grad_value,
+            grad_out,
+            grad_norms[1, :held],
+            grad_gate,
+            grad_up,
+            grad_down,
+        )
+
     branch = flat(branch)
     out_w_terms = dot(attended.T, branch).astype(bf16)
     grad_attended = by_row(dot_t(branch, out_weight).astype(bf16))
@@ -1910,70 +2145,32 @@
     last_terms = split(dot_t(grad_pre, qkv_weight).astype(bf16))
     head_terms = dot(normed_one.T, grad_pre).astype(bf16)
 
-    if fast:
-        (
-            grad_tokens,
-            out_tokens,
-            gain_sums,
-            down_last,
-            grad_out,
-            units_back,
-            heads_back,
-            *_,
-        ) = tail_plane(
-            groups,
-            shards,
-            last_terms,
-            out_terms,
-            unit_terms,
-            down_terms,
-            head_terms.reshape(groups, -1, head_terms.shape[-1]),
-            out_w_terms.reshape(groups, -1, width),
-            unit_sums,
-            own_tokens,
-            hidden,
-            grad_hidden,
-            gain_one,
-            gain_two_term,
-            3,
+    if whole_heads:
+        grad_out = lax.psum_scatter(out_w_terms, "dp", scatter_dimension=0, tiled=True)
+    else:
+        placed = lax.dynamic_update_slice_in_dim(
+            jnp.zeros((width, width), bf16), out_w_terms, lax.axis_index("seq") * inner, 0
         )
-        grad_norms = gain_sums[:2, :held]
-        down_sums = jnp.concatenate([down_sums, down_last[None]]).reshape(hidden_held, width)
-    else:
-        if whole_heads:
-            grad_out = lax.psum_scatter(out_w_terms, "dp", scatter_dimension=0, tiled=True)
-        else:
-            placed = lax.dynamic_update_slice_in_dim(
-                jnp.zeros((width, width), bf16), out_w_terms, lax.axis_index("seq") * inner, 0
-            )
-            grad_out = lax.psum_scatter(placed, ("dp", "seq"), scatter_dimension=0, tiled=True)
-        back, gain_one_term = norm_back(
-            inputs, rms_scale(inputs), gain_one, reduce_plane(last_terms)
-        )
-        grad_tokens = (grad_hidden + back).astype(bf16)
-        out_tokens = (hidden + reduce_plane(out_terms)).astype(bf16)
-        head_sums = lax.psum_scatter(head_terms, "dp", scatter_dimension=0, tiled=True)
-        heads_back, units_back = exchange_plane(
-            [head_sums.reshape(shards, held, -1), unit_sums.reshape(shards, held, -1)], shards, 6
-        )
-        grad_norms = lax.psum_scatter(
-            jnp.concatenate([gain_one_term, gain_two_term]),
-            ("dp", "seq"),
-            scatter_dimension=1,
-            tiled=True,
-        )
-
+        grad_out = lax.psum_scatter(placed, both, scatter_dimension=0, tiled=True)
+    back, gain_one_term = norm_back(inputs, rms_scale(inputs), gain_one, reduce_plane(last_terms))
+    grad_tokens = (grad_hidden + back).astype(bf16)
+    out_tokens = (hidden + reduce_plane(out_terms)).astype(bf16)
+    head_sums = lax.psum_scatter(head_terms, "dp", scatter_dimension=0, tiled=True)
+    heads_back, units_back = exchange_plane(
+        [head_sums.reshape(shards, held, -1), unit_sums.reshape(shards, held, -1)], shards, 6
+    )
+    grad_norms = lax.psum_scatter(
+        jnp.concatenate([gain_one_term, gain_two_term]), both, scatter_dimension=1, tiled=True
+    )
     heads_back = heads_back.reshape(shards, held, pairs, 3, PAIR)
-    units_back = units_back.reshape(chunks, shards, held, 2, groups, piece)
+    units_back = units_back.reshape(shards, held, 2, groups, hidden_held)
 
     def head_grad(i):
         blocks = heads_back[:, :, :, i, :].reshape(shards, held, outer, inner)
         return jnp.moveaxis(blocks, 0, 2).reshape(held, width).astype(f32)
 
     def unit_grad(i):
-        return (
-            jnp.transpose(units_back[:, :, :, i], (2, 3, 1, 0, 4)).reshape(held, -1).astype(f32)
-        )
+        return jnp.transpose(units_back[:, :, i], (1, 2, 0, 3)).reshape(held, -1).astype(f32)
 
     return (
         out_tokens.reshape(tokens.shape),

time: 791 us -> 655 us (0.83)
  Pallas kernels: 683 us -> 618 us
  matrix products: 29 us -> 0 us
  local copies, waits for them, and re-layouts: 43.3 us -> 15.9 us
  other arithmetic: 24.1 us -> 9.72 us
    convert_element_type x13 -> x0, local copies, waits for them, and re-layouts: 30.4 us -> none  [the longest x4 22.6 us: unit_grad(): jnp.transpose(units_back[:, :, :, i], (2, 3, 1, 0, 4)).reshape(held, -1)]
    dot_general x4 -> x0, matrix products: 29 us -> none  [the longest x2 17.5 us: dot(): return jnp.dot(a, b, preferred_element_type=f32)]
    pallas_call x1 -> x0, Pallas kernels: 23.7 us -> none  [attend_back(): pl.pallas_call(attend_back_kernel, grid=(rows, pairs), out_shape=jax.Shap...]
    pallas_call x1, Pallas kernels: 273 us -> 253 us  [front_plane(): pl.pallas_call(functools.partial(front_kernel, groups), out_shape=[sds((r...]
    pallas_call x1, Pallas kernels: 179 us -> 161 us  [tail_plane(): pl.pallas_call(functools.partial(tail_kernel, devices), out_shape=[sds((r...]
    convert_element_type x4 -> x0, other arithmetic: 13.3 us -> none  [the longest x1 5.07 us: head_grad(): return jnp.moveaxis(blocks, 0, 2).reshape(held, width).astype(f32)]
    unnamed x33 -> x24, local copies, waits for them, and re-layouts: 2.01 us -> 13 us
    reshape x2 -> x0, local copies, waits for them, and re-layouts: 8.06 us -> none  [the longest x1 7.71 us: layer(): units_back = units_back.reshape(chunks, shards, held, 2, groups, piece)]
where the time goes in v4:
time: 655 us; the launch traced here: 645 us
  Pallas kernels  618 us (94%)
  local copies, waits for them, and re-layouts  15.9 us (2%)
  other arithmetic  9.72 us (1%)
    pallas_call x1, Pallas kernels, front_plane(): pl.pallas_call(functools.partial(front_kernel, groups), out_shape=[sds((r...  253 us
    pallas_call x1, Pallas kernels, feed_plane(): pl.pallas_call(feed_kernel, out_shape=[sds((rows, width), f32), sds((1, w...  204 us
    pallas_call x1, Pallas kernels, tail_plane(): pl.pallas_call(functools.partial(tail_kernel, devices), out_shape=[sds((r...  161 us

profile of v4, /device:TPU:0, one launch (start us, length us, event | category | flops | bytes accessed | tf_op | source)
XLA Modules:
  0.0 644.8 jit_solution(14576339402242716027)
XLA Ops:
  0.7 0.7 maximum_convert_fusion
  1.4 0.7 slice.18
  2.1 0.6 broadcast_in_dim.6.gains
  2.7 0.8 fusion.1
  3.6 0.6 reduce-window.6
  4.1 0.2 slice_reduce_fusion
  4.4 0.2 reduce-window.9
  4.5 0.7 subtract_convert_fusion
  5.2 3.7 fusion
  9.0 3.0 maximum_bitcast_fusion
  12.0 252.7 %shard_map.203 = (f32[256,2048]{1,0:T(8,128)}, f32[1,2048]{1,0:T(1,128)}, f32[1,2048]{1,0:T(1,128)}, bf16[8,2,128,768]{3,2,1,0:T(8,128)(2,1)}, bf16[8,2,128,256]...) custom-call(bf16[256,2048]{1,0:T(8,128)(2,1)} %bitcast.22, ...), custom_call_target="tpu_custom_call" | custom-call | bytes 700000000 | tf_op jit(solution)/shard_map/pallas_call | solution.py:1909
  264.6 204.0 %shard_map.204 = (f32[256,2048]{1,0:T(8,128)}, f32[1,2048]{1,0:T(1,128)}, bf16[8,256,2048]{2,1,0:T(8,128)(2,1)}, bf16[8,256,2048]{2,1,0:T(8,128)(2,1)}, bf16[3,5...) custom-call(bf16[8,256,2048]{2,1,0:T(8,128)(2,1)} %get-tuple-element, ...), custom_call_target="tpu_custom_call" | custom-call | bytes 560000000 | tf_op jit(solution)/shard_map/pallas_call | solution.py:989
  468.7 161.3 %shard_map.205 = (bf16[256,2048]{1,0:T(8,128)(2,1)}, bf16[256,2048]{1,0:T(8,128)(2,1)}, f32[8,128]{1,0:T(8,128)}, f32[64,2048]{1,0:T(8,128)}, f32[64,2048]{1,0:T...) custom-call(bf16[8,256,2048]{2,1,0:T(8,128)(2,1)} %get-tuple-element, ...), custom_call_target="tpu_custom_call" | custom-call | bytes 455000000 | tf_op jit(solution)/shard_map/pallas_call | solution.py:1415
  630.0 1.3 slice_bitcast_fusion
  631.3 2.4 copy.37
  633.7 2.5 copy.38
  636.2 0.8 copy.39
  637.0 0.8 copy.40
  637.8 0.8 copy.41
  638.6 0.8 copy.42
  639.3 1.3 copy.43
  640.7 1.3 copy.44
  642.0 1.0 copy-done
  643.0 1.3 copy.45
  (18 shorter events, 0.1 us)
Async XLA Ops:
  630.0 6.2 copy-start.6
  630.0 7.0 %copy-start.5 = (f32[64,2048]{1,0:T(8,128)S(1)}, f32[64,2048]{1,0:T(8,128)}, u32[]{:S(2)}) copy-start(f32[64,2048]{1,0:T(8,128)} %get-tuple-element.97) | copy-start | bytes 1572868
  631.3 6.4 copy-start.4
  631.3 7.2 %copy-start.3 = (f32[64,2048]{1,0:T(8,128)S(1)}, f32[64,2048]{1,0:T(8,128)}, u32[]{:S(2)}) copy-start(f32[64,2048]{1,0:T(8,128)} %get-tuple-element.99) | copy-start | bytes 1572868
  633.7 5.6 copy-start.2
  637.8 2.9 copy-start.1
  640.7 2.3 copy-start

commit v5 on v1

v5 whole, which is shorter than its diff:
```python
import functools
import types

import jax
import jax.numpy as jnp
from jax import lax
from jax.experimental import pallas as pl
from jax.experimental.pallas import tpu as pltpu
from jax.sharding import PartitionSpec as P

H = 32
HD = 64
PAIR = 2 * HD

rope_base = 130000.0
norm_eps = 1e-05

bf16 = jnp.bfloat16
f32 = jnp.float32
MESH = pl.DeviceIdType.MESH
ANY = pl.BlockSpec(memory_space=pl.ANY)
VMEM = pl.BlockSpec(memory_space=pltpu.VMEM)
DMA = pltpu.SemaphoreType.DMA
MIB = 1 << 20


def lasting(us):
    return pl.CostEstimate(flops=0, transcendentals=0, bytes_accessed=int(us * 3_500_000))


def plane():
    dp, s = lax.axis_index("dp"), lax.axis_index("seq")
    core, xb, yb = lax.rem(s, 2), lax.rem(lax.div(s, 2), 2), lax.div(s, 4)
    at = lambda y, x, c: y * 4 + x * 2 + c
    return dict(
        dp=dp,
        me=s,
        sib=at(yb, xb, 1 - core),
        xp=at(yb, 1 - xb, core),
        yp=at(1 - yb, xb, core),
        dg=at(1 - yb, 1 - xb, core),
        xs=at(yb, 1 - xb, 1 - core),
        ys=at(1 - yb, xb, 1 - core),
        ds=at(1 - yb, 1 - xb, 1 - core),
    )


def greet(p, names):
    barrier = pltpu.get_barrier_semaphore()
    for name in names:
        pl.semaphore_signal(barrier, inc=1, device_id=(p["dp"], p[name]), device_id_type=MESH)
    pl.semaphore_wait(barrier, len(names))


def remote(p, src, dst, send, recv, i, to):
    return pltpu.make_async_remote_copy(
        src_ref=src,
        dst_ref=dst,
        send_sem=send.at[i],
        recv_sem=recv.at[i],
        device_id=(p["dp"], p[to]),
        device_id_type=MESH,
    )


GATHER_SEMS = 25


def shard_of(out, owner):
    if len(out.shape) == 3:
        return out.at[owner]
    rows = out.shape[0] // 8
    return out.at[pl.ds(pl.multiple_of(owner * rows, rows), rows)]


def gather_copies(p, src, out, send, recv, base):
    quarter = src.shape[0] // 4
    part = lambda ref, k: ref.at[pl.ds(k * quarter, quarter)]
    mine = shard_of(out, p["me"])
    sent = {}
    for j in range(4):
        kx, ky = j, (j + 2) % 4
        sent["x", kx] = remote(p, part(src, kx), part(mine, kx), send, recv, base + kx, "xp")
        sent["y", ky] = remote(p, part(src, ky), part(mine, ky), send, recv, base + 4 + ky, "yp")
    sent["s"] = remote(p, src, mine, send, recv, base + 8, "sib")
    return sent


def gather_start(*args):
    sent = gather_copies(*args)
    for copy in sent.values():
        copy.start()
    return sent


def quarter_of(ref, k):
    rows = ref.shape[0] // 4
    return ref.at[pl.ds(k * rows, rows)]


def gather_pass(p, ref, send, recv, i, to):
    copy = remote(p, ref, ref, send, recv, i, to)
    copy.start()
    return copy


def gather_forward(p, sent, out, send, recv, base, halfway=None):
    part = lambda owner, k: quarter_of(shard_of(out, p[owner]), k)
    passed = []
    for j in range(4):
        kx, ky = j, (j + 2) % 4
        sent["x", kx].wait_recv()
        if j < 2:
            sent["far", kx] = gather_pass(p, part("xp", kx), send, recv, base + 9 + kx, "yp")
        passed.append(gather_pass(p, part("xp", kx), send, recv, base + 13 + kx, "sib"))
        sent["y", ky].wait_recv()
        if j < 2:
            sent["far", ky] = gather_pass(p, part("yp", ky), send, recv, base + 9 + ky, "xp")
        passed.append(gather_pass(p, part("yp", ky), send, recv, base + 17 + ky, "sib"))
        if j == 1 and halfway is not None:
            halfway()

    def last():
        for k in (0, 2, 1, 3):
            sent["far", k].wait_recv()
            passed.append(gather_pass(p, part("dg", k), send, recv, base + 21 + k, "sib"))

    return passed, last


def gather_wait(sent, late, halfway=None):
    passed, last = late
    last()
    if halfway is not None:
        halfway()
    sent["s"].wait_recv()
    for copy in passed:
        copy.wait_recv()
    for copy in list(sent.values()) + passed:
        copy.wait_send()


def gather_finish(p, sent, out, send, recv, base):
    gather_wait(sent, gather_forward(p, sent, out, send, recv, base))


def gather_kernel(count, *refs):
    sources, outs = refs[:count], refs[count : 2 * count]
    send, recv, local = refs[2 * count :]
    p = plane()
    greet(p, ("sib", "xp", "yp"))
    sent, kept = [], []
    for i in range(count):
        sent.append(gather_start(p, sources[i], outs[i], send, recv, i * GATHER_SEMS))
        kept.append(pltpu.make_async_copy(sources[i], outs[i].at[p["me"]], local.at[i]))
        kept[i].start()
    for i in range(count):
        gather_finish(p, sent[i], outs[i], send, recv, i * GATHER_SEMS)
    for copy in kept:
        copy.wait()


def gather_plane(arrays, shards, collective_id):
    if shards != 8:
        return [lax.all_gather(a, "seq") for a in arrays]
    count = len(arrays)
    return pl.pallas_call(
        functools.partial(gather_kernel, count),
        out_shape=[jax.ShapeDtypeStruct((8,) + a.shape, a.dtype) for a in arrays],
        in_specs=[ANY] * count,
        out_specs=[ANY] * count,
        scratch_shapes=[DMA((GATHER_SEMS * count,)), DMA((GATHER_SEMS * count,)), DMA((count,))],
        compiler_params=pltpu.CompilerParams(collective_id=collective_id, has_side_effects=True),
        cost_estimate=lasting(40 * count),
    )(*arrays)


def exchange_kernel(count, *refs):
    sources, outs = refs[:count], refs[count : 2 * count]
    send, recv, local = refs[2 * count :]
    p = plane()
    names = ("dg", "ds", "xp", "yp", "xs", "ys", "sib")
    greet(p, names)
    copies = []
    for i in range(count):
        for j, name in enumerate(names):
            copies.append(
                remote(
                    p, sources[i].at[p[name]], outs[i].at[p["me"]], send, recv, i * 7 + j, name
                )
            )
            copies[-1].start()
        copies.append(
            pltpu.make_async_copy(sources[i].at[p["me"]], outs[i].at[p["me"]], local.at[i])
        )
        copies[-1].start()
    for copy in copies:
        copy.wait()


def exchange_plane(arrays, shards, collective_id):
    if shards != 8:
        return [lax.all_to_all(a, "seq", split_axis=0, concat_axis=0) for a in arrays]
    count = len(arrays)
    return pl.pallas_call(
        functools.partial(exchange_kernel, count),
        out_shape=[jax.ShapeDtypeStruct(a.shape, a.dtype) for a in arrays],
        in_specs=[ANY] * count,
        out_specs=[ANY] * count,
        scratch_shapes=[DMA((7 * count,)), DMA((7 * count,)), DMA((count,))],
        compiler_params=pltpu.CompilerParams(collective_id=collective_id, has_side_effects=True),
        cost_estimate=lasting(35),
    )(*arrays)


BLOCK = 16


def over_rows(rows, step):
    @pl.loop(0, rows // BLOCK)
    def _(i):
        step(pl.ds(pl.multiple_of(i * BLOCK, BLOCK), BLOCK))


def scatter_scratch(rows, width):
    return [
        pltpu.VMEM((4, rows, width), bf16),
        pltpu.VMEM((4, rows, width), bf16),
        pltpu.VMEM((2, rows // 2, width), bf16),
        pltpu.VMEM((2, rows, width), bf16),
        DMA((12,)),
        DMA((12,)),
        DMA((4,)),
    ]


class FromMemory:
    def __init__(self, p, terms, kept, paired, send, recv, local):
        self.loads, self.pairs = {}, {}
        for i, own, other in ORDER:
            self.loads[i] = pltpu.make_async_copy(terms.at[p[own]], kept.at[i], local.at[i])
            self.loads[i].start()
            self.pairs[i] = remote(p, terms.at[p[other]], paired.at[i], send, recv, i, "sib")
            self.pairs[i].start()

    def ready(self, i):
        self.loads[i].wait()
        self.pairs[i].wait_recv()

    def finish(self):
        for copy in self.pairs.values():
            copy.wait_send()


ORDER = ((3, "dg", "ds"), (1, "xp", "xs"), (2, "yp", "ys"), (0, "me", "sib"))


class PlaneSum:
    def __init__(self, p, source, rows, kept, paired, far, final, send, recv):
        self.p, self.source, self.rows = p, source, rows
        self.kept, self.paired, self.far, self.final = kept, paired, far, final
        self.send, self.recv = send, recv
        self.half = rows // 2
        self.low, self.high = pl.ds(0, self.half), pl.ds(self.half, self.half)
        self.sends, self.near = [], []

    def add_pair(self, i):
        kept, paired = self.kept, self.paired
        self.source.ready(i)

        def step(at):
            kept[i, at, :] = (kept[i, at, :].astype(f32) + paired[i, at, :].astype(f32)).astype(
                bf16
            )

        over_rows(self.rows, step)

    def put(self, src, dst, i, to):
        copy = remote(self.p, src, dst, self.send, self.recv, i, to)
        copy.start()
        self.sends.append(copy)
        return copy

    def first(self):
        kept, far, final, low, high = self.kept, self.far, self.final, self.low, self.high
        self.add_pair(3)
        self.far_x = self.put(kept.at[3, low], far.at[0], 4, "xp")
        self.far_y = self.put(kept.at[3, high], far.at[1], 5, "yp")
        self.add_pair(1)
        self.near.append(self.put(kept.at[1, low], final.at[0, low], 6, "xp"))
        self.add_pair(2)
        self.near.append(self.put(kept.at[2, high], final.at[1, high], 7, "yp"))

    def second(self):
        kept, far, final, low, high = self.kept, self.far, self.final, self.low, self.high
        half = self.half
        self.far_x.wait_recv()

        def step_x(at):
            kept[2, at, :] = (kept[2, at, :].astype(f32) + far[0, at, :].astype(f32)).astype(bf16)

        over_rows(half, step_x)
        self.near.append(self.put(kept.at[2, low], final.at[1, low], 8, "yp"))
        self.far_y.wait_recv()

        def step_y(at):
            up = pl.ds(pl.multiple_of(at.start + half, BLOCK), BLOCK)
            kept[1, up, :] = (kept[1, up, :].astype(f32) + far[1, at, :].astype(f32)).astype(bf16)

        over_rows(half, step_y)
        self.near.append(self.put(kept.at[1, high], final.at[0, high], 9, "xp"))
        self.source.ready(0)

    def third(self):
        for copy in self.near:
            copy.wait_recv()

    def finish(self):
        self.source.finish()
        for copy in self.sends:
            copy.wait_send()


def scatter_plane(p, source, rows, kept, paired, far, final, send, recv, between, meanwhile):
    sums = PlaneSum(p, source, rows, kept, paired, far, final, send, recv)
    sums.first()
    between()
    sums.second()
    meanwhile()
    sums.third()
    return sums


def total(kept, paired, final, at):
    return (kept[0, at, :].astype(f32) + paired[0, at, :].astype(f32)) + (
        final[0, at, :].astype(f32) + final[1, at, :].astype(f32)
    )


def reduce_plane(terms):
    rows = terms.shape[1]
    return lax.psum_scatter(terms, "seq", scatter_dimension=0, tiled=False).astype(f32).reshape(
        rows, terms.shape[2]
    )


def rms_scale(values):
    return lax.rsqrt(jnp.mean(values * values, axis=-1, keepdims=True) + norm_eps)


def norm_back(values, scale, gain, grad):
    weighted = grad * gain
    inner = jnp.mean(weighted * values, axis=-1, keepdims=True)
    return (
        scale * weighted - values * (scale * scale * scale) * inner,
        jnp.sum(grad * values * scale, axis=0, keepdims=True),
    )


def swap_halves(v, first):
    width = v.shape[-1]
    return jnp.where(first, pltpu.roll(v, width - HD // 2, 1), pltpu.roll(v, HD // 2, 1))


def dot_t(a, b):
    return lax.dot_general(a, b, (((1,), (1,)), ((), ())), preferred_element_type=f32)


def dot(a, b):
    return jnp.dot(a, b, preferred_element_type=f32)


def dot_l(a, b):
    return lax.dot_general(a, b, (((0,), (0,)), ((), ())), preferred_element_type=f32)


def allowed_pairs(start, keys, queries, offset):
    key = lax.broadcasted_iota(jnp.int32, (keys, queries), 0)
    query = lax.broadcasted_iota(jnp.int32, (keys, queries), 1) + offset
    return (key >= start) & (key <= query)


def attend_pair(pre, cos, sin, starts, rotated, attended, stats, r, pair):
    shards, _, shard_len, _ = pre.shape
    length = shards * shard_len
    block = min(256, length)
    per = block // shard_len
    lanes = lambda i: pl.ds(pl.multiple_of((pair * 3 + i) * PAIR, PAIR), PAIR)
    first = lax.rem(lax.broadcasted_iota(jnp.int32, (length, PAIR), 1), HD) < HD // 2
    cos_all, sin_all = cos[:, r].reshape(length, PAIR), sin[:, r].reshape(length, PAIR)

    def rotate(i):
        v = pre[:, r, :, lanes(i)].reshape(length, PAIR)
        return (v * cos_all + swap_halves(v, first) * sin_all).astype(bf16)

    query, key = rotate(0), rotate(1)
    value = pre[:, r, :, lanes(2)].reshape(length, PAIR)
    value_t = value.T.astype(bf16)
    for i, v in enumerate((query, key, value.astype(bf16))):
        rotated[:, r, :, lanes(i)] = v.reshape(shards, shard_len, PAIR)
    left = lax.broadcasted_iota(jnp.int32, (block, PAIR), 1) < HD
    top = lax.broadcasted_iota(jnp.int32, (PAIR, block), 0) < HD
    scaled = query * jnp.asarray(0.125, bf16)
    here_lanes = pl.ds(pl.multiple_of(pair * PAIR, PAIR), PAIR)
    for i in range(length // block):
        keys = (i + 1) * block
        at = slice(i * block, (i + 1) * block)
        mask = allowed_pairs(starts[:, at], keys, block, i * block)
        here = scaled[at]
        results = []
        for h in range(2):
            own = jnp.where(left if h == 0 else ~left, here, jnp.zeros_like(here))
            scores = jnp.where(mask, dot_t(key[:keys], own), -1e30)
            peak = jnp.max(scores, axis=0, keepdims=True)
            shifted = jnp.exp(scores - peak)
            summed = jnp.sum(shifted, axis=0, keepdims=True)
            probs = (shifted * (1.0 / summed)).astype(bf16)
            results.append(dot(value_t[:, :keys], probs))
            stats[r, pair, h : h + 1, at] = peak + jnp.log(summed)
        merged = jnp.where(top, results[0], results[1]).T.astype(bf16)
        attended[i * per : (i + 1) * per, r, :, here_lanes] = merged.reshape(
            per, shard_len, PAIR
        )


def attend_kernel(pre, cos, sin, starts, rotated, attended, stats):
    attend_pair(pre, cos, sin, starts[0], rotated, attended, stats, 0, 0)


def attend(pre, cos, sin, starts):
    shards, rows, shard_len, width = pre.shape
    pairs = width // (3 * PAIR)
    length = shards * shard_len
    wide = pl.BlockSpec((shards, 1, shard_len, 3 * PAIR), lambda r, p: (0, r, 0, p))
    narrow = pl.BlockSpec((shards, 1, shard_len, PAIR), lambda r, p: (0, r, 0, p))
    table = pl.BlockSpec((shards, 1, shard_len, PAIR), lambda r, p: (0, r, 0, 0))
    return pl.pallas_call(
        attend_kernel,
        grid=(rows, pairs),
        out_shape=[
            jax.ShapeDtypeStruct(pre.shape, bf16),
            jax.ShapeDtypeStruct((shards, rows, shard_len, pairs * PAIR), bf16),
            jax.ShapeDtypeStruct((rows, pairs, 2, length), f32),
        ],
        in_specs=[wide, table, table, pl.BlockSpec((1, 1, length), lambda r, p: (r, 0, 0))],
        out_specs=[wide, narrow, pl.BlockSpec((1, 1, 2, length), lambda r, p: (r, p, 0, 0))],
        compiler_params=pltpu.CompilerParams(vmem_limit_bytes=48 * MIB),
        cost_estimate=pl.CostEstimate(
            flops=rows * pairs * 2 * length * length * 256 * 2,
            bytes_accessed=pre.size * 8,
            transcendentals=rows * pairs * length * length,
        ),
    )(pre, cos, sin, starts)


def attend_back_pair(rotated, grad, cos, sin, starts, stats, result, key_acc, value_acc, r, pair):
    shards, _, shard_len, _ = rotated.shape
    length = shards * shard_len
    block = min(256, length)
    per = block // shard_len
    lanes = lambda i: pl.ds(pl.multiple_of((pair * 3 + i) * PAIR, PAIR), PAIR)
    query, key, value = (rotated[:, r, :, lanes(i)].reshape(length, PAIR) for i in range(3))
    grad_all = grad[:, r, :, pl.ds(pl.multiple_of(pair * PAIR, PAIR), PAIR)].reshape(length, PAIR)
    key_t = key.astype(f32).T.astype(bf16)
    left = lax.broadcasted_iota(jnp.int32, (block, PAIR), 1) < HD
    top = lax.broadcasted_iota(jnp.int32, (PAIR, block), 0) < HD
    first = lax.rem(lax.broadcasted_iota(jnp.int32, (length, PAIR), 1), HD) < HD // 2
    key_acc[...] = jnp.zeros_like(key_acc)
    value_acc[...] = jnp.zeros_like(value_acc)

    for i in range(length // block):
        keys = (i + 1) * block
        at = slice(i * block, (i + 1) * block)
        here = slice(i * per, (i + 1) * per)
        mask = allowed_pairs(starts[:, at], keys, block, i * block)
        results = []
        for h in range(2):
            side = left if h == 0 else ~left
            own = jnp.where(side, query[at], jnp.zeros_like(query[at]))
            own_grad = jnp.where(side, grad_all[at], jnp.zeros_like(grad_all[at]))
            scores = dot_t(key[:keys], own * jnp.asarray(0.125, bf16))
            probs = jnp.exp(jnp.where(mask, scores - stats[r, pair, h : h + 1, at], -1e30))
            grad_probs = dot_t(value[:keys], own_grad)
            inner = jnp.sum(probs * grad_probs, axis=0, keepdims=True)
            grad_scores = (probs * (grad_probs - inner) * 0.125).astype(bf16)
            key_acc[:keys, :] += dot(grad_scores, own)
            value_acc[:keys, :] += dot(probs.astype(bf16), own_grad)
            results.append(dot(key_t[:, :keys], grad_scores))
        merged = jnp.where(top, results[0], results[1]).T
        cos_here, sin_here = cos[here, r].reshape(block, PAIR), sin[here, r].reshape(block, PAIR)
        turned = merged * cos_here - swap_halves(merged, first[:block]) * sin_here
        result[here, r, :, lanes(0)] = turned.astype(bf16).reshape(per, shard_len, PAIR)
    cos_all, sin_all = cos[:, r].reshape(length, PAIR), sin[:, r].reshape(length, PAIR)
    key_grad = key_acc[...]
    turned = key_grad * cos_all - swap_halves(key_grad, first) * sin_all
    result[:, r, :, lanes(1)] = turned.astype(bf16).reshape(shards, shard_len, PAIR)
    result[:, r, :, lanes(2)] = value_acc[...].astype(bf16).reshape(shards, shard_len, PAIR)


def attend_back_kernel(rotated, grad, cos, sin, starts, stats, result, key_acc, value_acc):
    attend_back_pair(
        rotated, grad, cos, sin, starts[0], stats, result, key_acc, value_acc, 0, 0
    )


def attend_back(rotated, grad, cos, sin, starts, stats):
    shards, rows, shard_len, width = rotated.shape
    pairs = width // (3 * PAIR)
    length = shards * shard_len
    wide = pl.BlockSpec((shards, 1, shard_len, 3 * PAIR), lambda r, p: (0, r, 0, p))
    narrow = pl.BlockSpec((shards, 1, shard_len, PAIR), lambda r, p: (0, r, 0, p))
    table = pl.BlockSpec((shards, 1, shard_len, PAIR), lambda r, p: (0, r, 0, 0))
    return pl.pallas_call(
        attend_back_kernel,
        grid=(rows, pairs),
        out_shape=jax.ShapeDtypeStruct(rotated.shape, bf16),
        in_specs=[
            wide,
            narrow,
            table,
            table,
            pl.BlockSpec((1, 1, length), lambda r, p: (r, 0, 0)),
            pl.BlockSpec((1, 1, 2, length), lambda r, p: (r, p, 0, 0)),
        ],
        out_specs=wide,
        scratch_shapes=[pltpu.VMEM((length, PAIR), f32), pltpu.VMEM((length, PAIR), f32)],
        compiler_params=pltpu.CompilerParams(vmem_limit_bytes=48 * MIB),
        cost_estimate=pl.CostEstimate(
            flops=rows * pairs * 5 * length * length * 256 * 2,
            bytes_accessed=rotated.size * 6,
            transcendentals=rows * pairs * length * length,
        ),
    )(rotated, grad, cos, sin, starts, stats)


def document_starts(doc_ids):
    places = lax.broadcasted_iota(jnp.int32, doc_ids.shape, 1)
    earlier = jnp.concatenate([doc_ids[:, :1], doc_ids[:, :-1]], axis=1)
    return lax.cummax(jnp.where(doc_ids != earlier, places, 0), axis=1)


def rope_frequency():
    return rope_base ** (-(jnp.arange(HD // 2, dtype=f32) * 2.0 / HD))


def rope_tables(starts, shards):
    rows, length = starts.shape
    positions = (lax.broadcasted_iota(jnp.int32, starts.shape, 1) - starts).astype(f32)
    angles = positions[..., None] * rope_frequency()
    cos, sin = jnp.cos(angles), jnp.sin(angles)
    lay = lambda v: jnp.moveaxis(
        jnp.concatenate(v, axis=-1).reshape(rows, shards, length // shards, PAIR), 0, 1
    )
    return lay([cos] * 4), lay([-sin, sin, -sin, sin])


class LineSum:
    def __init__(self, p, view, land, send, recv, base):
        self.p, self.view, self.land = p, view, land
        self.send, self.recv, self.base = send, recv, base
        self.z = p["dp"]
        self.inward = 1 - 2 * lax.div(self.z, 2)
        self.end = (self.z == 0) | (self.z == 3)

    def copy(self, src, slot, i, to):
        return pltpu.make_async_remote_copy(
            src_ref=src,
            dst_ref=self.land.at[slot],
            send_sem=self.send.at[self.base + i],
            recv_sem=self.recv.at[self.base + slot],
            device_id=(to, self.p["me"]),
            device_id_type=MESH,
        )

    def arrived(self, slot):
        self.copy(self.land.at[slot], slot, 0, self.z).wait_recv()

    def first(self):
        z, inward = self.z, self.inward

        @pl.when(self.end)
        def _():
            near, mid, far = z + inward, z + 2 * inward, z + 3 * inward
            self.copy(self.view(far), near, 0, near).start()
            self.copy(self.view(mid), far, 1, near).start()
            self.copy(self.view(near), z, 2, near).start()

    def second(self, acc, extra, local, i):
        z, inward = self.z, self.inward

        @pl.when(jnp.logical_not(self.end))
        def _():
            outer, inner, far = z - inward, z + inward, z + 2 * inward
            own = [
                pltpu.make_async_copy(self.view(to), acc.at[k], local.at[i + k])
                for k, to in enumerate((far, inner))
            ]
            other = [
                pltpu.make_async_copy(self.land.at[slot], extra.at[k], local.at[i + 2 + k])
                for k, slot in enumerate((z, far))
            ]
            for copy in own:
                copy.start()
            for k, slot in enumerate((z, far)):
                self.arrived(slot)
                other[k].start()
            for k, to in enumerate((far, inner)):
                own[k].wait()
                other[k].wait()

                def step(at):
                    acc[k, at, :] = (acc[k, at, :].astype(f32) + extra[k, at, :].astype(f32)).astype(
                        bf16
                    )

                over_rows(acc.shape[1], step)
                self.copy(acc.at[k], z, k, to).start()
            self.copy(self.view(outer), z, 2, outer).start()

    def total(self, parts, local, i):
        z, inward = self.z, self.inward
        one = jnp.where(self.end, z + 2 * inward, z - inward)
        two = z + inward
        loads = [pltpu.make_async_copy(self.view(z), parts.at[0], local.at[i])]
        loads[0].start()
        for k, slot in ((1, one), (2, two)):
            self.arrived(slot)
            loads.append(pltpu.make_async_copy(self.land.at[slot], parts.at[k], local.at[i + k]))
            loads[k].start()
        for load in loads:
            load.wait()

        def step(at):
            parts[0, at, :] = (
                (parts[0, at, :].astype(f32) + parts[1, at, :].astype(f32))
                + parts[2, at, :].astype(f32)
            ).astype(bf16)

        over_rows(parts.shape[1], step)

    def finish(self):
        for i in range(3):
            self.copy(self.land.at[0], 0, i, self.z).wait_send()


LINE_SEMS = 5


class LineGather:
    def __init__(self, p, src, out, send, recv, base, own=None):
        self.p, self.src, self.out = p, src, out
        self.send, self.recv, self.base = send, recv, base * LINE_SEMS
        self.z = p["dp"]
        self.inward = 1 - 2 * lax.div(self.z, 2)
        self.end = (self.z == 0) | (self.z == 3)
        self.own = None if own is None else pltpu.make_async_copy(src, out.at[self.z], own)

    def copy(self, src, owner, i, to):
        return pltpu.make_async_remote_copy(
            src_ref=src,
            dst_ref=self.out.at[owner],
            send_sem=self.send.at[self.base + i],
            recv_sem=self.recv.at[self.base + owner],
            device_id=(to, self.p["me"]),
            device_id_type=MESH,
        )

    def arrived(self, owner):
        self.copy(self.src, owner, 0, self.z).wait_recv()

    def start(self):
        z, inward = self.z, self.inward
        if self.own is not None:
            self.own.start()
        self.copy(self.src, z, 0, z + inward).start()

        @pl.when(jnp.logical_not(self.end))
        def _():
            self.copy(self.src, z, 1, z - inward).start()

    def second(self):
        z, inward = self.z, self.inward

        @pl.when(jnp.logical_not(self.end))
        def _():
            outer, inner = z - inward, z + inward
            self.arrived(inner)
            self.copy(self.out.at[inner], inner, 2, outer).start()
            self.arrived(outer)
            self.copy(self.out.at[outer], outer, 3, inner).start()

    def third(self):
        z, inward = self.z, self.inward

        @pl.when(jnp.logical_not(self.end))
        def _():
            far = z + 2 * inward
            self.arrived(far)
            self.copy(self.out.at[far], far, 4, z - inward).start()

    def finish(self):
        z, inward = self.z, self.inward

        @pl.when(self.end)
        def _():
            for k in range(1, 4):
                self.arrived(z + k * inward)

        if self.own is not None:
            self.own.wait()
        self.copy(self.src, 0, 0, z).wait_send()

        @pl.when(jnp.logical_not(self.end))
        def _():
            for i in range(1, 5):
                self.copy(self.src, 0, i, z).wait_send()


CHUNKS = 4
OTHERS = ("dg", "ds", "xp", "yp", "xs", "ys", "sib")


def meet_all(p, devices):
    mine = p["dp"] * 8 + p["me"]
    barrier = pltpu.get_barrier_semaphore()

    def other(k):
        to = lax.rem(mine + k, devices)
        return dict(device_id=(lax.div(to, 8), lax.rem(to, 8)), device_id_type=MESH), to

    @pl.loop(1, devices)
    def _(k):
        pl.semaphore_signal(barrier, inc=1, **other(k)[0])

    return other, lambda: pl.semaphore_wait(barrier, devices - 1)


class Local:
    def __init__(self, sems):
        self.sems, self.used, self.free = sems, 0, []

    def take(self, count=1):
        if count == 1 and self.free:
            return self.free.pop(0)
        self.used += count
        assert self.used <= self.sems.shape[0], self.used
        return self.used - count


class Produced:
    def __init__(self, p, produce, stage, kept, paired, send, recv):
        self.p, self.produce, self.stage = p, produce, stage
        self.kept, self.paired, self.send, self.recv = kept, paired, send, recv
        self.pairs = {}

    def ready(self, i):
        k = len(self.pairs)
        _, own, other = ORDER[k]
        rows = self.kept.shape[1]
        stage = self.stage.at[pl.ds(k % 2 * rows, rows)]
        if k >= 2:
            self.pairs[ORDER[k - 2][0]].wait_send()
        self.produce(other, stage)
        self.pairs[i] = remote(self.p, stage, self.paired.at[i], self.send, self.recv, i, "sib")
        self.pairs[i].start()
        self.produce(own, self.kept.at[i])
        self.pairs[i].wait_recv()

    def finish(self):
        for i, _, _ in ORDER[2:]:
            if i in self.pairs:
                self.pairs[i].wait_send()


MAIN_INPUTS = (
    "w_query",
    "w_key",
    "w_value",
    "w_gate",
    "w_up",
    "w_out",
    "w_down",
    "tokens",
    "own_cot",
    "gains",
    "starts",
    "frequency",
)
RESULTS = (
    "gain_sums",
    "grad_tokens",
    "out_tokens",
    "grad_query",
    "grad_key",
    "grad_value",
    "grad_out",
    "grad_gate",
    "grad_up",
    "grad_down",
)
HELD_IN_HBM = (
    "cos",
    "sin",
    "rotated",
    "attended",
    "normed_one",
    "cot",
    "branch",
    "qkv",
    "out_weight",
    "units",
    "down",
    "out_terms",
    "unit_sums",
    "unit_terms",
    "down_terms",
    "kept_units",
    "kept_acts",
    "head_terms",
    "wo_terms",
    "head_sums",
    "unit_land",
    "down_land",
    "head_land",
    "wo_land",
    "units_out",
    "heads_out",
)
SCATTER_NAMES = ("kept", "paired", "far", "final", "send", "recv")
GATHER_NAMES = tuple(k + way for k in "ac" for way in ("send", "recv"))
MAIN_OUTPUTS = RESULTS + HELD_IN_HBM
MAIN_SCRATCH = (
    "hidden",
    "grad_hidden",
    "gain_one",
    "gain_two",
    "gain_term",
    "stats",
    "gains_land",
    "gain_mine",
    "gain_sum_land",
    "x",
    "unit_acc",
    "down_acc",
    "mine",
    "stage",
    "kept",
    "paired",
    "far",
    "final",
    "send",
    "recv",
    "asend",
    "arecv",
    "csend",
    "crecv",
    "gsend",
    "grecv",
    "esend",
    "erecv",
    "zsend",
    "zrecv",
    "ssend",
    "srecv",
    "ready",
    "local",
)


def main_kernel(groups, *refs):
    r = types.SimpleNamespace(**dict(zip(MAIN_INPUTS + MAIN_OUTPUTS + MAIN_SCRATCH, refs)))
    p = plane()
    devices = groups * 8
    other, met = meet_all(p, devices)
    shards = 8
    rows, width = r.tokens.shape
    held = r.w_query.shape[0]
    batch, shard_len, wide = r.rotated.shape[1:]
    pairs = width // 8 // PAIR
    piece, chunk = r.down.shape[2], r.units.shape[3]
    part = chunk // 2
    me, z = p["me"], p["dp"]
    mine_index = z * 8 + me
    held_at = pl.ds(pl.multiple_of(me * held, held), held)
    sems = Local(r.local)
    x = r.x

    lent = {}

    def move(src, dst, i=None):
        place = sems.take() if i is None else i
        copy = pltpu.make_async_copy(src, dst, r.local.at[place])
        if i is None:
            lent[id(copy)] = (copy, place)
        return copy

    def start(*copies):
        for copy in copies:
            copy.start()
        return copies

    def wait(copies):
        for copy in copies:
            copy.wait()
        for copy in copies:
            if id(copy) in lent:
                sems.free.append(lent.pop(id(copy))[1])

    def shard_rows(s, count=1):
        return pl.ds(pl.multiple_of(s * rows, rows), count * rows)

    def line(src, out, i, own):
        sem = r.local.at[sems.take()] if own else None
        return LineGather(p, src, out, r.zsend, r.zrecv, i, sem)

    wo_line = line(r.w_out, r.out_weight, 0, True)
    qkv_line = line(r.qkv.at[z], r.qkv, 1, False)
    chunk_lines = [
        (
            line(r.units.at[j, z], r.units.at[j], 2 + 2 * j, False),
            line(r.w_down.at[pl.ds(j * piece, piece)], r.down.at[j], 3 + 2 * j, True),
        )
        for j in range(CHUNKS)
    ]

    def serve(j, what, *only):
        for k in only or (0, 1):
            getattr(chunk_lines[j][k], what)()

    def gain_copy(k, sender):
        return pltpu.make_async_remote_copy(
            src_ref=r.gains,
            dst_ref=r.gains_land.at[sender],
            send_sem=r.gsend.at[k],
            recv_sem=r.grecv.at[sender],
            **other(k)[0],
        )

    def exchange(block, out, i):
        copies = [
            remote(p, block(p[name]), out, r.esend, r.erecv, i * 7 + j, name)
            for j, name in enumerate(OTHERS)
        ]
        return start(*copies, move(block(me), out))

    def of_owner(ref, count):
        return lambda owner: ref.at[pl.ds(pl.multiple_of(owner * count, count), count)]

    def scatter(produce, between, meanwhile):
        source = Produced(p, produce, r.stage, r.kept, r.paired, r.send, r.recv)
        return scatter_plane(
            p, source, rows, r.kept, r.paired, r.far, r.final, r.send, r.recv, between, meanwhile
        )

    def before(
        w_query, w_key, w_value, w_gate, w_up, cos, sin, head_blocks, unit_blocks, w, wo, pre, rotated, attended
    ):
        head_loads = start(move(r.w_query, w_query), move(r.w_key, w_key), move(r.w_value, w_value))
        unit_loads = start(move(r.w_gate, w_gate), move(r.w_up, w_up))
        wait(head_loads)
        for s in range(shards):
            for pair in range(pairs):
                for i, weight in enumerate((w_query, w_key, w_value)):
                    head = lambda k: ((2 * pair + k) * 8 + s) * HD
                    base = (pair * 3 + i) * PAIR
                    head_blocks[s, :, base : base + PAIR] = jnp.concatenate(
                        [weight[:, head(k) : head(k) + HD] for k in range(2)], axis=1
                    )
        met()

        @pl.loop(1, devices)
        def _(k):
            gain_copy(k, mine_index).start()

        r.gains_land[mine_index] = r.gains[...]
        head_copies = exchange(lambda s: head_blocks.at[s], r.qkv.at[z, held_at], 0)
        wait(unit_loads)
        for s in range(shards):
            for i, weight in enumerate((w_gate, w_up)):
                for j in range(CHUNKS):
                    for pair in range(groups // 2):
                        unit = lambda k: ((2 * pair + k) * 8 + s) * CHUNKS * piece + j * piece
                        base = i * groups * piece + pair * 2 * piece
                        unit_blocks[s, j, :, base : base + 2 * piece] = jnp.concatenate(
                            [weight[:, unit(k) : unit(k) + piece] for k in range(2)], axis=1
                        )

        @pl.loop(1, devices)
        def _(k):
            gain_copy(k, lax.rem(mine_index + devices - k, devices)).wait()

        for out, base in ((r.gain_one, 0), (r.gain_two, held)):
            for k in range(0, devices, 2):
                out[:, k * held : (k + 2) * held] = jnp.concatenate(
                    [r.gains_land[k + i, 0:1, base : base + held] for i in range(2)], axis=1
                )

        def norm_tokens(at):
            t = r.tokens[at, :].astype(f32)
            scale = lax.rsqrt(jnp.mean(t * t, axis=-1, keepdims=True) + norm_eps)
            r.mine[at, :] = (t * scale * r.gain_one[...]).astype(bf16)

        over_rows(rows, norm_tokens)
        wait(head_copies)
        qkv_line.start()
        n1_sent = gather_start(p, r.mine, x, r.asend, r.arecv, 0)
        n1_own = start(move(r.mine, x.at[shard_rows(me)]))
        n1_late = gather_forward(p, n1_sent, x, r.asend, r.arecv, 0, qkv_line.second)
        qkv_line.third()
        serve(0, "start", 1)
        wo_line.start()
        unit_exchange = lambda j: exchange(
            lambda s: unit_blocks.at[s, j], r.units.at[j, z, held_at], 1 + j
        )
        unit_copies = [unit_exchange(0)]

        def halfway():
            for j in range(1, CHUNKS):
                unit_copies.append(unit_exchange(j))

        gather_wait(n1_sent, n1_late, halfway)
        wait(n1_own)
        wait(unit_copies[0])
        serve(0, "start", 0)
        keep_normed = start(
            *[move(x.at[shard_rows(s)], r.normed_one.at[s]) for s in range(shards)]
        )
        for row in range(batch):
            length = shards * shard_len
            since = jnp.broadcast_to(r.starts[row].astype(f32), (PAIR, length)).T
            place = lax.broadcasted_iota(jnp.int32, (length, PAIR), 0).astype(f32)
            angles = (place - since) * r.frequency[...]
            lane = lax.broadcasted_iota(jnp.int32, (length, PAIR), 1)
            sign = jnp.where(lax.rem(lane, HD) < HD // 2, -1.0, 1.0)
            cos[:, row] = jnp.cos(angles).reshape(shards, shard_len, PAIR)
            sin[:, row] = (sign * jnp.sin(angles)).reshape(shards, shard_len, PAIR)
        keep_tables = start(move(cos, r.cos), move(sin, r.sin))
        qkv_line.finish()
        load_w = start(move(r.qkv, w))
        serve(0, "second", 1)
        wo_line.second()
        wait(load_w)

        @pl.loop(0, shards, step=2)
        def _(s):
            here = dot(x[shard_rows(s, 2)], w[...].reshape(width, wide))
            pre[pl.ds(s, 2)] = here.reshape((2,) + pre.shape[1:])

        for copies in unit_copies[1:]:
            wait(copies)
        serve(0, "second", 0)
        serve(0, "third", 1)
        wo_line.third()
        serve(1, "start")
        cot_sent = gather_start(p, r.own_cot, r.cot, r.csend, r.crecv, 0)
        cot_own = start(move(r.own_cot, r.cot.at[me]))

        def attention(row):
            @pl.loop(0, pairs)
            def _(pair):
                attend_pair(
                    pre, cos, sin, r.starts[row], rotated, attended, r.stats, row, pair
                )

        attention(0)
        attention(1)
        cot_late = gather_forward(p, cot_sent, r.cot, r.csend, r.crecv, 0)
        serve(0, "third", 0)
        keep_heads = start(move(rotated, r.rotated), move(attended, r.attended))
        wo_line.finish()
        wait(keep_normed)
        wait(start(move(r.out_weight, wo)))

        def produce(name, out):
            terms = attended[p[name]].reshape(rows, attended.shape[3])

            @pl.loop(0, width // 512)
            def _(n):
                at = pl.ds(pl.multiple_of(n * 512, 512), 512)
                out[:, at] = dot(terms, wo[:, :, at].reshape(terms.shape[1], 512)).astype(bf16)

        def between():
            serve(1, "second")
            serve(2, "start")

        def meanwhile():
            gather_wait(cot_sent, cot_late)
            wait(cot_own)

        scatter(produce, between, meanwhile).finish()
        wait(keep_heads)
        wait(keep_tables)

    vm = lambda shape, dtype=bf16: pltpu.VMEM(shape, dtype)
    pl.run_scoped(
        before,
        *[vm(ref.shape) for ref in (r.w_query, r.w_key, r.w_value, r.w_gate, r.w_up)],
        *[vm(ref.shape, f32) for ref in (r.cos, r.sin)],
        vm((shards, held, wide)),
        vm((shards, CHUNKS, held, chunk)),
        vm(r.qkv.shape),
        vm(r.out_weight.shape),
        vm(r.rotated.shape, f32),
        vm(r.rotated.shape),
        vm(r.attended.shape),
    )

    def norm_hidden(at):
        h = r.tokens[at, :].astype(f32) + total(r.kept, r.paired, r.final, at)
        r.hidden[at, :] = h
        scale = lax.rsqrt(jnp.mean(h * h, axis=-1, keepdims=True) + norm_eps)
        r.mine[at, :] = (h * scale * r.gain_two[...]).astype(bf16)

    over_rows(rows, norm_hidden)
    n2_sent = gather_start(p, r.mine, x, r.asend, r.arecv, 0)
    n2_own = start(move(r.mine, x.at[shard_rows(me)]))
    serve(1, "third")
    serve(2, "second")
    serve(3, "start")

    span = r.unit_land.shape[2]
    sum_lines = [
        (
            LineSum(
                p, of_owner(r.unit_terms.at[j], span), r.unit_land.at[j], r.ssend, r.srecv, 8 * j
            ),
            LineSum(
                p,
                of_owner(r.down_terms.at[j], piece),
                r.down_land.at[j],
                r.ssend,
                r.srecv,
                8 * j + 4,
            ),
        )
        for j in range(CHUNKS)
    ]
    head_lines = [
        LineSum(
            p, of_owner(r.head_terms.at[k], span), r.head_land.at[k], r.ssend, r.srecv, 8 * CHUNKS + 4 * k
        )
        for k in range(pairs)
    ]
    wo_sum = LineSum(
        p, of_owner(r.wo_terms, held), r.wo_land, r.ssend, r.srecv, 8 * CHUNKS + 4 * pairs
    )

    chunk_sem, keep_sem, term_sem, kept_sem, act_sem, out_sem, z_sem = (
        sems.take(k) for k in (4, 2, 2, 2, 2, 2, 8)
    )

    def after(
        c,
        w,
        d,
        unit_stage,
        act_stage,
        unit_kept,
        act_kept,
        unit_grad,
        down_grad,
        unit_parts,
        down_parts,
    ):
        def chunk_loads(j):
            return (
                move(r.units.at[j], w.at[j % 2], chunk_sem + j % 2),
                move(r.down.at[j], d.at[j % 2], chunk_sem + 2 + j % 2),
            )

        def pass_on(j):
            sum_lines[j][0].second(r.unit_acc.at[j], unit_parts, r.local, z_sem)
            sum_lines[j][1].second(r.down_acc.at[j], down_parts, r.local, z_sem + 4)

        def keep(j, what):
            for copy in (
                move(unit_stage, r.kept_units.at[:, pl.ds(j * chunk, chunk)], keep_sem),
                move(act_stage, r.kept_acts.at[:, pl.ds(j * part, part)], keep_sem + 1),
            ):
                getattr(copy, what)()

        def work(j):
            slot = j % 2
            wait(chunk_loads(j))
            if j > 0:
                keep(j - 1, "wait")

            @pl.loop(0, shards, step=2)
            def _(s):
                both = shard_rows(s, 2)
                pre = dot(x[both], w[slot].reshape(width, chunk))
                grad_act = dot_t(c[both], d[slot].reshape(part, width))
                gate, up = pre[:, :part], pre[:, part:]
                sigmoid = 1.0 / (1.0 + jnp.exp(-gate))
                silu = gate * sigmoid
                act_stage[both] = (silu * up).astype(bf16)
                unit_stage[both, :part] = (
                    grad_act * up * sigmoid * (1.0 + gate * (1.0 - sigmoid))
                ).astype(bf16)
                unit_stage[both, part:] = (grad_act * silu).astype(bf16)

            keep(j, "start")

        def weigh_units(j):
            @pl.loop(0, width // 512)
            def _(n):
                at = pl.ds(pl.multiple_of(n * 512, 512), 512)
                unit_grad[at] = dot_l(x[:, at], unit_stage[...]).astype(bf16)

            wait(start(move(unit_grad, r.unit_terms.at[j], term_sem)))
            sum_lines[j][0].first()

        def weigh_down(j):
            @pl.loop(0, width // 512)
            def _(n):
                at = pl.ds(pl.multiple_of(n * 512, 512), 512)
                down_grad[:, at] = dot_l(act_stage[...], c[:, at]).astype(bf16)

            wait(start(move(down_grad, r.down_terms.at[j], term_sem + 1)))
            sum_lines[j][1].first()

        c_loads = start(*[move(r.cot.at[s], c.at[shard_rows(s)]) for s in range(shards)])
        serve(0, "finish")
        start(*chunk_loads(0))
        n2_late = gather_forward(p, n2_sent, x, r.asend, r.arecv, 0)
        gather_wait(n2_sent, n2_late)
        wait(n2_own)
        wait(c_loads)
        work(0)
        serve(2, "third")
        weigh_units(0)
        serve(3, "second")
        weigh_down(0)
        serve(1, "finish")
        start(*chunk_loads(1))
        work(1)
        weigh_down(1)
        serve(3, "third")
        weigh_units(1)
        serve(2, "finish")
        start(*chunk_loads(2))
        work(2)
        pass_on(0)
        weigh_units(2)
        weigh_down(2)
        serve(3, "finish")
        start(*chunk_loads(3))
        work(3)
        weigh_down(3)
        load_w = start(
            *[
                move(
                    r.units.at[j, k // 2, pl.ds(k % 2 * rows, rows)],
                    c.at[shard_rows(k), pl.ds(j * chunk, chunk)],
                )
                for j in range(CHUNKS)
                for k in range(shards)
            ]
        )
        keep(CHUNKS - 1, "wait")
        order = [name for _, own, partner in ORDER for name in (partner, own)]

        def load_kept(k):
            return move(
                r.kept_units.at[shard_rows(p[order[k]])],
                unit_kept.at[pl.ds(k % 2 * rows, rows)],
                kept_sem + k % 2,
            )

        load_kept(0).start()

        def produce(name, out):
            k = order.index(name)
            load_kept(k).wait()
            if k + 1 < len(order):
                load_kept(k + 1).start()
            if k == 0:
                wait(load_w)

            @pl.loop(0, width // 1024)
            def _(n):
                at = pl.ds(pl.multiple_of(n * 1024, 1024), 1024)
                out[:, at] = dot_t(unit_kept[k % 2 * rows : (k % 2 + 1) * rows], c[at]).astype(
                    bf16
                )

        def act_load(s):
            slot = lax.rem(s, 2)
            return move(r.kept_acts.at[shard_rows(s)], act_kept.at[slot], act_sem + slot)

        def out_store(s):
            slot = lax.rem(s, 2)
            return move(r.stage.at[shard_rows(slot)], r.out_terms.at[s], out_sem + slot)

        def out_of_units():
            load_d = start(
                *[
                    move(r.down.at[j, k], x.at[pl.ds(j * part + k * piece, piece)])
                    for j in range(CHUNKS)
                    for k in range(groups)
                ]
            )
            act_load(0).start()
            wait(load_d)

            @pl.loop(0, shards)
            def _(s):
                act_load(s).wait()

                @pl.when(s + 1 < shards)
                def _():
                    act_load(s + 1).start()

                @pl.when(s >= 2)
                def _():
                    out_store(s - 2).wait()

                slot = lax.rem(s, 2)
                acts = act_kept[slot]

                @pl.loop(0, width // 1024)
                def _(n):
                    at = pl.ds(pl.multiple_of(n * 1024, 1024), 1024)
                    r.stage[shard_rows(slot), at] = dot(acts, x[: acts.shape[1], at]).astype(bf16)

                out_store(s).start()

            out_store(shards - 2).wait()
            out_store(shards - 1).wait()
            pass_on(2)

        def last_weights():
            weigh_units(3)
            pass_on(1)

        sums = scatter(produce, lambda: None, last_weights)
        sums.source.finish()
        sums.source.pairs.clear()
        r.gain_term[...] = jnp.zeros_like(r.gain_term)

        def norm_back_rows(at):
            g = total(r.kept, r.paired, r.final, at)
            h = r.hidden[at, :]
            scale = lax.rsqrt(jnp.mean(h * h, axis=-1, keepdims=True) + norm_eps)
            weighted = g * r.gain_two[...]
            inner = jnp.mean(weighted * h, axis=-1, keepdims=True)
            back = scale * weighted - h * (scale * scale * scale * inner)
            out = r.own_cot[at, :].astype(f32) + back
            r.grad_hidden[at, :] = out
            r.mine[at, :] = out.astype(bf16)
            r.gain_term[...] += jnp.sum(g * h * scale, axis=0, keepdims=True)

        over_rows(rows, norm_back_rows)
        gather_start(p, r.mine, r.branch, r.asend, r.arecv, 0)
        out_of_units()
        sums.finish()

    pl.run_scoped(
        after,
        vm((shards * rows, width)),
        vm((2,) + r.units.shape[1:]),
        vm((2,) + r.down.shape[1:]),
        vm((shards * rows, chunk)),
        vm((shards * rows, part)),
        vm((2 * rows, CHUNKS * chunk)),
        vm((2, rows, CHUNKS * part)),
        vm((width, chunk)),
        vm((part, width)),
        vm((2, span, chunk)),
        vm((2, piece, width)),
    )

    b_own = start(move(r.mine, r.branch.at[me]))

    def end(
        rotated,
        attended,
        cos,
        sin,
        qkv,
        wo,
        grads,
        key_acc,
        value_acc,
        head_grad,
        wo_grad,
        units,
        heads,
        wide_out,
        row_out,
        narrow_out,
        gain_one_term,
        head_acc,
        wo_acc,
        parts,
        row_parts,
    ):
        loads = start(
            move(r.out_weight, wo),
            move(r.attended, attended),
            move(r.rotated, rotated),
            move(r.cos, cos),
            move(r.sin, sin),
            move(r.qkv, qkv),
        )
        narrow = parts.at[:, :, pl.ds(0, chunk)]

        def sum_up(j):
            sum_lines[j][0].total(narrow, r.local, z_sem)
            wait(start(move(parts.at[0, :, pl.ds(0, chunk)], r.unit_sums.at[j], z_sem)))
            copies = exchange(
                of_owner(r.unit_sums.at[j], held), r.units_out.at[j, me], 1 + j
            )
            sum_lines[j][1].total(row_parts, r.local, z_sem)
            row_out[...] = row_parts[0].astype(f32)
            wait(start(move(row_out, r.grad_down.at[pl.ds(j * piece, piece)], z_sem)))
            return copies

        def pass_on(j):
            sum_lines[j][0].second(
                r.unit_acc.at[j % 3], parts.at[1:3, :, pl.ds(0, chunk)], r.local, z_sem
            )
            sum_lines[j][1].second(r.down_acc.at[j % 3], row_parts.at[1:3], r.local, z_sem + 4)

        unit_copies = []
        b_sent = gather_copies(p, r.mine, r.branch, r.asend, r.arecv, 0)
        b_late = gather_forward(p, b_sent, r.branch, r.asend, r.arecv, 0)
        unit_copies += sum_up(0)
        gather_wait(b_sent, b_late)
        wait(b_own)
        wait(start(*[move(r.branch.at[s], x.at[shard_rows(s)]) for s in range(shards)]))
        out_sem_base = sems.take(4)
        out_source = FromMemory(
            p, r.out_terms, r.kept, r.paired, r.send, r.recv, r.local.at[pl.ds(out_sem_base, 4)]
        )
        out_sum = PlaneSum(
            p, out_source, rows, r.kept, r.paired, r.far, r.final, r.send, r.recv
        )
        wait(loads[:2])

        @pl.loop(0, shards, step=2)
        def _(s):
            grad = dot_t(x[shard_rows(s, 2)], wo[...].reshape(-1, width)).astype(bf16)
            grads[pl.ds(s, 2)] = grad.reshape((2,) + grads.shape[1:])

        out_sum.first()

        @pl.loop(0, width // 512)
        def _(n):
            at = pl.ds(pl.multiple_of(n * 512, 512), 512)
            acts = attended[...].reshape(shards * rows, -1)
            wo_grad[:, at] = dot_l(acts, x[:, at]).astype(bf16)

        wait(start(move(wo_grad, r.wo_terms)))
        wo_sum.first()
        n1_loads = start(*[move(r.normed_one.at[s], x.at[shard_rows(s)]) for s in range(shards)])
        wait(loads[2:])

        def attention(pair):
            @pl.loop(0, batch)
            def _(row):
                attend_back_pair(
                    rotated,
                    grads,
                    cos,
                    sin,
                    r.starts[row],
                    r.stats,
                    rotated,
                    key_acc,
                    value_acc,
                    row,
                    pair,
                )

        def weigh_heads(pair):
            lanes = slice(pair * 3 * PAIR, (pair + 1) * 3 * PAIR)

            @pl.loop(0, width // 512)
            def _(n):
                at = pl.ds(pl.multiple_of(n * 512, 512), 512)
                grad = rotated[:, :, :, lanes].reshape(shards * rows, 3 * PAIR)
                head_grad[at] = dot_l(x[:, at], grad).astype(bf16)

            wait(start(move(head_grad, r.head_terms.at[pair])))
            head_lines[pair].first()

        attention(0)
        wait(n1_loads)
        weigh_heads(0)
        out_sum.second()
        for one in sum_lines[0]:
            one.finish()
        pass_on(CHUNKS - 1)
        for pair in range(1, pairs):
            attention(pair)
            weigh_heads(pair)
        wo_sum.second(wo_acc, row_parts.at[1:3], r.local, z_sem)
        out_sum.third()

        def step_out(at):
            out = r.hidden[at, :] + total(r.kept, r.paired, r.final, at)
            r.mine[at, :] = out.astype(bf16)

        over_rows(rows, step_out)
        keep_tokens = [*start(move(r.mine, r.out_tokens))]
        out_sum.finish()
        for name in ("sib", "xp", "yp"):
            pl.semaphore_signal(r.ready, inc=1, device_id=(z, p[name]), device_id_type=MESH)
        pl.semaphore_wait(r.ready, 3)

        def produce(name, out):
            grad = rotated[p[name]].reshape(rows, wide)

            @pl.loop(0, groups)
            def _(n):
                at = pl.ds(pl.multiple_of(n * span, span), span)
                out[:, at] = dot_t(grad, qkv[n]).astype(bf16)

        def pass_heads(k):
            head_lines[k].second(
                head_acc.at[k], parts.at[1:3, :, pl.ds(0, 3 * PAIR)], r.local, z_sem
            )

        def meanwhile():
            unit_copies.extend(sum_up(1))
            unit_copies.extend(sum_up(2))
            unit_copies.extend(sum_up(3))

        pass_heads(0)
        sums = scatter(produce, lambda: pass_heads(1), meanwhile)
        gain_one_term[...] = jnp.zeros_like(gain_one_term)

        def norm_back_rows(at):
            g = total(r.kept, r.paired, r.final, at)
            t = r.tokens[at, :].astype(f32)
            scale = lax.rsqrt(jnp.mean(t * t, axis=-1, keepdims=True) + norm_eps)
            weighted = g * r.gain_one[...]
            inner = jnp.mean(weighted * t, axis=-1, keepdims=True)
            back = scale * weighted - t * (scale * scale * scale * inner)
            r.stage[at, :] = (r.grad_hidden[at, :] + back).astype(bf16)
            gain_one_term[...] += jnp.sum(g * t * scale, axis=0, keepdims=True)

        sums.source.finish()
        sums.source.pairs.clear()
        over_rows(rows, norm_back_rows)
        keep_tokens += start(move(r.stage.at[pl.ds(0, rows)], r.grad_tokens))
        r.gain_mine[...] = jnp.zeros_like(r.gain_mine)
        for k in range(devices):
            at = slice(k * held, (k + 1) * held)
            r.gain_mine[k, 0:1, :held] = gain_one_term[:, at]
            r.gain_mine[k, 1:2, :held] = r.gain_term[:, at]

        def gain_back(k):
            where, to = other(k)
            return pltpu.make_async_remote_copy(
                src_ref=r.gain_mine.at[to],
                dst_ref=r.gain_sum_land.at[k],
                send_sem=r.gsend.at[k],
                recv_sem=r.grecv.at[k],
                **where,
            )

        @pl.loop(1, devices)
        def _(k):
            gain_back(k).start()

        wo_sum.total(row_parts, r.local, z_sem)
        row_out[...] = row_parts[0].astype(f32)
        keep_wo = start(move(row_out, r.grad_out))

        def sum_heads(k):
            head_lines[k].total(parts.at[:, :, pl.ds(0, 3 * PAIR)], r.local, z_sem)
            wait(start(move(parts.at[0, :, pl.ds(0, 3 * PAIR)], r.head_sums.at[k], z_sem)))
            return exchange(
                of_owner(r.head_sums.at[k], held), r.heads_out.at[k, me], 1 + CHUNKS + k
            )

        head_copies = [sum_heads(0)]
        wait(unit_copies)
        wait(start(move(r.units_out, units)))
        stores = []
        for i, out in enumerate((r.grad_gate, r.grad_up)):
            if i == 1:
                head_copies += [sum_heads(k) for k in range(1, pairs)]
            for k in range(groups):
                if len(stores) >= 2:
                    stores[-2].wait()
                for s in range(shards):
                    for a in range(CHUNKS // 2):
                        base = (i * groups + k) * piece
                        tile = jnp.concatenate(
                            [units[2 * a + b, s, :, base : base + piece] for b in range(2)], axis=1
                        )
                        at = (s * 2 + a) * 2 * piece
                        wide_out[k % 2, :, at : at + 2 * piece] = tile.astype(f32)
                span_out = wide_out.shape[2]
                stores.append(move(wide_out.at[k % 2], out.at[:, pl.ds(k * span_out, span_out)]))
                stores[-1].start()
        r.gain_sum_land[0] = r.gain_mine[mine_index]

        @pl.loop(1, devices)
        def _(k):
            gain_back(k).wait()

        r.gain_sums[...] = jnp.sum(r.gain_sum_land[...], axis=0)
        for copies in head_copies:
            wait(copies)
        wait(start(move(r.heads_out, heads)))
        for i, out in enumerate((r.grad_query, r.grad_key, r.grad_value)):
            for k in range(groups):
                for s in range(0, shards, 2):
                    base = i * PAIR + k % 2 * HD
                    tile = jnp.concatenate(
                        [heads[k // 2, s + b, :, base : base + HD] for b in range(2)], axis=1
                    )
                    at = (k * shards + s) * HD
                    narrow_out[i, :, at : at + 2 * HD] = tile.astype(f32)
            stores.append(move(narrow_out.at[i], out))
            stores[-1].start()
        wait(stores[-5:])
        wait(keep_tokens)
        wait(keep_wo)
        for one in (*[one for pair in sum_lines[1:] for one in pair], wo_sum, *head_lines):
            one.finish()
        sums.finish()

    pl.run_scoped(
        end,
        vm(r.rotated.shape),
        vm(r.attended.shape),
        *[vm(ref.shape, f32) for ref in (r.cos, r.sin)],
        vm(r.qkv.shape),
        vm(r.out_weight.shape),
        vm(r.attended.shape),
        vm((shards * shard_len, PAIR), f32),
        vm((shards * shard_len, PAIR), f32),
        vm((width, 3 * PAIR)),
        vm(r.wo_terms.shape),
        vm(r.units_out.shape),
        vm(r.heads_out.shape),
        vm((2, held, width), f32),
        vm((piece, width), f32),
        vm((3, held, width), f32),
        vm((1, width), f32),
        vm((pairs, 2, span, 3 * PAIR)),
        vm((2, held, width)),
        vm((3, span, chunk)),
        vm((3, piece, width)),
    )


def main_plane(groups, shards, batch, tokens, cotangent, gains, weights, starts, collective_id):
    w_query, w_key, w_value, w_out, w_gate, w_up, w_down = weights
    shard_len = tokens.shape[0] // batch
    rows, width = tokens.shape
    held, devices = w_query.shape[0], groups * shards
    mine = width // shards
    wide = 3 * mine
    hidden_here = groups * w_down.shape[0]
    chunk = 2 * hidden_here // CHUNKS
    piece = w_down.shape[0] // CHUNKS
    span = width // groups
    pairs = mine // PAIR
    low = lambda *shape: jax.ShapeDtypeStruct(shape, bf16)
    full = lambda *shape: jax.ShapeDtypeStruct(shape, f32)
    outputs = dict(
        gain_sums=full(8, 128),
        grad_tokens=low(rows, width),
        out_tokens=low(rows, width),
        grad_query=full(held, width),
        grad_key=full(held, width),
        grad_value=full(held, width),
        grad_out=full(held, width),
        grad_gate=full(held, hidden_here * shards),
        grad_up=full(held, hidden_here * shards),
        grad_down=full(CHUNKS * piece, width),
        cos=full(shards, batch, shard_len, PAIR),
        sin=full(shards, batch, shard_len, PAIR),
        rotated=low(shards, batch, shard_len, wide),
        attended=low(shards, batch, shard_len, mine),
        normed_one=low(shards, rows, width),
        cot=low(shards, rows, width),
        branch=low(shards, rows, width),
        qkv=low(groups, span, wide),
        out_weight=low(groups, held, width),
        units=low(CHUNKS, groups, span, chunk),
        down=low(CHUNKS, groups, piece, width),
        out_terms=low(shards, rows, width),
        unit_sums=low(CHUNKS, span, chunk),
        unit_terms=low(CHUNKS, width, chunk),
        down_terms=low(CHUNKS, chunk // 2, width),
        kept_units=low(shards * rows, CHUNKS * chunk),
        kept_acts=low(shards * rows, hidden_here),
        head_terms=low(pairs, width, 3 * PAIR),
        wo_terms=low(groups * held, width),
        head_sums=low(pairs, span, 3 * PAIR),
        unit_land=low(CHUNKS, 4, span, chunk),
        down_land=low(CHUNKS, 4, piece, width),
        head_land=low(pairs, 4, span, 3 * PAIR),
        wo_land=low(4, held, width),
        units_out=low(CHUNKS, shards, held, chunk),
        heads_out=low(pairs, shards, held, 3 * PAIR),
    )
    assert tuple(outputs) == tuple(MAIN_OUTPUTS)
    scratch = dict(
        hidden=pltpu.VMEM((rows, width), f32),
        grad_hidden=pltpu.VMEM((rows, width), f32),
        gain_one=pltpu.VMEM((1, width), f32),
        gain_two=pltpu.VMEM((1, width), f32),
        gain_term=pltpu.VMEM((1, width), f32),
        stats=pltpu.VMEM((batch, pairs, 2, shards * shard_len), f32),
        gains_land=pltpu.VMEM((devices, 8, 2 * held), f32),
        gain_mine=pltpu.VMEM((devices, 8, 128), f32),
        gain_sum_land=pltpu.VMEM((devices, 8, 128), f32),
        x=pltpu.VMEM((shards * rows, width), bf16),
        unit_acc=pltpu.VMEM((CHUNKS - 1, 2, span, chunk), bf16),
        down_acc=pltpu.VMEM((CHUNKS - 1, 2, piece, width), bf16),
        mine=pltpu.VMEM((rows, width), bf16),
        stage=pltpu.VMEM((2 * rows, width), bf16),
    )
    for name, buffer in zip(SCATTER_NAMES, scatter_scratch(rows, width)):
        scratch[name] = buffer
    for name in GATHER_NAMES:
        scratch[name] = DMA((GATHER_SEMS,))
    exchanges, sums = 7 * (1 + CHUNKS + pairs), 8 * CHUNKS + 4 * pairs + 4
    for name, count in (
        ("gsend", devices),
        ("grecv", devices),
        ("esend", exchanges),
        ("erecv", exchanges),
        ("zsend", LINE_SEMS * (2 + 2 * CHUNKS)),
        ("zrecv", LINE_SEMS * (2 + 2 * CHUNKS)),
        ("ssend", sums),
        ("srecv", sums),
    ):
        scratch[name] = DMA((count,))
    scratch["ready"] = pltpu.SemaphoreType.REGULAR
    scratch["local"] = DMA((104,))
    assert tuple(scratch) == tuple(MAIN_SCRATCH)
    in_vmem = 1
    done = pl.pallas_call(
        functools.partial(main_kernel, groups),
        out_shape=list(outputs.values()),
        in_specs=[ANY] * 7 + [VMEM] * 5,
        out_specs=[VMEM] * in_vmem + [ANY] * (len(outputs) - in_vmem),
        scratch_shapes=list(scratch.values()),
        compiler_params=pltpu.CompilerParams(
            collective_id=collective_id, has_side_effects=True, vmem_limit_bytes=63 * MIB
        ),
        cost_estimate=lasting(500),
    )(
        w_query,
        w_key,
        w_value,
        w_gate,
        w_up,
        w_out,
        w_down,
        tokens,
        cotangent,
        jnp.broadcast_to(gains.reshape(1, -1).astype(f32), (8, 2 * held)),
        starts,
        jnp.tile(rope_frequency(), 2 * PAIR // HD)[None],
    )
    count = len(RESULTS) - 1
    shapes = list(outputs.values())[1 : 1 + count]
    results = pl.pallas_call(
        hand_over,
        out_shape=shapes,
        in_specs=[ANY] * count,
        out_specs=[ANY] * count,
        scratch_shapes=[*[pltpu.VMEM(s.shape, s.dtype) for s in shapes], DMA((2, count))],
        compiler_params=pltpu.CompilerParams(vmem_limit_bytes=63 * MIB),
    )(*done[1 : 1 + count])
    return types.SimpleNamespace(**dict(zip(RESULTS, [done[0], *results])))


def hand_over(*refs):
    count = (len(refs) - 1) // 3
    ways = [
        [
            pltpu.make_async_copy(refs[way * 2 * count + i], refs[(2 - way) * count + i], refs[-1].at[way, i])
            for i in range(count)
        ]
        for way in range(2)
    ]
    for copy in ways[0]:
        copy.start()
    for copy, out in zip(*ways):
        copy.wait()
        out.start()
    for copy in ways[1]:
        copy.wait()


def layer(
    groups,
    shards,
    tokens,
    doc_ids,
    cotangent,
    norm1_gain,
    w_query,
    w_key,
    w_value,
    w_out,
    norm2_gain,
    w_gate,
    w_up,
    w_down,
):
    rows, shard_len, width = tokens.shape
    count = rows * shard_len
    held = w_query.shape[0]
    hidden_held = w_down.shape[0]
    hidden_here = groups * hidden_held
    whole_heads = held % HD == 0
    outer, inner = (groups, held) if whole_heads else (1, width // shards)
    pairs = width // shards // PAIR
    both = ("dp", "seq")
    fast = groups == 4 and shards == 8
    flat = lambda v: v.reshape(shards * count, v.shape[-1])
    split = lambda v: v.reshape(shards, count, v.shape[-1])

    gains = jnp.stack([norm1_gain, norm2_gain])
    own_tokens = tokens.reshape(count, width)
    own_cotangent = cotangent.reshape(count, width)
    inputs = own_tokens.astype(f32)
    starts = document_starts(doc_ids)
    by_row = lambda v: v.reshape(shards, rows, shard_len, v.shape[-1])

    if fast:
        done = main_plane(
            groups,
            shards,
            rows,
            own_tokens,
            own_cotangent,
            gains,
            (w_query, w_key, w_value, w_out, w_gate, w_up, w_down),
            starts[:, None, :],
            1,
        )
        return (
            done.out_tokens.reshape(tokens.shape),
            done.grad_tokens.reshape(tokens.shape),
            done.gain_sums[0, :held],
            done.grad_query,
            done.grad_key,
            done.grad_value,
            done.grad_out,
            done.gain_sums[1, :held],
            done.grad_gate,
            done.grad_up,
            done.grad_down,
        )

    cos, sin = rope_tables(starts, shards)
    starts = starts[:, None, :]
    gains = lax.all_gather(gains, both, axis=1, tiled=True).astype(f32)
    gain_one, gain_two = gains[:1], gains[1:]

    def by_head(w):
        blocks = w.reshape(held, outer, shards, inner)
        return jnp.moveaxis(blocks, 2, 0).reshape(shards, held, pairs, PAIR)

    blocks = jnp.stack([w_gate, w_up]).reshape(2, held, groups, shards, hidden_held)
    units = jnp.transpose(blocks, (3, 1, 0, 2, 4)).reshape(shards, held, 2 * hidden_here)
    heads = jnp.stack([by_head(w) for w in (w_query, w_key, w_value)], axis=3)
    heads, units = exchange_plane([heads.reshape(shards, held, -1), units], shards, 1)
    spread = lambda w: lax.all_gather(w, "dp", axis=0, tiled=True)
    qkv_weight = spread(heads.reshape(shards * held, -1))
    unit_weight = spread(units.reshape(shards * held, -1))
    down_weight = spread(w_down)
    if whole_heads:
        out_weight = spread(w_out)
    else:
        whole = lax.all_gather(w_out, both, axis=0, tiled=True)
        out_weight = lax.dynamic_slice_in_dim(whole, lax.axis_index("seq") * inner, inner, 0)
    own_normed = (inputs * rms_scale(inputs) * gain_one).astype(bf16)
    normed_one, cot = [flat(v) for v in gather_plane([own_normed, own_cotangent], shards, 2)]
    pre = by_row(dot(normed_one, qkv_weight))
    rotated, attended, stats = attend(pre, cos, sin, starts)
    attended = flat(attended)
    hidden = inputs + reduce_plane(split(dot(attended, out_weight).astype(bf16)))
    normed_two = (hidden * rms_scale(hidden) * gain_two).astype(bf16)
    normed_two = flat(lax.all_gather(normed_two, "seq"))
    gate_weight, up_weight = unit_weight[:, :hidden_here], unit_weight[:, hidden_here:]
    gate_pre, up_pre = dot(normed_two, gate_weight), dot(normed_two, up_weight)
    sigmoid = jax.nn.sigmoid(gate_pre)
    silu = gate_pre * sigmoid
    activated = (silu * up_pre).astype(bf16)
    out_terms = split(dot(activated, down_weight).astype(bf16))
    grad_act = dot_t(cot, down_weight)
    grad_gate_pre = grad_act * up_pre * sigmoid * (1.0 + gate_pre * (1.0 - sigmoid))
    grad_up_pre = grad_act * silu
    grad_units = jnp.concatenate([grad_gate_pre, grad_up_pre], axis=-1).astype(bf16)
    middle_terms = split(dot_t(grad_units, unit_weight).astype(bf16))
    unit_sums = lax.psum_scatter(
        dot(normed_two.T, grad_units).astype(bf16), "dp", scatter_dimension=0, tiled=True
    )
    down_sums = lax.psum_scatter(
        dot(activated.T, cot).astype(bf16), "dp", scatter_dimension=0, tiled=True
    )
    back, gain_two_term = norm_back(
        hidden, rms_scale(hidden), gain_two, reduce_plane(middle_terms)
    )
    grad_hidden = own_cotangent.astype(f32) + back
    branch = lax.all_gather(grad_hidden.astype(bf16), "seq")

    branch = flat(branch)
    out_w_terms = dot(attended.T, branch).astype(bf16)
    grad_attended = by_row(dot_t(branch, out_weight).astype(bf16))
    grad_pre = flat(attend_back(rotated, grad_attended, cos, sin, starts, stats))
    last_terms = split(dot_t(grad_pre, qkv_weight).astype(bf16))
    head_terms = dot(normed_one.T, grad_pre).astype(bf16)

    if whole_heads:
        grad_out = lax.psum_scatter(out_w_terms, "dp", scatter_dimension=0, tiled=True)
    else:
        placed = lax.dynamic_update_slice_in_dim(
            jnp.zeros((width, width), bf16), out_w_terms, lax.axis_index("seq") * inner, 0
        )
        grad_out = lax.psum_scatter(placed, both, scatter_dimension=0, tiled=True)
    back, gain_one_term = norm_back(inputs, rms_scale(inputs), gain_one, reduce_plane(last_terms))
    grad_tokens = (grad_hidden + back).astype(bf16)
    out_tokens = (hidden + reduce_plane(out_terms)).astype(bf16)
    head_sums = lax.psum_scatter(head_terms, "dp", scatter_dimension=0, tiled=True)
    heads_back, units_back = exchange_plane(
        [head_sums.reshape(shards, held, -1), unit_sums.reshape(shards, held, -1)], shards, 6
    )
    grad_norms = lax.psum_scatter(
        jnp.concatenate([gain_one_term, gain_two_term]), both, scatter_dimension=1, tiled=True
    )
    heads_back = heads_back.reshape(shards, held, pairs, 3, PAIR)
    units_back = units_back.reshape(shards, held, 2, groups, hidden_held)

    def head_grad(i):
        blocks = heads_back[:, :, :, i, :].reshape(shards, held, outer, inner)
        return jnp.moveaxis(blocks, 0, 2).reshape(held, width).astype(f32)

    def unit_grad(i):
        return jnp.transpose(units_back[:, :, i], (1, 2, 0, 3)).reshape(held, -1).astype(f32)

    return (
        out_tokens.reshape(tokens.shape),
        grad_tokens.reshape(tokens.shape),
        grad_norms[0],
        head_grad(0),
        head_grad(1),
        head_grad(2),
        grad_out.astype(f32),
        grad_norms[1],
        unit_grad(0),
        unit_grad(1),
        down_sums.astype(f32),
    )


def solution(mesh):
    both = ("dp", "seq")
    return jax.shard_map(
        functools.partial(layer, mesh.shape["dp"], mesh.shape["seq"]),
        mesh=mesh,
        in_specs=(
            P("dp", "seq", None),
            P("dp", None),
            P("dp", "seq", None),
            P(both),
            P(both, None),
            P(both, None),
            P(both, None),
            P(both, None),
            P(both),
            P(both, None),
            P(both, None),
            P(both, None),
        ),
        out_specs=(
            P("dp", "seq", None),
            P("dp", "seq", None),
            P(both),
            P(both, None),
            P(both, None),
            P(both, None),
            P(both, None),
            P(both),
            P(both, None),
            P(both, None),
            P(both, None),
        ),
        check_vma=False,
    )
```

time: 1200 us -> 569 us (0.47)
  waiting for transfers between devices: 437 us -> 0 us
  matrix products: 180 us -> 0 us
  Pallas kernels: 441 us -> 551 us
  local copies, waits for them, and re-layouts: 53.7 us -> 3.44 us
  blocking collectives: 41.1 us -> 0 us
  other arithmetic: 26.7 us -> 2.99 us
  between operations: 14.7 us -> 1.11 us
    reduce_scatter x4 -> x0, waiting for transfers between devices: 307 us -> none  [the longest x1 147 us: layer(): lax.psum_scatter(unit_terms, 'dp', scatter_dimension=0, tiled=True)]
    dot_general x13 -> x0, matrix products: 180 us -> none  [the longest x9 126 us: dot(): return jnp.dot(a, b, preferred_element_type=f32)]
    pallas_call x8 -> x2, Pallas kernels: 441 us -> 551 us  [the longest x1 544 us: main_plane(): pl.pallas_call(functools.partial(main_kernel, groups), out_shape=list(out...]
    unnamed x10 -> x0, waiting for transfers between devices: 78 us -> none
    all_gather x4 -> x0, waiting for transfers between devices: 51.6 us -> none  [the longest x1 51.6 us: layer(): unit_weight = lax.all_gather(units, 'dp', axis=0, tiled=True)]
    all_gather x1 -> x0, blocking collectives: 41.1 us -> none  [layer(): lax.all_gather(jnp.stack([norm1_gain, norm2_gain]), ('dp', 'seq'), axis=1...]
    convert_element_type x15 -> x1, local copies, waits for them, and re-layouts: 20.9 us -> 0.08 us  [main_plane(): gains.reshape(1, -1).astype(f32)]
    unnamed x50 -> x1, local copies, waits for them, and re-layouts: 17.5 us -> 0.01 us
  transfers between devices with their start and end apart: 9 -> 0, of which waited for: 6 -> 0; matrix products, arithmetic and copies ran while one was open for 9% -> 0% of each run, Pallas kernels for 15% -> 0%
where the time goes in v5:
time: 569 us; the launch traced here: 559 us
  Pallas kernels  551 us (97%)
    pallas_call x1, Pallas kernels, main_plane(): pl.pallas_call(functools.partial(main_kernel, groups), out_shape=list(out...  544 us

profile of v5, /device:TPU:0, one launch (start us, length us, event | category | flops | bytes accessed | tf_op | source)
XLA Modules:
  0.0 558.7 jit_solution(14933004094235207685)
XLA Ops:
  0.7 0.7 maximum_convert_fusion
  1.3 0.1 reshape.84
  1.4 0.7 slice.18
  2.1 0.6 broadcast_in_dim_tile.3.refs_11_
  2.7 0.6 broadcast_in_dim.10.refs_9_
  3.3 0.8 fusion
  4.2 0.6 reduce-window.6
  4.7 0.2 slice_reduce_fusion
  5.0 0.2 reduce-window.9
  5.1 0.7 broadcast_maximum_fusion
  5.8 543.6 %shard_map.203 = (f32[8,128]{1,0:T(8,128)}, bf16[256,2048]{1,0:T(8,128)(2,1)}, bf16[256,2048]{1,0:T(8,128)(2,1)}, f32[64,2048]{1,0:T(8,128)}, f32[64,2048]{1,0:T...) custom-call(bf16[64,2048]{1,0:T(8,128)(2,1)} %refs_0_.1, ...), custom_call_target="tpu_custom_call" | custom-call | bytes 1750000000 | tf_op jit(solution)/shard_map/pallas_call | solution.py:1742
  549.4 7.5 %shard_map.204 = (bf16[256,2048]{1,0:T(8,128)(2,1)}, bf16[256,2048]{1,0:T(8,128)(2,1)}, f32[64,2048]{1,0:T(8,128)}, f32[64,2048]{1,0:T(8,128)}, f32[64,2048]{1,0...) custom-call(bf16[256,2048]{1,0:T(8,128)(2,1)} %get-tuple-element.30.refs_0_, ...), custom_call_target="tpu_custom_call" | custom-call | tf_op jit(solution)/shard_map/pallas_call | solution.py:1768
  556.9 1.3 slice_bitcast_fusion
  (3 shorter events, 0.0 us)

commit v6 on v5

--- a/solution.py
+++ b/solution.py
@@ -1007,7 +1007,6 @@
         n1_own = start(move(r.mine, x.at[shard_rows(me)]))
         n1_late = gather_forward(p, n1_sent, x, r.asend, r.arecv, 0, qkv_line.second)
         qkv_line.third()
-        serve(0, "start", 1)
         wo_line.start()
         unit_exchange = lambda j: exchange(
             lambda s: unit_blocks.at[s, j], r.units.at[j, z, held_at], 1 + j
@@ -1021,7 +1020,7 @@
         gather_wait(n1_sent, n1_late, halfway)
         wait(n1_own)
         wait(unit_copies[0])
-        serve(0, "start", 0)
+        serve(0, "start")
         keep_normed = start(
             *[move(x.at[shard_rows(s)], r.normed_one.at[s]) for s in range(shards)]
         )
@@ -1035,11 +1034,9 @@
             cos[:, row] = jnp.cos(angles).reshape(shards, shard_len, PAIR)
             sin[:, row] = (sign * jnp.sin(angles)).reshape(shards, shard_len, PAIR)
         keep_tables = start(move(cos, r.cos), move(sin, r.sin))
+        wo_line.second()
         qkv_line.finish()
-        load_w = start(move(r.qkv, w))
-        serve(0, "second", 1)
-        wo_line.second()
-        wait(load_w)
+        wait(start(move(r.qkv, w)))
 
         @pl.loop(0, shards, step=2)
         def _(s):
@@ -1048,10 +1045,7 @@
 
         for copies in unit_copies[1:]:
             wait(copies)
-        serve(0, "second", 0)
-        serve(0, "third", 1)
         wo_line.third()
-        serve(1, "start")
         cot_sent = gather_start(p, r.own_cot, r.cot, r.csend, r.crecv, 0)
         cot_own = start(move(r.own_cot, r.cot.at[me]))
 
@@ -1063,9 +1057,10 @@
                 )
 
         attention(0)
+        serve(0, "second")
+        serve(1, "start")
         attention(1)
         cot_late = gather_forward(p, cot_sent, r.cot, r.csend, r.crecv, 0)
-        serve(0, "third", 0)
         keep_heads = start(move(rotated, r.rotated), move(attended, r.attended))
         wo_line.finish()
         wait(keep_normed)
@@ -1080,6 +1075,7 @@
                 out[:, at] = dot(terms, wo[:, :, at].reshape(terms.shape[1], 512)).astype(bf16)
 
         def between():
+            serve(0, "third")
             serve(1, "second")
             serve(2, "start")
 
@@ -1114,9 +1110,6 @@
     over_rows(rows, norm_hidden)
     n2_sent = gather_start(p, r.mine, x, r.asend, r.arecv, 0)
     n2_own = start(move(r.mine, x.at[shard_rows(me)]))
-    serve(1, "third")
-    serve(2, "second")
-    serve(3, "start")
 
     span = r.unit_land.shape[2]
     sum_lines = [
@@ -1223,24 +1216,29 @@
         serve(0, "finish")
         start(*chunk_loads(0))
         n2_late = gather_forward(p, n2_sent, x, r.asend, r.arecv, 0)
-        gather_wait(n2_sent, n2_late)
+        serve(1, "third")
+
+        def next_chunks():
+            serve(2, "second")
+            serve(3, "start")
+
+        gather_wait(n2_sent, n2_late, next_chunks)
         wait(n2_own)
         wait(c_loads)
         work(0)
-        serve(2, "third")
         weigh_units(0)
-        serve(3, "second")
         weigh_down(0)
         serve(1, "finish")
         start(*chunk_loads(1))
         work(1)
+        serve(2, "third")
         weigh_down(1)
-        serve(3, "third")
+        serve(3, "second")
         weigh_units(1)
         serve(2, "finish")
         start(*chunk_loads(2))
         work(2)
-        pass_on(0)
+        serve(3, "third")
         weigh_units(2)
         weigh_down(2)
         serve(3, "finish")
@@ -1333,7 +1331,7 @@
             weigh_units(3)
             pass_on(1)
 
-        sums = scatter(produce, lambda: None, last_weights)
+        sums = scatter(produce, lambda: pass_on(0), last_weights)
         sums.source.finish()
         sums.source.pairs.clear()
         r.gain_term[...] = jnp.zeros_like(r.gain_term)

time: 569 us -> 552 us (0.970)
  Pallas kernels: 551 us -> 535 us
    pallas_call x1, Pallas kernels: 544 us -> 528 us  [main_plane(): pl.pallas_call(functools.partial(main_kernel, groups), out_shape=list(out...]
where the time goes in v6:
time: 552 us; the launch traced here: 543 us
  Pallas kernels  535 us (97%)
    pallas_call x1, Pallas kernels, main_plane(): pl.pallas_call(functools.partial(main_kernel, groups), out_shape=list(out...  528 us

profile of v6, /device:TPU:0, one launch (start us, length us, event | category | flops | bytes accessed | tf_op | source)
XLA Modules:
  0.0 542.8 jit_solution(16015628493422040162)
XLA Ops:
  0.7 0.7 maximum_convert_fusion
  1.3 0.1 reshape.84
  1.4 0.7 slice.18
  2.1 0.6 broadcast_in_dim_tile.3.refs_11_
  2.7 0.6 broadcast_in_dim.10.refs_9_
  3.3 0.8 fusion
  4.2 0.6 reduce-window.6
  4.7 0.2 slice_reduce_fusion
  5.0 0.2 reduce-window.9
  5.1 0.7 broadcast_maximum_fusion
  5.8 527.7 %shard_map.203 = (f32[8,128]{1,0:T(8,128)}, bf16[256,2048]{1,0:T(8,128)(2,1)}, bf16[256,2048]{1,0:T(8,128)(2,1)}, f32[64,2048]{1,0:T(8,128)}, f32[64,2048]{1,0:T...) custom-call(bf16[64,2048]{1,0:T(8,128)(2,1)} %refs_0_.1, ...), custom_call_target="tpu_custom_call" | custom-call | bytes 1750000000 | tf_op jit(solution)/shard_map/pallas_call | solution.py:1740
  533.6 7.5 %shard_map.204 = (bf16[256,2048]{1,0:T(8,128)(2,1)}, bf16[256,2048]{1,0:T(8,128)(2,1)}, f32[64,2048]{1,0:T(8,128)}, f32[64,2048]{1,0:T(8,128)}, f32[64,2048]{1,0...) custom-call(bf16[256,2048]{1,0:T(8,128)(2,1)} %get-tuple-element.30.refs_0_, ...), custom_call_target="tpu_custom_call" | custom-call | tf_op jit(solution)/shard_map/pallas_call | solution.py:1766
  541.1 1.3 slice_bitcast_fusion
  (3 shorter events, 0.0 us)

commit v7 on v6

--- a/solution.py
+++ b/solution.py
@@ -1449,8 +1449,7 @@
             acts = attended[...].reshape(shards * rows, -1)
             wo_grad[:, at] = dot_l(acts, x[:, at]).astype(bf16)
 
-        wait(start(move(wo_grad, r.wo_terms)))
-        wo_sum.first()
+        keep_wo_terms = start(move(wo_grad, r.wo_terms))
         n1_loads = start(*[move(r.normed_one.at[s], x.at[shard_rows(s)]) for s in range(shards)])
         wait(loads[2:])
 
@@ -1493,7 +1492,6 @@
         for pair in range(1, pairs):
             attention(pair)
             weigh_heads(pair)
-        wo_sum.second(wo_acc, row_parts.at[1:3], r.local, z_sem)
         out_sum.third()
 
         def step_out(at):
@@ -1525,8 +1523,13 @@
             unit_copies.extend(sum_up(2))
             unit_copies.extend(sum_up(3))
 
+        def between():
+            pass_heads(1)
+            wait(keep_wo_terms)
+            wo_sum.first()
+
         pass_heads(0)
-        sums = scatter(produce, lambda: pass_heads(1), meanwhile)
+        sums = scatter(produce, between, meanwhile)
         gain_one_term[...] = jnp.zeros_like(gain_one_term)
 
         def norm_back_rows(at):
@@ -1563,9 +1566,7 @@
         def _(k):
             gain_back(k).start()
 
-        wo_sum.total(row_parts, r.local, z_sem)
-        row_out[...] = row_parts[0].astype(f32)
-        keep_wo = start(move(row_out, r.grad_out))
+        wo_sum.second(wo_acc, row_parts.at[1:3], r.local, z_sem)
 
         def sum_heads(k):
             head_lines[k].total(parts.at[:, :, pl.ds(0, 3 * PAIR)], r.local, z_sem)
@@ -1595,6 +1596,9 @@
                 span_out = wide_out.shape[2]
                 stores.append(move(wide_out.at[k % 2], out.at[:, pl.ds(k * span_out, span_out)]))
                 stores[-1].start()
+        wo_sum.total(row_parts, r.local, z_sem)
+        row_out[...] = row_parts[0].astype(f32)
+        keep_wo = start(move(row_out, r.grad_out))
         r.gain_sum_land[0] = r.gain_mine[mine_index]
 
         @pl.loop(1, devices)

time: 552 us -> 549 us (level)
  no operation moved by 1% of the time
where the time goes in v7:
time: 549 us; the launch traced here: 540 us
  Pallas kernels  532 us (97%)
    pallas_call x1, Pallas kernels, main_plane(): pl.pallas_call(functools.partial(main_kernel, groups), out_shape=list(out...  525 us

profile of v7, /device:TPU:0, one launch (start us, length us, event | category | flops | bytes accessed | tf_op | source)
XLA Modules:
  0.0 539.6 jit_solution(10644088378733358485)
XLA Ops:
  0.7 0.7 maximum_convert_fusion
  1.3 0.1 reshape.84
  1.4 0.7 slice.18
  2.1 0.6 broadcast_in_dim_tile.3.refs_11_
  2.7 0.6 broadcast_in_dim.10.refs_9_
  3.3 0.8 fusion
  4.2 0.6 reduce-window.6
  4.7 0.2 slice_reduce_fusion
  5.0 0.2 reduce-window.9
  5.1 0.7 broadcast_maximum_fusion
  5.8 524.6 %shard_map.203 = (f32[8,128]{1,0:T(8,128)}, bf16[256,2048]{1,0:T(8,128)(2,1)}, bf16[256,2048]{1,0:T(8,128)(2,1)}, f32[64,2048]{1,0:T(8,128)}, f32[64,2048]{1,0:T...) custom-call(bf16[64,2048]{1,0:T(8,128)(2,1)} %refs_0_.1, ...), custom_call_target="tpu_custom_call" | custom-call | bytes 1750000000 | tf_op jit(solution)/shard_map/pallas_call | solution.py:1744
  530.4 7.5 %shard_map.204 = (bf16[256,2048]{1,0:T(8,128)(2,1)}, bf16[256,2048]{1,0:T(8,128)(2,1)}, f32[64,2048]{1,0:T(8,128)}, f32[64,2048]{1,0:T(8,128)}, f32[64,2048]{1,0...) custom-call(bf16[256,2048]{1,0:T(8,128)(2,1)} %get-tuple-element.30.refs_0_, ...), custom_call_target="tpu_custom_call" | custom-call | tf_op jit(solution)/shard_map/pallas_call | solution.py:1770
  537.9 1.3 slice_bitcast_fusion
  (3 shorter events, 0.0 us)
